TPU v7x, 32 devices: a whole 2x2x4 slice. The times are simulated.
32 devices in a mesh: dp: 4 (over y, x), seq: 2 (over core), fsdp: 4 (over z).
Axes of the slice: x: 2, y: 2, z: 4, core: 2. Of those that a mesh axis runs over, the one named last changes fastest.
Arguments:
- layer_input: bfloat16 [4, 1024, 2048], P('dp', ('seq', 'fsdp')), may hold values from -6 to 6
- out_grad: bfloat16 [4, 1024, 2048], P('dp', ('seq', 'fsdp')), may hold values from -6 to 6
- norm_gain: float32 [2048], P(('dp', 'seq', 'fsdp')), may hold values from 0.4 to 1.6
- in_weight: bfloat16 [2048, 8512], P(('dp', 'seq', 'fsdp')), may hold values from -0.125 to 0.125
- conv_weight: float32 [4352, 4], P(('dp', 'seq', 'fsdp')), may hold values from -3 to 3
- conv_bias: float32 [4352], P(('dp', 'seq', 'fsdp')), may hold values from -0.5 to 0.5
- step_bias: float32 [64], replicated, may hold values from -7 to -3
- log_rate: float32 [64], replicated, may hold values from -1 to 1.5
- skip_gain: float32 [64], replicated, may hold values from 0.5 to 1.5
- gate_gain: float32 [4096], P(('dp', 'seq', 'fsdp')), may hold values from 0.25 to 1.75
- out_weight: bfloat16 [4096, 2048], P(('dp', 'seq', 'fsdp')), may hold values from -0.1875 to 0.1875
- nest_level: int32 [4], P('dp'), may hold values from 0 to 3
- doc_lengths: int32 [4, 4], P('dp'), may hold values from 1 to 512, 1024 in all within a row
Outputs:
- layer_output: bfloat16 [4, 1024, 2048], P('dp', ('seq', 'fsdp'))
- input_grad: bfloat16 [4, 1024, 2048], P('dp', ('seq', 'fsdp'))
- norm_gain_grad: float32 [2048], P(('dp', 'seq', 'fsdp'))
- in_weight_grad: float32 [2048, 8512], P(('dp', 'seq', 'fsdp'))
- conv_weight_grad: float32 [4352, 4], P(('dp', 'seq', 'fsdp'))
- conv_bias_grad: float32 [4352], P(('dp', 'seq', 'fsdp'))
- step_bias_grad: float32 [64], replicated
- log_rate_grad: float32 [64], replicated
- skip_gain_grad: float32 [64], replicated
- gate_gain_grad: float32 [4096], P(('dp', 'seq', 'fsdp'))
- out_weight_grad: float32 [4096, 2048], P(('dp', 'seq', 'fsdp'))
Inputs may be any that keep to these rules, and one draw needn't show every extreme that they name: `doc_lengths`: each row holds the 4 document lengths of one sequence, which add up to 1024; the longest is 512. `nest_level`: the level of a sequence: it uses the first 64 / 2^(3 - level) heads.
All inputs are finite; a program needn't handle non-finite values.
Results may differ from a plain program's by a relative error of at most 0.011.
Values may be sent and summed in bfloat16 or wider, within the bound.
A program may use at most 192 MiB of HBM per device.

v0:
```python
import jax
import jax.numpy as jnp
from jax import lax
from jax.sharding import PartitionSpec as P

HEADS = 64
HEAD_DIM = 64
STATE = 128
KW = 4
INNER = 4096
CONV = 4352
EXTENT = 8512


HIGH = lax.Precision.HIGHEST
EPSILON = 1e-05


def shifted(value, axis, steps):
    count = lax.axis_size(axis)
    leading, last = (max(0, -steps), min(count, count - steps))
    return lax.ppermute(value, axis, [(source, source + steps) for source in range(leading, last)])


def prefix(array, axis, combine, identity):
    peers, place = (lax.axis_size(axis), lax.axis_index(axis))
    everything = jax.tree.map(
        lambda part, kind: lax.all_gather(part.astype(kind), axis),
        array,
        (jnp.bfloat16, jnp.bfloat16),
    )
    start = jax.tree.map(
        lambda part, zero: jnp.broadcast_to(jnp.asarray(zero, part.dtype), part.shape),
        array,
        identity,
    )

    def prefix_lap(k, before):
        reached = k < place
        new = combine(
            before, jax.tree.map(lambda part, own: part[k].astype(own.dtype), everything, array)
        )
        return jax.tree.map(lambda a, b: jnp.where(reached, a, b), new, before)

    return lax.fori_loop(0, peers, prefix_lap, start)


def carried_in(array, axis, combine, identity):
    peers, place = (lax.axis_size(axis), lax.axis_index(axis))
    everything = jax.tree.map(
        lambda part, kind: lax.all_gather(part.astype(kind), axis),
        array,
        jax.tree.map(lambda a: jnp.bfloat16 if a.dtype == jnp.float32 else a.dtype, array),
    )
    start = jax.tree.map(
        lambda part, zero: jnp.broadcast_to(jnp.asarray(zero, part.dtype), part.shape),
        array,
        identity,
    )

    def carried_lap(k, before):
        at = peers - 1 - k
        reached = at > place
        new = combine(
            before, jax.tree.map(lambda part, own: part[at].astype(own.dtype), everything, array)
        )
        return jax.tree.map(lambda a, b: jnp.where(reached, a, b), new, before)

    return lax.fori_loop(0, peers, carried_lap, start)


def doc_begins(lengths, positions):
    endings = jnp.cumsum(lengths, axis=1) - lengths
    reached = endings[:, None, :] <= positions[None, :, None]
    return jnp.max(jnp.where(reached, endings[:, None, :], 0), axis=2)


def input_norm(hidden, gain):
    inv_rms = lax.rsqrt(jnp.mean(hidden * hidden, axis=1, keepdims=True) + EPSILON)
    return hidden * inv_rms * gain


def causal_conv(extended, taps, bias, validity):
    block_len = validity.shape[2]
    running = bias + jnp.zeros((extended.shape[0], block_len, extended.shape[2]), jnp.float32)
    for tap in range(taps.shape[1]):
        running = (
            running + extended[:, tap : tap + block_len] * taps[:, tap] * validity[tap][:, :, None]
        )
    return jax.nn.silu(running)


def scan_parts(signal, key_side, query_side, rate_in, step_bias, log_rate, begins, block_start):
    step = jax.nn.softplus(rate_in + step_bias)
    log_decay = step * -jnp.exp(log_rate)
    cumulative = jnp.cumsum(log_decay, axis=1)
    by_head = jnp.swapaxes(cumulative, 1, 2)
    indices = jnp.arange(signal.shape[1])
    same_doc = (begins[:, :, None] == begins[:, None, :]) & (
        indices[None, None, :] <= indices[None, :, None]
    )
    gaps = by_head[:, :, :, None] - by_head[:, :, None, :]
    kernel = jnp.exp(jnp.where(same_doc[:, None], gaps, 0.0)) * same_doc[:, None]
    intersection = jnp.einsum("btn,bsn->bts", query_side, key_side, precision=HIGH)
    mixing = kernel * intersection[:, None] * jnp.swapaxes(step, 1, 2)[:, :, None, :]
    local_out = jnp.einsum("bhts,bshp->bthp", mixing, signal, precision=HIGH)
    inherits = (begins < block_start).astype(jnp.float32)
    carried = jnp.exp(cumulative) * inherits[:, :, None]
    last_same = begins == begins[:, -1:]
    tail_weight = (
        jnp.exp(jnp.where(last_same[:, :, None], cumulative[:, -1:] - cumulative, 0.0))
        * last_same[:, :, None]
        * step
    )
    fresh_state = jnp.einsum("bsh,bshp,bsn->bhpn", tail_weight, signal, key_side, precision=HIGH)
    return (local_out, carried, carried[:, -1], fresh_state)


def gated_norm(scan_out, signal, skip_gain, gate_in, gate_gain, head_mask, unit_count):
    mixed = (scan_out + skip_gain[:, None] * signal) * head_mask[:, None, :, None]
    gated = mixed.reshape(gate_in.shape) * jax.nn.silu(gate_in)
    mean_square = jnp.sum(gated * gated, axis=2, keepdims=True) / unit_count[:, None, None]
    return gated * lax.rsqrt(mean_square + EPSILON) * gate_gain


def combine_states(earlier, later):
    return (earlier[0] * later[0], later[1] + later[0][:, :, None, None] * earlier[1])


def local(
    layer_input,
    out_grad,
    norm_gain,
    in_weight,
    conv_weight,
    conv_bias,
    step_bias,
    log_rate,
    skip_gain,
    gate_gain,
    out_weight,
    nest_level,
    doc_lengths,
):
    seq_count, block_len, model_width = layer_input.shape
    token_count = seq_count * block_len
    gain_all, taps_all, bias_all, gate_all = (
        lax.all_gather(norm_gain, ("dp", "seq", "fsdp"), axis=0, tiled=True),
        lax.all_gather(conv_weight, ("dp", "seq", "fsdp"), axis=0, tiled=True),
        lax.all_gather(conv_bias, ("dp", "seq", "fsdp"), axis=0, tiled=True),
        lax.all_gather(gate_gain, ("dp", "seq", "fsdp"), axis=0, tiled=True),
    )
    block_start = lax.axis_index(("seq", "fsdp")) * block_len
    positions = block_start + jnp.arange(block_len, dtype=jnp.int32)
    begins = doc_begins(doc_lengths, positions)
    hidden = layer_input.reshape(token_count, model_width).astype(jnp.float32)
    normed = input_norm(hidden, gain_all).astype(jnp.bfloat16)
    columns = normed
    projected = jnp.dot(
        columns,
        lax.all_gather(in_weight, ("dp", "seq", "fsdp"), axis=0, tiled=True),
        preferred_element_type=jnp.float32,
    ).astype(jnp.bfloat16)
    projected = projected.reshape(seq_count, block_len, EXTENT)
    gate_in = projected[:, :, :INNER].astype(jnp.float32)
    conv_in = projected[:, :, INNER : INNER + CONV]
    rate_in = projected[:, :, INNER + CONV :].astype(jnp.float32)
    edge_rows = shifted(conv_in[:, block_len - (KW - 1) :], ("seq", "fsdp"), 1)
    extended = jnp.concatenate([edge_rows, conv_in], axis=1).astype(jnp.float32)
    validity = jnp.stack(
        [(positions[None, :] - (KW - 1) + tap >= begins).astype(jnp.float32) for tap in range(KW)]
    )
    activated, conv_pull = jax.vjp(
        lambda ext_in, taps, bias: causal_conv(ext_in, taps, bias, validity),
        extended,
        taps_all,
        bias_all,
    )
    signal = activated[:, :, :INNER].reshape(seq_count, block_len, HEADS, HEAD_DIM)
    key_side = activated[:, :, INNER : INNER + STATE]
    query_side = activated[:, :, INNER + STATE :]
    local_out, carried, decays, fresh_state = scan_parts(
        signal, key_side, query_side, rate_in, step_bias, log_rate, begins, block_start
    )
    identity = (jnp.ones_like(decays), jnp.zeros_like(fresh_state))
    entry_state = prefix((decays, fresh_state), ("seq", "fsdp"), combine_states, identity)[1]
    scan_out = local_out + carried[..., None] * jnp.einsum(
        "btn,bhpn->bthp", query_side, entry_state, precision=HIGH
    )
    active = jnp.right_shift(HEADS, 3 - nest_level)
    head_mask = (jnp.arange(HEADS)[None, :] < active[:, None]).astype(jnp.float32)
    unit_count = (active * HEAD_DIM).astype(jnp.float32)
    gate_normed, gate_pull = jax.vjp(
        lambda sv, xv, sk, gi, gg: gated_norm(sv, xv, sk, gi, gg, head_mask, unit_count),
        scan_out,
        signal,
        skip_gain,
        gate_in,
        gate_all,
    )
    normed_out = gate_normed.reshape(token_count, INNER).astype(jnp.bfloat16)
    columns = normed_out
    branch_out = jnp.dot(
        columns,
        lax.all_gather(out_weight, ("dp", "seq", "fsdp"), axis=0, tiled=True),
        preferred_element_type=jnp.float32,
    )
    layer_output = (
        (hidden + branch_out).astype(jnp.bfloat16).reshape(seq_count, block_len, model_width)
    )
    grad_flat = out_grad.reshape(token_count, model_width)
    grad_normed_out = lax.dot_general(
        grad_flat,
        lax.all_gather(out_weight, ("dp", "seq", "fsdp"), axis=0, tiled=True),
        (((1,), (1,)), ((), ())),
        preferred_element_type=jnp.float32,
    )
    grad_scan, grad_skip_signal, grad_skip, grad_gate_in, grad_gate_gain = gate_pull(
        grad_normed_out.reshape(seq_count, block_len, INNER)
    )
    lead_grad = jnp.einsum("bth,bthp,btn->bhpn", carried, grad_scan, query_side, precision=HIGH)
    later_grad = carried_in((decays, lead_grad), ("seq", "fsdp"), combine_states, identity)[1]

    def full_scan(signal_in, key_in, query_in, rate_values, bias_values, rate_logs):
        part_out, part_carried, part_decays, part_fresh = scan_parts(
            signal_in, key_in, query_in, rate_values, bias_values, rate_logs, begins, block_start
        )
        joined_out = part_out + part_carried[..., None] * jnp.einsum(
            "btn,bhpn->bthp", query_in, entry_state, precision=HIGH
        )
        return (joined_out, part_decays[:, :, None, None] * entry_state + part_fresh)

    scan_pull = jax.vjp(full_scan, signal, key_side, query_side, rate_in, step_bias, log_rate)[1]
    grad_signal, grad_key, grad_query, grad_rate, grad_step_bias, grad_log_rate = scan_pull(
        (grad_scan, later_grad)
    )
    grad_activated = jnp.concatenate(
        [
            (grad_signal + grad_skip_signal).reshape(seq_count, block_len, INNER),
            grad_key,
            grad_query,
        ],
        axis=2,
    )
    grad_extended, grad_taps, grad_bias = conv_pull(grad_activated)
    returned = shifted(grad_extended[:, : KW - 1].astype(jnp.bfloat16), ("seq", "fsdp"), -1).astype(
        jnp.float32
    )
    grad_conv_in = grad_extended[:, KW - 1 :] + jnp.pad(
        returned, ((0, 0), (block_len - (KW - 1), 0), (0, 0))
    )
    grad_projected = (
        jnp.concatenate([grad_gate_in, grad_conv_in, grad_rate], axis=2)
        .reshape(token_count, EXTENT)
        .astype(jnp.bfloat16)
    )
    grad_normed = lax.dot_general(
        grad_projected,
        lax.all_gather(in_weight, ("dp", "seq", "fsdp"), axis=0, tiled=True),
        (((1,), (1,)), ((), ())),
        preferred_element_type=jnp.float32,
    )
    replicas = lax.axis_size("dp")
    members = lax.axis_size(("seq", "fsdp"))
    width_in = model_width // lax.axis_size(("dp", "seq", "fsdp"))
    width_out = INNER // lax.axis_size(("dp", "seq", "fsdp"))
    in_cols, out_cols = (
        lax.all_to_all(
            normed.reshape(token_count, replicas, members, width_in),
            ("seq", "fsdp"),
            split_axis=2,
            concat_axis=0,
            tiled=True,
        ),
        lax.all_to_all(
            normed_out.reshape(token_count, replicas, members, width_out),
            ("seq", "fsdp"),
            split_axis=2,
            concat_axis=0,
            tiled=True,
        ),
    )
    in_cols = in_cols.reshape(members * token_count, replicas * width_in)
    out_cols = out_cols.reshape(members * token_count, replicas * width_out)
    in_new = lax.dot_general(
        in_cols,
        lax.all_gather(grad_projected, ("seq", "fsdp"), axis=0, tiled=True),
        (((0,), (0,)), ((), ())),
        preferred_element_type=jnp.float32,
    )
    out_new = lax.dot_general(
        out_cols,
        lax.all_gather(grad_flat, ("seq", "fsdp"), axis=0, tiled=True),
        (((0,), (0,)), ((), ())),
        preferred_element_type=jnp.float32,
    )
    in_weight_grad, out_weight_grad = (
        lax.psum_scatter(in_new.astype(jnp.bfloat16), "dp", scatter_dimension=0, tiled=True).astype(
            jnp.float32
        ),
        lax.psum_scatter(
            out_new.astype(jnp.bfloat16), "dp", scatter_dimension=0, tiled=True
        ).astype(jnp.float32),
    )
    norm_pull = jax.vjp(input_norm, hidden, gain_all)[1]
    grad_hidden, grad_gain = norm_pull(grad_normed)
    input_grad = (
        (grad_flat.astype(jnp.float32) + grad_hidden)
        .astype(jnp.bfloat16)
        .reshape(seq_count, block_len, model_width)
    )
    norm_gain_grad, conv_weight_grad, conv_bias_grad, gate_gain_grad = (
        lax.psum_scatter(grad_gain, ("dp", "seq", "fsdp"), scatter_dimension=0, tiled=True),
        lax.psum_scatter(grad_taps, ("dp", "seq", "fsdp"), scatter_dimension=0, tiled=True),
        lax.psum_scatter(grad_bias, ("dp", "seq", "fsdp"), scatter_dimension=0, tiled=True),
        lax.psum_scatter(grad_gate_gain, ("dp", "seq", "fsdp"), scatter_dimension=0, tiled=True),
    )
    step_bias_grad, log_rate_grad, skip_gain_grad = lax.psum(
        (grad_step_bias, grad_log_rate, grad_skip), ("dp", "seq", "fsdp")
    )
    return (
        layer_output,
        input_grad,
        norm_gain_grad,
        in_weight_grad,
        conv_weight_grad,
        conv_bias_grad,
        step_bias_grad,
        log_rate_grad,
        skip_gain_grad,
        gate_gain_grad,
        out_weight_grad,
    )


def solution(mesh):
    return jax.shard_map(
        local,
        mesh=mesh,
        in_specs=(
            P("dp", ("seq", "fsdp"), None),
            P("dp", ("seq", "fsdp"), None),
            P(("dp", "seq", "fsdp")),
            P(("dp", "seq", "fsdp"), None),
            P(("dp", "seq", "fsdp"), None),
            P(("dp", "seq", "fsdp")),
            P(),
            P(),
            P(),
            P(("dp", "seq", "fsdp")),
            P(("dp", "seq", "fsdp"), None),
            P("dp"),
            P("dp", None),
        ),
        out_specs=(
            P("dp", ("seq", "fsdp"), None),
            P("dp", ("seq", "fsdp"), None),
            P(("dp", "seq", "fsdp")),
            P(("dp", "seq", "fsdp"), None),
            P(("dp", "seq", "fsdp"), None),
            P(("dp", "seq", "fsdp")),
            P(),
            P(),
            P(),
            P(("dp", "seq", "fsdp")),
            P(("dp", "seq", "fsdp"), None),
        ),
        check_vma=False,
    )
```

profile of v0, /device:TPU:0, one launch (start us, length us, event | category | flops | bytes accessed | tf_op | source)
XLA Modules:
  0.0 1071.5 jit_solution(13819584643997705953)
XLA Ops:
  10.2 73.2 %all-gather.4 = f32[32,136,4]{1,2,0:T(4,128)S(1)} all-gather(f32[1,136,4]{1,2,0:T(4,128)} %bitcast.343), channel_id=1, replica_groups=mesh['dp'=4,'seq'=2,'fsdp'=4] {'dp','seq','fsdp'}, dimensions={0}, use_global_device_ids=true | all-gather | bytes 71808 | tf_op jit(solution)/shard_map/all_gather | solution.py:149
  85.2 38.6 %all-reduce.18 = (f32[2048]{0:T(1024)S(1)}, f32[4352]{0:T(1024)S(1)}) all-reduce(f32[2048]{0:T(1024)S(1)} %dynamic-update-slice.1, f32[4352]{0:T(1024)S(1)} %dynamic-update-slice), channel_id=1, replica_groups=mesh['dp'=4,'seq'=2,'fsdp'=4] {'dp','seq','fsdp'}, use_global_device_ids=true, to_apply=%add.12 | all-reduce | flops 6400 | bytes 51200
  125.5 93.7 %all-gather.13.cloned.1.call-done = bf16[2048,8512]{1,0:T(8,128)(2,1)} async-done(((bf16[64,8512]{1,0:T(8,128)(2,1)}), bf16[2048,8512]{1,0:T(8,128)(2,1)}) %all-gather.13.cloned.1.call-update) | async-done | bytes 34865168 | tf_op jit(solution)/shard_map/all_gather | solution.py:161
  219.2 18.0 %fusion.7 = bf16[1,128,8512]{1,2,0:T(8,128)(2,1)S(1)} fusion(bf16[2048,8512]{1,0:T(8,128)(2,1)} %all-gather.13.cloned.1.call-done, bf16[1,128,2048]{2,1,0:T(8,128)(2,1)S(1)} %copy-done.12, f32[2048]{0:T(1024)S(1)} %get-tuple-element.358, f32[128]{0:T(128)S(1)} %fusion.163), kind=kOutput, calls=%fused_computation.10 | convolution fusion | flops 4464877568 | bytes 37577216 | tf_op jit(solution)/shard_map/dot_general | solution.py:159
  237.2 1.7 slice.85
  244.9 2.1 maximum_convert_fusion
  247.0 6.7 fusion.25
  255.7 2.8 fusion.80
  260.7 67.3 %all-gather.5 = f32[32,1,128]{2,1,0:T(1,128)S(1)} all-gather(f32[1,1,128]{2,1,0:T(1,128)S(1)} %bitcast.346), channel_id=1, replica_groups=mesh['dp'=4,'seq'=2,'fsdp'=4] {'dp','seq','fsdp'}, dimensions={0}, use_global_device_ids=true | all-gather | bytes 16896 | tf_op jit(solution)/shard_map/all_gather | solution.py:151
  329.0 13.1 %all_gather.50 = bf16[8,1,64]{2,1,0:T(2,128)(2,1)S(1)} all-gather(bf16[1,1,64]{2,1,0:T(2,128)(2,1)S(1)} %copy.110), channel_id=1, replica_groups=mesh['dp'=4,'seq'=2,'fsdp'=4] {'seq','fsdp'}, dimensions={0}, use_global_device_ids=true | all-gather | bytes 1152 | tf_op jit(solution)/shard_map/all_gather | solution.py:28
  343.3 15.0 %while.30 = (s32[]{:T(128)}, f32[1,64,64,128]{3,2,1,0:T(8,128)S(1)}, s32[]{:T(128)}, bf16[8,1,64,64,128]{4,3,2,1,0:T(8,128)(2,1)}, bf16[8,1,64]{2,1,0:T(2,128)(2,1)S(1)}, /*index=5*/s32[]{:T(128)}, s32[]{:T(128)}) while((s32[]{:T(128)}, f32[1,64,64,128]{3,2,1,0:T(8,128)S(1)}, s32[]{:T(128)}, ...), condition=%wide.region_5.6_spmd.clone, body=%wide.region_4.5_spmd.clone.sunk | while | flops 2621508 | bytes 5243633 | solution.py:45
  343.3 1.8 fusion.186
  345.1 1.8 fusion.186
  347.0 1.8 fusion.186
  348.8 1.8 fusion.186
  350.6 1.8 fusion.186
  352.5 1.8 fusion.186
  354.4 1.8 fusion.186
  356.2 1.8 fusion.186
  358.3 2.9 fusion.52
  361.3 8.6 fusion.38
  369.9 4.1 multiply_reduce_fusion.9
  374.0 84.3 %all-gather.15.cloned.1.call-done = bf16[4096,2048]{1,0:T(8,128)(2,1)} async-done(((bf16[128,2048]{1,0:T(8,128)(2,1)}), bf16[4096,2048]{1,0:T(8,128)(2,1)}) %all-gather.15.cloned.1.call-update) | async-done | bytes 16777232 | tf_op jit(solution)/shard_map/all_gather | solution.py:205
  458.3 11.5 %fusion.39 = (f32[4096]{0:T(1024)S(1)}, f32[128]{0:T(128)S(1)}, f32[128,4096]{0,1:T(8,128)S(1)}) fusion(f32[1,128,4096]{1,2,0:T(8,128)} %get-tuple-element.370, f32[128]{0:T(128)S(1)} %get-tuple-element.367, f32[4096]{0:T(1024)S(1)} %bitcast.340, bf16[4096,2048]{1,0:T(8,128)(2,1)} %all-gather.15.cloned.1.call-done, bf16[1,128,2048]{2,1,0:T(8,128)(2,1)S(1)} %copy-done.19), kind=kOutput, calls=%fused_computation.64 | convolution fusion | flops 2150625280 | bytes 21529600 | tf_op jit(solution)/shard_map/dot_general | solution.py:212
  469.9 4.8 multiply_reduce_fusion.6
  476.0 2.8 fusion.83
  479.5 2.7 multiply_reduce_fusion.8
  484.1 10.7 fusion.27
  494.8 3.5 fusion.88
  500.4 58.8 %all-gather.19.cloned.1.call-done = bf16[512,64,128]{2,1,0:T(8,128)(2,1)} async-done(((bf16[64,64,128]{2,1,0:T(8,128)(2,1)}), bf16[512,64,128]{2,1,0:T(8,128)(2,1)}) %all-gather.19.cloned.1.call-update) | async-done | bytes 8388624 | tf_op jit(solution)/shard_map/all_gather | solution.py:51
  559.2 33.8 %while.31 = (s32[]{:T(128)}, f32[1,64,64,128]{3,2,1,0:T(8,128)}, s32[]{:T(128)}, bf16[8,1,64,64,128]{4,3,2,1,0:T(8,128)(2,1)}, bf16[8,1,64]{2,1,0:T(2,128)(2,1)}...) while((s32[]{:T(128)}, f32[1,64,64,128]{3,2,1,0:T(8,128)}, s32[]{:T(128)}, ...), condition=%wide.region_9.10_spmd.clone, body=%wide.region_8.9_spmd.clone.sunk | while | flops 2621512 | bytes 5243695 | solution.py:69
  559.9 3.0 fusion.187
  563.5 3.6 fusion.187
  567.8 3.6 fusion.187
  572.1 3.6 fusion.187
  576.4 3.6 fusion.187
  580.6 3.6 fusion.187
  584.9 3.6 fusion.187
  589.2 3.6 fusion.187
  593.0 2.2 multiply_reduce_fusion.7
  595.3 5.5 fusion.41
  603.3 5.2 fusion.97
  608.6 5.4 fusion.36
  614.1 6.2 multiply_reduce_fusion.5
  620.3 3.0 multiply_multiply_fusion.3
  623.3 3.5 pad_add_fusion
  626.8 2.0 copy-done.13
  631.7 3.6 collective-permute-done.1
  636.7 3.6 fusion.24
  640.3 12.7 %pad_maximum_fusion.1 = bf16[1,128,8512]{1,2,0:T(8,128)(2,1)} fusion(bf16[1,128,64]{1,2,0:T(8,128)(2,1)S(1)} %get-tuple-element.363, bf16[1,128,4352]{1,2,0:T(8,128)(2,1)S(1)} %fusion.24, bf16[1,128,4096]{1,2,0:T(8,128)(2,1)S(1)} %copy-done.21), kind=kLoop, calls=%fused_computation.49 | loop fusion | flops 6537216 | bytes 4358144 | tf_op jit(solution)/shard_map/concatenate | solution.py:253
  653.3 59.6 %all_to_all.30 = bf16[128,4,8,128]{0,3,1,2:T(8,128)(2,1)S(1)} all-to-all(bf16[128,4,8,128]{0,3,1,2:T(8,128)(2,1)S(1)} %copy.128), channel_id=1, replica_groups=mesh['dp'=4,'seq'=2,'fsdp'=4] {'seq','fsdp'}, dimensions={2} | all-to-all | bytes 2097152 | tf_op jit(solution)/shard_map/all_to_all | solution.py:275
  714.5 6.2 fusion.17
  723.7 41.5 %all_to_all.31 = bf16[128,4,8,64]{0,3,1,2:T(8,128)(2,1)S(1)} all-to-all(bf16[128,4,8,64]{0,3,1,2:T(8,128)(2,1)S(1)} %copy.124), channel_id=1, replica_groups=mesh['dp'=4,'seq'=2,'fsdp'=4] {'seq','fsdp'}, dimensions={2} | all-to-all | bytes 1048576 | tf_op jit(solution)/shard_map/all_to_all | solution.py:268
  766.4 73.3 %all-gather.21.cloned.1.call-done = bf16[1,1024,8512]{1,2,0:T(8,128)(2,1)} async-done(((bf16[1,128,8512]{1,2,0:T(8,128)(2,1)}), bf16[1,1024,8512]{1,2,0:T(8,128)(2,1)}) %all-gather.21.cloned.1.call-update) | async-done | bytes 17432592 | tf_op jit(solution)/shard_map/all_gather | solution.py:287
  839.6 19.1 %fusion.4 = bf16[256,8512]{1,0:T(8,128)(2,1)} fusion(bf16[1,1024,8512]{1,2,0:T(8,128)(2,1)} %all-gather.21.cloned.1.call-done, bf16[32,8,8,128]{3,2,1,0:T(8,128)(2,1)S(1)} %bitcast.339), kind=kOutput, calls=%fused_computation.8 | convolution fusion | flops 4464918528 | bytes 22315008 | tf_op jit(solution)/shard_map/dot_general | solution.py:285
  858.9 9.1 fusion.21
  868.0 9.4 reduce-scatter.6.cloned.1.call-done
  877.5 2.1 convert_element_type.271
  879.6 24.4 %fusion.110 = (f32[2048]{0:T(1024)S(1)}, f32[128]{0:T(128)S(1)}, f32[128,2048]{1,0:T(8,128)}) fusion(bf16[1,128,2048]{2,1,0:T(8,128)(2,1)S(1)} %copy-done.12, f32[128]{0:T(128)S(1)} %copy-done.36, f32[2048]{0:T(1024)S(1)} %get-tuple-element.358, bf16[2048,8512]{1,0:T(8,128)(2,1)} %all-gather.13.cloned.1.call-done, ...), kind=kOutput, calls=%fused_computation.137 | convolution fusion | flops 4471109632 | bytes 38634496 | tf_op jit(solution)/shard_map/dot_general | solution.py:257
  904.1 40.6 %all-reduce.17 = (f32[2048]{0:T(1024)S(1)}, f32[4352]{0:T(1024)S(1)}, f32[64]{0:T(128)}, f32[64]{0:T(128)}, f32[64]{0:T(128)}, /*index=5*/f32[4096]{0:T(1024)S(1)}) all-reduce(f32[2048]{0:T(1024)S(1)} %get-tuple-element.326, f32[4352]{0:T(1024)S(1)} %get-tuple-element.325, ...), channel_id=6, replica_groups=mesh['dp'=4,'seq'=2,'fsdp'=4] {'dp','seq','fsdp'}, use_global_device_ids=true, to_apply=%region_20.21.clone | all-reduce | flops 10688 | bytes 85504
  946.5 2.4 fusion.121
  948.8 53.1 %all-reduce.21.cloned.1.call-done = f32[4352,4]{0,1:T(4,128)} async-done(((f32[4352,4]{0,1:T(4,128)}), f32[4352,4]{0,1:T(4,128)}) %all-reduce.21.cloned.1.call-update) | async-done | bytes 69648
  1003.3 58.6 %reduce-scatter.4.cloned.1.call-done = bf16[64,8512]{1,0:T(8,128)(2,1)} async-done(((bf16[256,8512]{1,0:T(8,128)(2,1)}), bf16[64,8512]{1,0:T(8,128)(2,1)}) %reduce-scatter.4.cloned.1.call-update) | async-done | bytes 1089552 | tf_op jit(solution)/shard_map/reduce_scatter | solution.py:298
  1061.9 2.7 convert_element_type.268
  (231 shorter events, 45.4 us)
Async XLA Ops:
  7.2 116.9 %copy-start.12 = (bf16[1,128,2048]{2,1,0:T(8,128)(2,1)S(1)}, bf16[1,128,2048]{2,1,0:T(8,128)(2,1)}, u32[]{:S(2)}) copy-start(bf16[1,128,2048]{2,1,0:T(8,128)(2,1)} %param.17) | copy-start | bytes 1572868
  7.2 117.1 %copy-start.55 = (f32[64]{0:T(128)S(1)}, f32[64]{0:T(128)}, u32[]{:S(2)}) copy-start(f32[64]{0:T(128)} %param.24) | copy-start | bytes 772
  7.2 212.0 %all-gather.13.cloned.1.call-start = ((), (), s32[]{:S(2)}) async-start(), calls=%async_computation.4 | async-start | bytes 36225024 | tf_op jit(solution)/shard_map/all_gather | solution.py:161
  7.9 335.4 %all-gather.17.cloned.1.call-start = ((), (), s32[]{:S(2)}) async-start(), calls=%async_computation.8 | async-start | bytes 9437184 | tf_op jit(solution)/shard_map/all_gather | solution.py:28
  124.3 95.0 %copy-start.35 = (f32[128]{0:T(128)}, f32[128]{0:T(128)S(1)}, u32[]{:S(2)}) copy-start(f32[128]{0:T(128)S(1)} %fusion.163) | copy-start | bytes 1540
  124.8 114.1 %copy-start.48 = (f32[64]{0:T(128)}, f32[64]{0:T(128)S(1)}, u32[]{:S(2)}) copy-start(f32[64]{0:T(128)S(1)} %exponential_negate_fusion) | copy-start | bytes 772
  125.4 117.2 %copy-start.37 = (f32[128]{0:T(128)}, f32[128]{0:T(128)S(1)}, u32[]{:S(2)}) copy-start(f32[128]{0:T(128)S(1)} %get-tuple-element.371) | copy-start | bytes 1540
  125.5 117.2 %copy-start.39 = (pred[128]{0:T(512)(128)(4,1)}, pred[128]{0:T(512)(128)(4,1)S(1)}, u32[]{:S(2)}) copy-start(pred[128]{0:T(512)(128)(4,1)S(1)} %get-tuple-element.372) | copy-start | bytes 388
  125.5 121.5 %copy-start.29 = (f32[128]{0:T(128)}, f32[128]{0:T(128)S(1)}, u32[]{:S(2)}) copy-start(f32[128]{0:T(128)S(1)} %get-tuple-element.390) | copy-start | bytes 1540
  125.5 121.5 %copy-start.31 = (f32[128]{0:T(128)}, f32[128]{0:T(128)S(1)}, u32[]{:S(2)}) copy-start(f32[128]{0:T(128)S(1)} %get-tuple-element.391) | copy-start | bytes 1540
  125.5 216.6 %copy-start.43 = (f32[128]{0:T(128)}, f32[128]{0:T(128)S(1)}, u32[]{:S(2)}) copy-start(f32[128]{0:T(128)S(1)} %get-tuple-element.387) | copy-start | bytes 1540
  237.2 6.6 copy-start.10
  239.4 5.5 copy-start.41
  241.1 3.3 collective-permute-start
  242.7 118.5 %copy-start.25 = (f32[64,128]{1,0:T(8,128)}, f32[64,128]{1,0:T(8,128)S(1)}, u32[]{:S(2)}) copy-start(f32[64,128]{1,0:T(8,128)S(1)} %get-tuple-element.381) | copy-start | bytes 98308
  247.0 6.7 copy-start.1
  253.8 1.9 copy-start.2
  255.7 5.0 copy-start.52
  258.5 199.8 %all-gather.15.cloned.1.call-start = ((), (), s32[]{:S(2)}) async-start(), calls=%async_computation.5 | async-start | bytes 17301504 | tf_op jit(solution)/shard_map/all_gather | solution.py:205
  259.2 300.0 %all-gather.19.cloned.1.call-start = ((), (), s32[]{:S(2)}) async-start(), calls=%async_computation.9 | async-start | bytes 9437184 | tf_op jit(solution)/shard_map/all_gather | solution.py:51
  260.0 101.3 %copy-start.45 = (f32[64]{0:T(128)}, f32[64]{0:T(128)S(1)}, u32[]{:S(2)}) copy-start(f32[64]{0:T(128)S(1)} %compare_convert_fusion) | copy-start | bytes 772
  328.1 33.1 %copy-start.27 = (pred[128,128]{1,0:T(8,128)(4,1)}, pred[128,128]{1,0:T(8,128)(4,1)S(1)}, u32[]{:S(2)}) copy-start(pred[128,128]{1,0:T(8,128)(4,1)S(1)} %get-tuple-element.385) | copy-start | bytes 49156
  329.0 32.2 %copy-start.23 = (f32[64,128]{1,0:T(8,128)}, f32[64,128]{1,0:T(8,128)S(1)}, u32[]{:S(2)}) copy-start(f32[64,128]{1,0:T(8,128)S(1)} %copy.104) | copy-start | bytes 98308
  358.3 11.6 %copy-start.47 = (bf16[8,1,64]{2,1,0:T(2,128)(2,1)}, bf16[8,1,64]{2,1,0:T(2,128)(2,1)S(1)}, u32[]{:S(2)}) copy-start(bf16[8,1,64]{2,1,0:T(2,128)(2,1)S(1)} %get-tuple-element.546) | copy-start | bytes 3076
  358.3 2.9 copy-start.3
  358.3 2.9 copy-start.53
  361.2 8.7 copy-start.16
  369.9 4.1 copy-start.17
  369.9 88.4 %copy-start.19 = (bf16[1,128,2048]{2,1,0:T(8,128)(2,1)S(1)}, bf16[1,128,2048]{2,1,0:T(8,128)(2,1)}, u32[]{:S(2)}) copy-start(bf16[1,128,2048]{2,1,0:T(8,128)(2,1)} %param.18) | copy-start | bytes 1572868
  458.3 11.5 %copy-start.9 = (f32[1,128,4352]{1,2,0:T(8,128)S(1)}, f32[1,128,4352]{1,2,0:T(8,128)}, u32[]{:S(2)}) copy-start(f32[1,128,4352]{1,2,0:T(8,128)} %copy-done.8) | copy-start | bytes 6684676
  458.3 11.5 %copy-start.11 = (f32[1,128,4096]{1,2,0:T(8,128)S(1)}, f32[1,128,4096]{1,2,0:T(8,128)}, u32[]{:S(2)}) copy-start(f32[1,128,4096]{1,2,0:T(8,128)} %get-tuple-element.370) | copy-start | bytes 6291460
  458.3 11.5 %copy-start.18 = (f32[1,128,64,64]{1,3,2,0:T(8,128)S(1)}, f32[1,128,64,64]{1,3,2,0:T(8,128)}, u32[]{:S(2)}) copy-start(f32[1,128,64,64]{1,3,2,0:T(8,128)} %copy-done.17) | copy-start | bytes 6291460
  469.9 6.1 copy-start.46
  478.8 235.7 %all-gather.23.cloned.1.call-start = ((), (), s32[]{:S(2)}) async-start(), calls=%async_computation.11 | async-start | bytes 4718592 | tf_op jit(solution)/shard_map/all_gather | solution.py:293
  479.4 360.2 %all-gather.21.cloned.1.call-start = ((), (), s32[]{:S(2)}) async-start(), calls=%async_computation.10 | async-start | bytes 19611648 | tf_op jit(solution)/shard_map/all_gather | solution.py:287
  479.5 2.9 copy-start.6
  482.4 1.7 copy-start.24
  482.4 1.7 copy-start.26
  482.4 1.7 copy-start.28
  595.3 5.5 copy-start.34
  595.3 5.5 copy-start.38
  595.3 5.5 copy-start.40
  595.3 5.5 copy-start.42
  595.3 6.5 copy-start.44
  595.3 8.0 copy-start
  603.2 5.4 copy-start.54
  603.3 5.3 copy-start.7
  603.3 5.3 copy-start.22
  608.5 5.5 slice-start
  608.6 5.5 slice-start.1
  608.6 5.5 copy-start.15
  608.6 5.5 copy-start.30
  608.6 5.5 copy-start.32
  626.8 2.0 copy-start.13
  628.8 1.9 copy-start.49
  629.4 5.8 collective-permute-start.1
  636.7 3.6 copy-start.21
  640.3 12.8 %copy-start.14 = (bf16[1,128,4096]{1,2,0:T(8,128)(2,1)S(1)}, bf16[1,128,4096]{1,2,0:T(8,128)(2,1)}, u32[]{:S(2)}) copy-start(bf16[1,128,4096]{1,2,0:T(8,128)(2,1)} %get-tuple-element.383) | copy-start | bytes 3145732
  653.1 224.4 %reduce-scatter.6.cloned.1.call-start = ((), (), s32[]{:S(2)}) async-start(), calls=%async_computation.7 | async-start | bytes 2621440 | tf_op jit(solution)/shard_map/reduce_scatter | solution.py:301
  720.8 281.1 %all-reduce.21.cloned.1.call-start = ((), (), s32[]{:S(2)}) async-start(), calls=%async_computation.12 | async-start | bytes 139264
  766.3 295.6 %reduce-scatter.4.cloned.1.call-start = ((), (), s32[]{:S(2)}) async-start(), calls=%async_computation.6 | async-start | bytes 5488640 | tf_op jit(solution)/shard_map/reduce_scatter | solution.py:298
  858.9 20.7 %copy-start.56 = (f32[64]{0:T(128)S(1)}, f32[64]{0:T(128)}, u32[]{:S(2)}) copy-start(f32[64]{0:T(128)} %param.24) | copy-start | bytes 772
  879.6 66.9 %copy-start.51 = (f32[128]{0:T(128)S(1)}, f32[128]{0:T(128)}, u32[]{:S(2)}) copy-start(f32[128]{0:T(128)} %copy-done.50) | copy-start | bytes 1540
  879.6 66.9 %copy-start.20 = (bf16[1,128,2048]{2,1,0:T(8,128)(2,1)S(1)}, bf16[1,128,2048]{2,1,0:T(8,128)(2,1)}, u32[]{:S(2)}) copy-start(bf16[1,128,2048]{2,1,0:T(8,128)(2,1)} %param.18) | copy-start | bytes 1572868
  (6 other events, 8.0 us)
Sparse Core Ops, SparseCore 0:
  10.9 208.3 all-gather.12
  258.6 83.2 all-gather.16
  344.9 113.4 all-gather.14
  479.0 80.2 all-gather.18
  560.7 45.6 all-gather.22
  653.2 186.3 all-gather.20
  842.6 34.8 reduce-scatter.5
  884.0 117.8 all-reduce.20
  1005.2 56.5 reduce-scatter.3
where the time goes:
time: 1080 us; the launch traced here: 1070 us
  waiting for transfers between devices  437 us (40%)
  blocking collectives  334 us (31%)
  matrix products  139 us (13%)
  other arithmetic  117 us (11%)
  local copies, waits for them, and re-layouts  24.9 us (2%)
  between operations  15.9 us (1%)
    all_gather x1, waiting for transfers between devices, local(): lax.all_gather(in_weight, ('dp', 'seq', 'fsdp'), axis=0, tiled=True)  93.7 us
    all_gather x1, waiting for transfers between devices, local(): lax.all_gather(out_weight, ('dp', 'seq', 'fsdp'), axis=0, tiled=True)  84.3 us
    unnamed x2, blocking collectives  79.2 us
    all_gather x1, waiting for transfers between devices, local(): lax.all_gather(grad_projected, ('seq', 'fsdp'), axis=0, tiled=True)  73.3 us
    all_gather x1, blocking collectives, local(): lax.all_gather(conv_weight, ('dp', 'seq', 'fsdp'), axis=0, tiled=True)  73.2 us
    all_gather x1, blocking collectives, local(): lax.all_gather(gate_gain, ('dp', 'seq', 'fsdp'), axis=0, tiled=True)  67.3 us
    all_to_all x1, blocking collectives, local(): lax.all_to_all(normed_out.reshape(token_count, replicas, members, width_o...  59.6 us
    all_gather x1, waiting for transfers between devices, carried_in(): lax.all_gather(part.astype(kind), axis)  58.8 us
  transfers between devices with their start and end apart: 11, of which 9 were waited for; matrix products, arithmetic and copies ran while one was open for 20% of the time, Pallas kernels for 0%

commit v1 on v0

--- a/solution.py
+++ b/solution.py
@@ -1,6 +1,10 @@
+import functools
+
 import jax
 import jax.numpy as jnp
 from jax import lax
+from jax.experimental import pallas as pl
+from jax.experimental.pallas import tpu as pltpu
 from jax.sharding import PartitionSpec as P
 
 HEADS = 64
@@ -70,7 +74,9 @@
 
 
 def doc_begins(lengths, positions):
-    endings = jnp.cumsum(lengths, axis=1) - lengths
+    places = jnp.arange(lengths.shape[1])
+    ahead = places[:, None] < places[None, :]
+    endings = jnp.sum(jnp.where(ahead[None], lengths[:, :, None], 0), axis=1)
     reached = endings[:, None, :] <= positions[None, :, None]
     return jnp.max(jnp.where(reached, endings[:, None, :], 0), axis=2)
 
@@ -93,7 +99,9 @@
 def scan_parts(signal, key_side, query_side, rate_in, step_bias, log_rate, begins, block_start):
     step = jax.nn.softplus(rate_in + step_bias)
     log_decay = step * -jnp.exp(log_rate)
-    cumulative = jnp.cumsum(log_decay, axis=1)
+    places = jnp.arange(log_decay.shape[1])
+    lower = (places[None, :] <= places[:, None]).astype(jnp.float32)
+    cumulative = jnp.einsum("ts,bsh->bth", lower, log_decay, precision=HIGH)
     by_head = jnp.swapaxes(cumulative, 1, 2)
     indices = jnp.arange(signal.shape[1])
     same_doc = (begins[:, :, None] == begins[:, None, :]) & (
@@ -127,7 +135,7 @@
     return (earlier[0] * later[0], later[1] + later[0][:, :, None, None] * earlier[1])
 
 
-def local(
+def token_split(
     layer_input,
     out_grad,
     norm_gain,
@@ -333,9 +341,1015 @@
     )
 
 
+MESH = pl.DeviceIdType.MESH
+F32 = jnp.float32
+BF16 = jnp.bfloat16
+TILE = 128
+SPAN = 128
+MODEL = 2048
+COMMON = 384
+NEG = -1e30
+LIMIT = 56 * 2**20
+VM = pl.BlockSpec(memory_space=pltpu.VMEM)
+SM = pl.BlockSpec(memory_space=pltpu.SMEM)
+ANY = pl.BlockSpec(memory_space=pl.ANY)
+DMA = pltpu.SemaphoreType.DMA
+
+
+def remote(src, dst, sends, recvs, device):
+    return pltpu.make_async_remote_copy(
+        src_ref=src,
+        dst_ref=dst,
+        send_sem=sends,
+        recv_sem=recvs,
+        device_id=device,
+        device_id_type=MESH,
+    )
+
+
+def dot(a, b, over=((1,), (0,))):
+    return lax.dot_general(a, b, (over, ((), ())), preferred_element_type=F32)
+
+
+def exact(a, b, over=((1,), (0,))):
+    return lax.dot_general(a, b, (over, ((), ())), precision=HIGH, preferred_element_type=F32)
+
+
+def begin_at(place, starts, docs):
+    begin = jnp.zeros_like(place)
+    for doc in range(1, docs):
+        begin = jnp.where(starts[0, doc] <= place, starts[0, doc], begin)
+    return begin
+
+
+def iota(shape, dim):
+    return lax.broadcasted_iota(jnp.int32, shape, dim)
+
+
+def silu_slope(value):
+    gate = jax.nn.sigmoid(value)
+    return gate * (1.0 + value * (1.0 - gate))
+
+
+def softplus(value):
+    return jnp.maximum(value, 0.0) + jnp.log1p(jnp.exp(-jnp.abs(value)))
+
+
+def conv_tile(extended, taps, bias, first, starts, docs, lanes):
+    place = first + iota((SPAN, TILE), 0)
+    begin = begin_at(place, starts, docs)
+    total = jnp.broadcast_to(bias[0:1, lanes], (SPAN, TILE))
+    for tap in range(KW):
+        back = KW - 1 - tap
+        moved = extended if back == 0 else pltpu.roll(extended, back, 0)
+        valid = place - back >= begin
+        total = total + jnp.where(valid, moved[16:], 0.0) * taps[tap : tap + 1, lanes]
+    return total
+
+
+def tile_of(index):
+    return slice(index * TILE, (index + 1) * TILE)
+
+
+def head_col(values, head):
+    return jnp.broadcast_to(values[:, head : head + 1], (SPAN, TILE))
+
+
+class HeadSplit:
+    def __init__(self, nd, nc, nz):
+        self.nd, self.nc, self.nz = nd, nc, nz
+        self.nm = nc * nz
+        self.span = self.nm * SPAN
+        self.rows_in = MODEL // (nd * self.nm)
+
+    def fits(self):
+        return INNER == self.nd * self.nm * TILE and self.rows_in % 16 == 0
+
+    def place(self):
+        return lax.axis_index("dp"), lax.axis_index("seq"), lax.axis_index("fsdp")
+
+    def group_steps(self):
+        return [(e, d) for d in range(self.nz) for e in range(self.nc) if e or d]
+
+    def target(self, step):
+        dp, c, z = self.place()
+        ct, zt = lax.rem(c + step[0], self.nc), lax.rem(z + step[1], self.nz)
+        return (dp, ct, zt), ct * self.nz + zt
+
+    def source(self, step):
+        dp, c, z = self.place()
+        cs, zs = lax.rem(c + self.nc - step[0], self.nc), lax.rem(z + self.nz - step[1], self.nz)
+        return cs * self.nz + zs
+
+    def barrier(self, group=True, line=True):
+        dp, c, z = self.place()
+        sem = pltpu.get_barrier_semaphore()
+        count = 0
+        if group:
+            for step in self.group_steps():
+                pl.semaphore_signal(sem, inc=1, device_id=self.target(step)[0], device_id_type=MESH)
+                count += 1
+        if line:
+            for k in range(1, self.nd):
+                pl.semaphore_signal(
+                    sem, inc=1, device_id=(lax.rem(dp + k, self.nd), c, z), device_id_type=MESH
+                )
+                count += 1
+        pl.semaphore_wait(sem, count)
+
+    def gather_kernel(
+        self, x_ref, par_ref, g_ref, wm_ref, wc_ref, wo_ref,
+        xall, gall, wall, wcall, woall, parall,
+        normed, parbuf, pd_s, pd_r, pg_s, pg_r, wz_s, wz_r, wd_s, wd_r, cz_s, cz_r, cd_s, cd_r,
+        xz_s, xz_r, xc_s, xc_r, gz_s, gz_r, gc_s, gc_r, wo_s, wo_r, loc,
+    ):
+        nd, nc, nz, nm = self.nd, self.nc, self.nz, self.nm
+        dp, c, z = self.place()
+        me = c * nz + z
+        steps = self.group_steps()
+        lines = [(k, lax.rem(dp + k, nd), lax.rem(dp + nd - k, nd)) for k in range(1, nd)]
+        parbuf[dp] = par_ref[...]
+        self.barrier()
+        started = []
+
+        def go(copy):
+            copy.start()
+            started.append(copy)
+
+        for k, to, _ in lines:
+            go(remote(parbuf.at[dp], parbuf.at[dp], pd_s.at[k], pd_r.at[k], (to, c, z)))
+        for j, step in enumerate(steps):
+            device, there = self.target(step)
+            go(remote(wm_ref.at[there], wall.at[dp, me], wz_s.at[j], wz_r.at[j], device))
+            go(remote(wc_ref, wcall.at[dp, me], cz_s.at[j], cz_r.at[j], device))
+        own = [
+            pltpu.make_async_copy(wm_ref.at[me], wall.at[dp, me], loc.at[0]),
+            pltpu.make_async_copy(wc_ref, wcall.at[dp, me], loc.at[1]),
+            pltpu.make_async_copy(g_ref, gall.at[me], loc.at[2]),
+            pltpu.make_async_copy(wo_ref, woall.at[dp], loc.at[3]),
+        ]
+        for copy in own:
+            copy.start()
+        for k, to, _ in lines:
+            go(remote(wo_ref, woall.at[dp], wo_s.at[k], wo_r.at[k], (to, c, z)))
+            go(remote(wm_ref.at[me], wall.at[dp, me], wd_s.at[k, nm - 1], wd_r.at[k, nm - 1], (to, c, z)))
+            go(remote(wc_ref, wcall.at[dp, me], cd_s.at[k, nm - 1], cd_r.at[k, nm - 1], (to, c, z)))
+        for k, to, frm in lines:
+            remote(parbuf.at[frm], parbuf.at[frm], pd_s.at[k], pd_r.at[k], (to, c, z)).wait_recv()
+        parall[me] = parbuf[...]
+        for j, step in enumerate(steps):
+            device, _ = self.target(step)
+            go(remote(parbuf, parall.at[me], pg_s.at[j], pg_r.at[j], device))
+        for j, step in enumerate(steps):
+            device, _ = self.target(step)
+            remote(parbuf, parall.at[self.source(step)], pg_s.at[j], pg_r.at[j], device).wait_recv()
+        gains = []
+        for first in range(0, nd * nm, 2):
+            left = parall[first % nm, first // nm][0:1, : self.rows_in]
+            right = parall[(first + 1) % nm, (first + 1) // nm][0:1, : self.rows_in]
+            gains.append(jnp.concatenate([left, right], axis=1))
+        gain = jnp.concatenate(gains, axis=1)
+        hidden = x_ref[...].astype(F32)
+        inverse = lax.rsqrt(jnp.mean(hidden * hidden, axis=1, keepdims=True) + EPSILON)
+        normed[...] = (hidden * inverse * gain).astype(BF16)
+        mine = pltpu.make_async_copy(normed, xall.at[me], loc.at[4])
+        mine.start()
+        own.append(mine)
+        other = (dp, nc - 1 - c, z)
+
+        def spread(source, every, z_s, z_r, c_s, c_r):
+            for d in range(1, nz):
+                go(remote(source, every.at[me], z_s.at[d], z_r.at[d], (dp, c, lax.rem(z + d, nz))))
+            go(remote(source, every.at[me], c_s.at[0], c_r.at[0], other))
+
+        spread(normed, xall, xz_s, xz_r, xc_s, xc_r)
+        spread(g_ref, gall, gz_s, gz_r, gc_s, gc_r)
+        for j, step in enumerate(steps):
+            device, _ = self.target(step)
+            frm = self.source(step)
+            block, common = wall.at[dp, frm], wcall.at[dp, frm]
+            remote(block, block, wz_s.at[j], wz_r.at[j], device).wait_recv()
+            remote(common, common, cz_s.at[j], cz_r.at[j], device).wait_recv()
+            for k, to, _ in lines:
+                go(remote(block, block, wd_s.at[k, j], wd_r.at[k, j], (to, c, z)))
+                go(remote(common, common, cd_s.at[k, j], cd_r.at[k, j], (to, c, z)))
+
+        def pass_on(every, z_s, z_r, c_s, c_r):
+            for d in range(1, nz):
+                block = every.at[c * nz + lax.rem(z + nz - d, nz)]
+                remote(block, block, z_s.at[d], z_r.at[d], other).wait_recv()
+                go(remote(block, block, c_s.at[d], c_r.at[d], other))
+
+        pass_on(xall, xz_s, xz_r, xc_s, xc_r)
+        pass_on(gall, gz_s, gz_r, gc_s, gc_r)
+        for d in range(nz):
+            frm = (nc - 1 - c) * nz + lax.rem(z + nz - d, nz)
+            remote(xall.at[frm], xall.at[frm], xc_s.at[d], xc_r.at[d], other).wait_recv()
+            remote(gall.at[frm], gall.at[frm], gc_s.at[d], gc_r.at[d], other).wait_recv()
+        for k, to, frm in lines:
+            remote(woall.at[frm], woall.at[frm], wo_s.at[k], wo_r.at[k], (to, c, z)).wait_recv()
+            for j in range(nm):
+                here = me if j == nm - 1 else self.source(steps[j])
+                block, common = wall.at[frm, here], wcall.at[frm, here]
+                remote(block, block, wd_s.at[k, j], wd_r.at[k, j], (to, c, z)).wait_recv()
+                remote(common, common, cd_s.at[k, j], cd_r.at[k, j], (to, c, z)).wait_recv()
+        for copy in own:
+            copy.wait()
+        for copy in started:
+            copy.wait_send()
+
+    def gather(self, x, par, g, wm, wc, wo):
+        nd, nz, nm, rows = self.nd, self.nz, self.nm, self.rows_in
+        out = [
+            jax.ShapeDtypeStruct((nm, SPAN, MODEL), BF16),
+            jax.ShapeDtypeStruct((nm, SPAN, MODEL), BF16),
+            jax.ShapeDtypeStruct((nd, nm, rows, 2 * nd * TILE), BF16),
+            jax.ShapeDtypeStruct((nd, nm, rows, COMMON), BF16),
+            jax.ShapeDtypeStruct((nd, TILE, MODEL), BF16),
+            jax.ShapeDtypeStruct((nm, nd, 8, TILE), F32),
+        ]
+        return pl.pallas_call(
+            self.gather_kernel,
+            out_shape=out,
+            in_specs=[VM, VM, ANY, ANY, ANY, ANY],
+            out_specs=[ANY, ANY, ANY, ANY, ANY, VM],
+            scratch_shapes=[
+                pltpu.VMEM((SPAN, MODEL), BF16),
+                pltpu.VMEM((nd, 8, TILE), F32),
+                DMA((nd,)), DMA((nd,)), DMA((nm,)), DMA((nm,)),
+                DMA((nm,)), DMA((nm,)), DMA((nd, nm)), DMA((nd, nm)),
+                DMA((nm,)), DMA((nm,)), DMA((nd, nm)), DMA((nd, nm)),
+                DMA((nz,)), DMA((nz,)), DMA((nz,)), DMA((nz,)),
+                DMA((nz,)), DMA((nz,)), DMA((nz,)), DMA((nz,)),
+                DMA((nd,)), DMA((nd,)), DMA((5,)),
+            ],
+            compiler_params=pltpu.CompilerParams(
+                collective_id=0, has_side_effects=True, vmem_limit_bytes=LIMIT
+            ),
+            name="gather",
+        )(x, par, g, wm, wc, wo)
+
+    def forward_kernel(
+        self, docs, starts, pm, pm_prev, pc, pc_prev, g, wo, taps, bias, sel, hp, chp,
+        pre_sig, pre_bc, o, sin, step_o, cum_o, dg_o, y_o, st_o, state,
+    ):
+        nd = self.nd
+        chunk = pl.program_id(0)
+        first = chunk * SPAN
+
+        @pl.when(chunk == 0)
+        def _():
+            state[...] = jnp.zeros_like(state)
+
+        lane = iota((SPAN, TILE), 1)
+        row = iota((SPAN, TILE), 0)
+        for i in range(nd):
+            lanes = tile_of(i)
+            cols = slice(nd * TILE + i * TILE, nd * TILE + (i + 1) * TILE)
+            ext = jnp.concatenate([pm_prev[SPAN - 16 :, lanes], pm[:, cols]], axis=0).astype(F32)
+            pre_sig[:, lanes] = conv_tile(ext, taps, bias, first, starts, docs, lanes)
+        sides = []
+        for i in range(2):
+            lanes = tile_of(i)
+            ext = jnp.concatenate([pc_prev[SPAN - 16 :, lanes], pc[:, lanes]], axis=0).astype(F32)
+            value = conv_tile(ext, taps, bias, first, starts, docs, tile_of(nd + i))
+            pre_bc[:, lanes] = value
+            sides.append((value * jax.nn.sigmoid(value)).astype(BF16))
+        key_side, query_side = sides
+        rate = dot(pc[:, 2 * TILE :], sel[...])
+        step = softplus(rate + hp[0:1, :])
+        log_decay = step * hp[1:2, :]
+        lower = (lane <= row).astype(F32)
+        cum = exact(lower, log_decay)
+        step_o[...] = step
+        cum_o[...] = cum
+        cum_t = cum.T
+        begin_t = begin_at(first + row, starts, docs)
+        begin_s = begin_at(first + lane, starts, docs)
+        shut = jnp.where((begin_t == begin_s) & (lane <= row), 0.0, NEG)
+        inherits = (begin_t < first).astype(F32)
+        begin_last = begin_at(jnp.full((SPAN, TILE), first + SPAN - 1, jnp.int32), starts, docs)
+        last_same = (begin_t == begin_last).astype(F32)
+        meet = dot(query_side, key_side, ((1,), (1,)))
+        before = state[...]
+        sin[0] = before
+        carried_out = dot(query_side, before.astype(BF16))
+        squares = jnp.zeros((SPAN, TILE), F32)
+        crosses = jnp.zeros((SPAN, TILE), F32)
+        lefts, fulls = [], []
+        grad = dot(g[...], wo[...], ((1,), (1,)))
+        dg_o[...] = grad
+        for i in range(nd):
+            lanes = tile_of(i)
+            low = lane < TILE // 2
+            pre = pre_sig[:, lanes]
+            signal = pre * jax.nn.sigmoid(pre)
+            cums = [head_col(cum, 2 * i), head_col(cum, 2 * i + 1)]
+            stepx = jnp.where(low, head_col(step, 2 * i), head_col(step, 2 * i + 1))
+            cumx = jnp.where(low, cums[0], cums[1])
+            fed = stepx * signal
+            fed_low = fed.astype(BF16)
+            local = []
+            for e in range(2):
+                head = 2 * i + e
+                kernel = jnp.exp(cums[e] - cum_t[head : head + 1, :] + shut)
+                local.append(dot((kernel * meet).astype(BF16), fed_low))
+            entry = jnp.exp(cumx) * inherits
+            out = jnp.where(low, local[0], local[1]) + entry * carried_out[:, lanes]
+            o[:, lanes] = out
+            last = cumx[SPAN - 1 : SPAN, :]
+            tail = jnp.exp((last - cumx) * last_same) * last_same
+            state[:, lanes] = entry[SPAN - 1 : SPAN, :] * before[:, lanes] + dot(
+                key_side, (tail * fed).astype(BF16), ((0,), (0,))
+            )
+            mixed = (out + chp[0:1, lanes] * signal) * chp[1:2, lanes]
+            gate_in = pm[:, lanes].astype(F32)
+            gated = mixed * (gate_in * jax.nn.sigmoid(gate_in))
+            scaled = gated * chp[2:3, lanes]
+            squares = squares + gated * gated
+            crosses = crosses + scaled * grad[:, lanes]
+            fulls.append(scaled.astype(BF16))
+        y_o[...] = dot(jnp.concatenate(fulls, axis=1), wo[...]).astype(BF16)
+        square = jnp.broadcast_to(jnp.sum(squares, axis=1, keepdims=True), (SPAN, TILE))
+        cross = jnp.broadcast_to(jnp.sum(crosses, axis=1, keepdims=True), (SPAN, TILE))
+        both = jnp.where(lane == 0, square, jnp.where(lane == 1, cross, 0.0))
+        st_o[0] = both.T[0:8, :]
+
+    def forward(self, docs, starts, projm, projc, gall, wo, taps, bias, sel, hp, chp):
+        nd, nm, span = self.nd, self.nm, self.span
+        wide = nd * TILE
+        whole = lambda shape: pl.BlockSpec(shape, lambda i: (0,) * len(shape))
+        prev = lambda i: jnp.maximum(i - 1, 0)
+        return pl.pallas_call(
+            functools.partial(self.forward_kernel, docs),
+            grid=(nm,),
+            in_specs=[
+                SM,
+                pl.BlockSpec((SPAN, 2 * wide), lambda i: (i, 0)),
+                pl.BlockSpec((SPAN, wide), lambda i: (prev(i), 1)),
+                pl.BlockSpec((SPAN, COMMON), lambda i: (i, 0)),
+                pl.BlockSpec((SPAN, COMMON), lambda i: (prev(i), 0)),
+                pl.BlockSpec((SPAN, MODEL), lambda i: (i, 0)),
+                whole((wide, MODEL)),
+                whole(taps.shape),
+                whole(bias.shape),
+                whole(sel.shape),
+                whole(hp.shape),
+                whole(chp.shape),
+            ],
+            out_specs=[
+                pl.BlockSpec((SPAN, wide), lambda i: (i, 0)),
+                pl.BlockSpec((SPAN, 2 * TILE), lambda i: (i, 0)),
+                pl.BlockSpec((SPAN, wide), lambda i: (i, 0)),
+                pl.BlockSpec((1, STATE, wide), lambda i: (i, 0, 0)),
+                pl.BlockSpec((SPAN, TILE), lambda i: (i, 0)),
+                pl.BlockSpec((SPAN, TILE), lambda i: (i, 0)),
+                pl.BlockSpec((SPAN, wide), lambda i: (i, 0)),
+                pl.BlockSpec((SPAN, MODEL), lambda i: (i, 0)),
+                pl.BlockSpec((1, 8, TILE), lambda i: (i, 0, 0)),
+            ],
+            out_shape=[
+                jax.ShapeDtypeStruct((span, wide), F32),
+                jax.ShapeDtypeStruct((span, 2 * TILE), F32),
+                jax.ShapeDtypeStruct((span, wide), F32),
+                jax.ShapeDtypeStruct((nm, STATE, wide), F32),
+                jax.ShapeDtypeStruct((span, TILE), F32),
+                jax.ShapeDtypeStruct((span, TILE), F32),
+                jax.ShapeDtypeStruct((span, wide), F32),
+                jax.ShapeDtypeStruct((span, MODEL), BF16),
+                jax.ShapeDtypeStruct((nm, 8, TILE), F32),
+            ],
+            scratch_shapes=[pltpu.VMEM((STATE, wide), F32)],
+            compiler_params=pltpu.CompilerParams(vmem_limit_bytes=LIMIT),
+            name="forward",
+        )(starts, projm, projm, projc, projc, gall, wo, taps, bias, sel, hp, chp)
+
+    def stats_kernel(self, st, total, heard, sends, recvs):
+        steps = self.group_steps()
+        self.barrier(line=False)
+        copies = []
+        for j, step in enumerate(steps):
+            device, _ = self.target(step)
+            copy = remote(st, heard.at[j], sends.at[j], recvs.at[j], device)
+            copy.start()
+            copies.append(copy)
+        value = st[...]
+        for j, copy in enumerate(copies):
+            copy.wait_recv()
+            value = value + heard[j]
+        total[...] = value
+        for copy in copies:
+            copy.wait_send()
+
+    def stats(self, st):
+        n = self.nm - 1
+        return pl.pallas_call(
+            self.stats_kernel,
+            out_shape=jax.ShapeDtypeStruct(st.shape, F32),
+            in_specs=[VM],
+            out_specs=VM,
+            scratch_shapes=[pltpu.VMEM((n, *st.shape), F32), DMA((n,)), DMA((n,))],
+            compiler_params=pltpu.CompilerParams(collective_id=1, has_side_effects=True),
+            name="stats",
+        )(st)
+
+    def backward_kernel(
+        self, docs, starts, unit, pm, pm_prev, pre_sig, pre_bc, o, sin, step_i, cum_i, dg_i, st, taps, sel, hp, chp,
+        dproj, dcom, normed_out, sums, heads, dstate, dnext,
+    ):
+        nd = self.nd
+        chunk = self.nm - 1 - pl.program_id(0)
+        first = chunk * SPAN
+
+        @pl.when(pl.program_id(0) == 0)
+        def _():
+            dstate[...] = jnp.zeros_like(dstate)
+            dnext[...] = jnp.zeros_like(dnext)
+            sums[...] = jnp.zeros_like(sums)
+            heads[...] = jnp.zeros_like(heads)
+
+        lane = iota((SPAN, TILE), 1)
+        row = iota((SPAN, TILE), 0)
+        low = lane < TILE // 2
+        begin_t = begin_at(first + row, starts, docs)
+        begin_s = begin_at(first + lane, starts, docs)
+        shut = jnp.where((begin_t == begin_s) & (lane <= row), 0.0, NEG)
+        inherits = (begin_t < first).astype(F32)
+        begin_last = begin_at(jnp.full((SPAN, TILE), first + SPAN - 1, jnp.int32), starts, docs)
+        last_same = (begin_t == begin_last).astype(F32)
+        lower = (lane <= row).astype(F32)
+        key_pre, query_pre = pre_bc[:, :TILE], pre_bc[:, TILE:]
+        key_side = (key_pre * jax.nn.sigmoid(key_pre)).astype(BF16)
+        query_side = (query_pre * jax.nn.sigmoid(query_pre)).astype(BF16)
+        meet = dot(query_side, key_side, ((1,), (1,)))
+        step, cum = step_i[...], cum_i[...]
+        cum_t = cum.T
+        stat = jnp.concatenate([st[0], jnp.zeros((SPAN - 8, TILE), F32)], axis=0).T
+        square, cross = head_col(stat, 0), head_col(stat, 1)
+        root = lax.rsqrt(square * unit[0, 0] + EPSILON)
+        pull = root * root * root * cross * unit[0, 0]
+        before = sin[0]
+        before_low = before.astype(BF16)
+        after = dstate[...]
+        after_low = after.astype(BF16)
+        carried_out = dot(query_side, before_low)
+        from_state = dot(key_side, after_low)
+        meet_grad = jnp.zeros((SPAN, SPAN), F32)
+        cum_cols = jnp.zeros((SPAN, TILE), F32)
+        cum_rows = jnp.zeros((8, SPAN), F32)
+        step_cols = jnp.zeros((SPAN, TILE), F32)
+        entered, tails, lasts = [], [], []
+        head_rows = iota((8, SPAN), 0)
+        next_rows = first + iota((SPAN + 16, TILE), 0)
+        next_begin = begin_at(next_rows, starts, docs)
+        tail_row = iota((SPAN, TILE), 0) == SPAN - 1
+        for i in range(nd):
+            lanes = tile_of(i)
+            pre = pre_sig[:, lanes]
+            gate_of = jax.nn.sigmoid(pre)
+            signal = pre * gate_of
+            gate_in = pm[:, lanes].astype(F32)
+            gate_sig = jax.nn.sigmoid(gate_in)
+            opened = gate_in * gate_sig
+            mask = chp[1:2, lanes]
+            mixed = (o[:, lanes] + chp[0:1, lanes] * signal) * mask
+            gated = mixed * opened
+            grad = dg_i[:, lanes]
+            gain = chp[2:3, lanes]
+            normed_out[:, lanes] = (gated * root * gain).astype(BF16)
+            sums[0:1, lanes] += jnp.sum(grad * gated * root, axis=0, keepdims=True)
+            gated_grad = root * grad * gain - gated * pull
+            mixed_grad = gated_grad * opened * mask
+            dproj[:, lanes] = (
+                gated_grad * mixed * (gate_sig * (1.0 + gate_in * (1.0 - gate_sig)))
+            ).astype(BF16)
+            sums[1:2, lanes] += jnp.sum(mixed_grad * signal, axis=0, keepdims=True)
+            cums = [head_col(cum, 2 * i), head_col(cum, 2 * i + 1)]
+            stepx = jnp.where(low, head_col(step, 2 * i), head_col(step, 2 * i + 1))
+            cumx = jnp.where(low, cums[0], cums[1])
+            fed = stepx * signal
+            fed_low = fed.astype(BF16)
+            out_grad = mixed_grad
+            out_low = out_grad.astype(BF16)
+            entry = jnp.exp(cumx) * inherits
+            last = cumx[SPAN - 1 : SPAN, :]
+            tail = jnp.exp((last - cumx) * last_same) * last_same
+            backs = []
+            for e in range(2):
+                head = 2 * i + e
+                kernel = jnp.exp(cums[e] - cum_t[head : head + 1, :] + shut)
+                mix = kernel * meet
+                half = low if e == 0 else jnp.logical_not(low)
+                mix_grad = dot(jnp.where(half, out_grad, 0.0).astype(BF16), fed_low, ((1,), (1,)))
+                meet_grad = meet_grad + kernel * mix_grad
+                weight = mix * mix_grad
+                cum_cols = cum_cols + jnp.where(
+                    lane == head, jnp.broadcast_to(jnp.sum(weight, axis=1, keepdims=True), (SPAN, TILE)), 0.0
+                )
+                cum_rows = cum_rows + jnp.where(
+                    head_rows == head, jnp.broadcast_to(jnp.sum(weight, axis=0, keepdims=True), (8, SPAN)), 0.0
+                )
+                backs.append(dot(mix.astype(BF16), out_low, ((0,), (0,))))
+            entry_grad = entry * out_grad
+            tail_fed = tail * fed
+            entered.append(entry_grad.astype(BF16))
+            tails.append(tail_fed.astype(BF16))
+            fed_grad = jnp.where(low, backs[0], backs[1]) + tail * from_state[:, lanes]
+            moved_in = entry_grad * carried_out[:, lanes]
+            moved_out = tail_fed * from_state[:, lanes]
+            direct = fed_grad * signal
+            end = entry[SPAN - 1 : SPAN, :]
+            kept = jnp.sum(after[:, lanes] * before[:, lanes], axis=0, keepdims=True) * end
+            at_end = jnp.sum(moved_out, axis=0, keepdims=True) + kept
+            local = moved_in - moved_out + jnp.where(tail_row, at_end, 0.0)
+            for e in range(2):
+                half = low if e == 0 else jnp.logical_not(low)
+                place = lane == 2 * i + e
+                cum_cols = cum_cols + jnp.where(
+                    place,
+                    jnp.broadcast_to(jnp.sum(jnp.where(half, local, 0.0), axis=1, keepdims=True), (SPAN, TILE)),
+                    0.0,
+                )
+                step_cols = step_cols + jnp.where(
+                    place,
+                    jnp.broadcast_to(jnp.sum(jnp.where(half, direct, 0.0), axis=1, keepdims=True), (SPAN, TILE)),
+                    0.0,
+                )
+            dstate[:, lanes] = end * after[:, lanes] + dot(
+                query_side, entry_grad.astype(BF16), ((0,), (0,))
+            )
+            signal_grad = stepx * fed_grad + chp[0:1, lanes] * mixed_grad
+            pre_grad = signal_grad * (gate_of * (1.0 + pre * (1.0 - gate_of)))
+            sums[2:3, lanes] += jnp.sum(pre_grad, axis=0, keepdims=True)
+            later = jnp.concatenate([pre_grad, dnext[:, lanes]], axis=0)
+            dnext[:, lanes] = pre_grad[0:16, :]
+            cols = slice(nd * TILE + i * TILE, nd * TILE + (i + 1) * TILE)
+            ext = jnp.concatenate([pm_prev[SPAN - 16 :, lanes], pm[:, cols]], axis=0).astype(F32)
+            back_grad = jnp.zeros((SPAN, TILE), F32)
+            for tap in range(KW):
+                back = KW - 1 - tap
+                masked = jnp.where(next_rows - back >= next_begin, later, 0.0)
+                moved = ext if back == 0 else pltpu.roll(ext, back, 0)
+                sums[4 + tap : 5 + tap, lanes] += jnp.sum(
+                    masked[:SPAN] * moved[16:], axis=0, keepdims=True
+                )
+                ahead = masked if back == 0 else pltpu.roll(masked, SPAN + 16 - back, 0)
+                back_grad = back_grad + ahead[:SPAN] * taps[tap : tap + 1, lanes]
+            dproj[:, cols] = back_grad.astype(BF16)
+        meet_low = meet_grad.astype(BF16)
+        state_rows = ((1,), (1,))
+        query_grad = dot(meet_low, key_side) + dot(jnp.concatenate(entered, axis=1), before_low, state_rows)
+        key_grad = dot(meet_low, query_side, ((0,), (0,))) + dot(
+            jnp.concatenate(tails, axis=1), after_low, state_rows
+        )
+        dcom[:, :TILE] = key_grad.astype(BF16)
+        dcom[:, TILE : 2 * TILE] = query_grad.astype(BF16)
+        rows_t = jnp.concatenate([cum_rows, jnp.zeros((SPAN - 8, SPAN), F32)], axis=0).T
+        decay_grad = exact(lower, cum_cols - rows_t, ((0,), (0,)))
+        log_decay = step * hp[1:2, :]
+        slope = 1.0 - jnp.exp(-step)
+        rate_grad = (step_cols + decay_grad * hp[1:2, :]) * slope
+        heads[0:1, :] += jnp.sum(rate_grad, axis=0, keepdims=True)
+        heads[1:2, :] += jnp.sum(decay_grad * log_decay, axis=0, keepdims=True)
+        dcom[:, 2 * TILE :] = dot(rate_grad.astype(BF16), sel[...], ((1,), (1,))).astype(BF16)
+
+    def backward(
+        self, docs, starts, unit, projm, pre_sig, pre_bc, o, sin, step, cum, dg, st, taps, sel, hp, chp
+    ):
+        nd, nm, span = self.nd, self.nm, self.span
+        wide = nd * TILE
+        whole = lambda shape: pl.BlockSpec(shape, lambda i: (0,) * len(shape))
+        at = lambda i: nm - 1 - i
+        prev = lambda i: jnp.maximum(nm - 2 - i, 0)
+        return pl.pallas_call(
+            functools.partial(self.backward_kernel, docs),
+            grid=(nm,),
+            in_specs=[
+                SM,
+                SM,
+                pl.BlockSpec((SPAN, 2 * wide), lambda i: (at(i), 0)),
+                pl.BlockSpec((SPAN, wide), lambda i: (prev(i), 1)),
+                pl.BlockSpec((SPAN, wide), lambda i: (at(i), 0)),
+                pl.BlockSpec((SPAN, 2 * TILE), lambda i: (at(i), 0)),
+                pl.BlockSpec((SPAN, wide), lambda i: (at(i), 0)),
+                pl.BlockSpec((1, STATE, wide), lambda i: (at(i), 0, 0)),
+                pl.BlockSpec((SPAN, TILE), lambda i: (at(i), 0)),
+                pl.BlockSpec((SPAN, TILE), lambda i: (at(i), 0)),
+                pl.BlockSpec((SPAN, wide), lambda i: (at(i), 0)),
+                pl.BlockSpec((1, 8, TILE), lambda i: (at(i), 0, 0)),
+                whole(taps.shape),
+                whole(sel.shape),
+                whole(hp.shape),
+                whole(chp.shape),
+            ],
+            out_specs=[
+                pl.BlockSpec((SPAN, 2 * wide), lambda i: (at(i), 0)),
+                pl.BlockSpec((SPAN, COMMON), lambda i: (at(i), 0)),
+                pl.BlockSpec((SPAN, wide), lambda i: (at(i), 0)),
+                whole((8, wide)),
+                whole((8, TILE)),
+            ],
+            out_shape=[
+                jax.ShapeDtypeStruct((span, 2 * wide), BF16),
+                jax.ShapeDtypeStruct((span, COMMON), BF16),
+                jax.ShapeDtypeStruct((span, wide), BF16),
+                jax.ShapeDtypeStruct((8, wide), F32),
+                jax.ShapeDtypeStruct((8, TILE), F32),
+            ],
+            scratch_shapes=[pltpu.VMEM((STATE, wide), F32), pltpu.VMEM((16, wide), F32)],
+            compiler_params=pltpu.CompilerParams(vmem_limit_bytes=LIMIT),
+            name="backward",
+        )(starts, unit, projm, projm, pre_sig, pre_bc, o, sin, step, cum, dg, st, taps, sel, hp, chp)
+
+    def common_kernel(
+        self, docs, starts, dcom, pre_bc, projc, taps, every, sums, padded, heard, mine,
+        sends, recvs, back_s, back_r,
+    ):
+        nm = self.nm
+        dp, c, z = self.place()
+        me = c * self.nz + z
+        steps = self.group_steps()
+        padded[0 : self.span, :] = dcom[...]
+        padded[self.span :, :] = jnp.zeros((16, COMMON), BF16)
+        self.barrier(line=False)
+        copies = []
+        long = SPAN + 16
+        for j, step in enumerate(steps):
+            device, there = self.target(step)
+            src = padded.at[pl.ds(pl.multiple_of(there * SPAN, SPAN), long), :]
+            copy = remote(src, heard.at[j], sends.at[j], recvs.at[j], device)
+            copy.start()
+            copies.append(copy)
+        base = pl.multiple_of(me * SPAN, SPAN)
+        total = padded[pl.ds(base, long), :].astype(F32)
+        for j, copy in enumerate(copies):
+            copy.wait_recv()
+            total = total + heard[j].astype(F32)
+        after = pl.multiple_of(lax.rem(me + 1, nm) * SPAN, SPAN)
+        ahead = pl.multiple_of(lax.rem(me + nm - 1, nm) * SPAN + SPAN - 16, 16)
+        rows = base + iota((long, TILE), 0)
+        begin = begin_at(rows, starts, docs)
+        inside = rows < self.span
+        for i in range(2):
+            lanes = tile_of(i)
+            pre = jnp.concatenate([pre_bc[pl.ds(base, SPAN), lanes], pre_bc[pl.ds(after, 16), lanes]], axis=0)
+            later = jnp.where(inside, total[:, lanes] * silu_slope(pre), 0.0)
+            ext = jnp.concatenate([projc[pl.ds(ahead, 16), lanes], projc[pl.ds(base, SPAN), lanes]], axis=0)
+            ext = ext.astype(F32)
+            sums[i : i + 1, :] = jnp.sum(later[:SPAN], axis=0, keepdims=True)
+            back_grad = jnp.zeros((SPAN, TILE), F32)
+            for tap in range(KW):
+                back = KW - 1 - tap
+                masked = jnp.where(rows - back >= begin, later, 0.0)
+                moved = ext if back == 0 else pltpu.roll(ext, back, 0)
+                sums[2 + 2 * tap + i : 3 + 2 * tap + i, :] = jnp.sum(
+                    masked[:SPAN] * moved[16:], axis=0, keepdims=True
+                )
+                shifted_up = masked if back == 0 else pltpu.roll(masked, long - back, 0)
+                side = tile_of(self.nd + i)
+                back_grad = back_grad + shifted_up[:SPAN] * taps[tap : tap + 1, side]
+            mine[:, lanes] = back_grad.astype(BF16)
+        mine[:, 2 * TILE :] = total[:SPAN, 2 * TILE :].astype(BF16)
+        sums[10:16, :] = jnp.zeros((6, TILE), F32)
+        every[me] = mine[...]
+        outs = []
+        for j, step in enumerate(steps):
+            device, _ = self.target(step)
+            copy = remote(mine, every.at[me], back_s.at[j], back_r.at[j], device)
+            copy.start()
+            outs.append(copy)
+        for j, step in enumerate(steps):
+            device, _ = self.target(step)
+            block = every.at[self.source(step)]
+            remote(mine, block, back_s.at[j], back_r.at[j], device).wait_recv()
+        for copy in copies + outs:
+            copy.wait_send()
+
+    def common(self, docs, starts, dcom, pre_bc, projc, taps):
+        nm = self.nm
+        n = nm - 1
+        return pl.pallas_call(
+            functools.partial(self.common_kernel, docs),
+            out_shape=[jax.ShapeDtypeStruct((nm, SPAN, COMMON), BF16), jax.ShapeDtypeStruct((16, TILE), F32)],
+            in_specs=[SM, VM, VM, VM, VM],
+            out_specs=[VM, VM],
+            scratch_shapes=[
+                pltpu.VMEM((self.span + 16, COMMON), BF16),
+                pltpu.VMEM((n, SPAN + 16, COMMON), BF16),
+                pltpu.VMEM((SPAN, COMMON), BF16),
+                DMA((n,)), DMA((n,)), DMA((n,)), DMA((n,)),
+            ],
+            compiler_params=pltpu.CompilerParams(
+                collective_id=2, has_side_effects=True, vmem_limit_bytes=LIMIT
+            ),
+            name="common",
+        )(starts, dcom, pre_bc, projc, taps)
+
+    def reduce_kernel(
+        self, unit, yp, dxp, dwp, dwop, dwcp, parp, x_ref, g_ref, dxc, st, gain,
+        y_out, dx_out, dw_out, dwo_out, dwc_out, par_out,
+        yc, xc, ysum, xsum, yz, xz, wd, wod, wcd, wsum, pard, parbuf,
+        yc_s, yc_r, xc_s, xc_r, yz_s, yz_r, xz_s, xz_r, wd_s, wd_r, wod_s, wod_r, wcd_s, wcd_r,
+        wz_s, wz_r, pd_s, pd_r, pg_s, pg_r,
+    ):
+        nd, nc, nz, nm = self.nd, self.nc, self.nz, self.nm
+        dp, c, z = self.place()
+        me = c * nz + z
+        steps = self.group_steps()
+        lines = [(k, (lax.rem(dp + k, nd), c, z), lax.rem(dp + k, nd)) for k in range(1, nd)]
+        self.barrier()
+        started = []
+
+        def go(copy):
+            copy.start()
+            started.append(copy)
+            return copy
+
+        other = (dp, nc - 1 - c, z)
+        theirs = pl.ds((nc - 1 - c) * nz, nz)
+        cores = [
+            go(remote(yp.at[theirs], yc, yc_s, yc_r, other)),
+            go(remote(dxp.at[theirs], xc, xc_s, xc_r, other)),
+        ]
+        overs = []
+        for k, device, to in lines:
+            overs.append(go(remote(dwp.at[to], wd.at[k - 1], wd_s.at[k], wd_r.at[k], device)))
+            overs.append(go(remote(dwop.at[to], wod.at[k - 1], wod_s.at[k], wod_r.at[k], device)))
+            overs.append(go(remote(dwcp.at[to], wcd.at[k - 1], wcd_s.at[k], wcd_r.at[k], device)))
+        zs = []
+        for part, came, total, heard, z_s, z_r, core in (
+            (yp, yc, ysum, yz, yz_s, yz_r, cores[0]),
+            (dxp, xc, xsum, xz, xz_s, xz_r, cores[1]),
+        ):
+            core.wait_recv()
+            for d in range(nz):
+                there = lax.rem(z + d, nz)
+
+                def add(r, _, part=part, came=came, total=total, there=there):
+                    at = pl.ds(pl.multiple_of(r * 16, 16), 16)
+                    total[there, at, :] = (
+                        part[c * nz + there, at, :].astype(F32) + came[there, at, :].astype(F32)
+                    ).astype(BF16)
+                    return 0
+
+                lax.fori_loop(0, SPAN // 16, add, 0)
+                if d:
+                    zs.append(
+                        go(remote(total.at[there], heard.at[d - 1], z_s.at[d], z_r.at[d], (dp, c, there)))
+                    )
+        for copy in overs:
+            copy.wait_recv()
+
+        def add_weight(r, _):
+            at = pl.ds(pl.multiple_of(r * 16, 16), 16)
+            total = dwp[dp, at, :].astype(F32)
+            for k in range(nd - 1):
+                total = total + wd[k, at, :].astype(F32)
+            wsum[at, :] = total.astype(BF16)
+            return 0
+
+        lax.fori_loop(0, nm * self.rows_in // 16, add_weight, 0)
+        block = lambda m: wsum.at[pl.ds(pl.multiple_of(m * self.rows_in, self.rows_in), self.rows_in), :]
+        for j, step in enumerate(steps):
+            device, there = self.target(step)
+            go(remote(block(there), dw_out.at[me], wz_s.at[j], wz_r.at[j], device))
+        dw_out[me] = block(me)[...]
+
+        def add_out(r, _):
+            at = pl.ds(pl.multiple_of(r * 16, 16), 16)
+            total = dwop[dp, at, :].astype(F32)
+            for k in range(nd - 1):
+                total = total + wod[k, at, :].astype(F32)
+            dwo_out[at, :] = total
+            return 0
+
+        lax.fori_loop(0, TILE // 16, add_out, 0)
+        total = dwcp[dp].astype(F32)
+        for k in range(nd - 1):
+            total = total + wcd[k].astype(F32)
+        dwc_out[...] = total
+        for copy in zs:
+            copy.wait_recv()
+        stat = jnp.concatenate([st[me], jnp.zeros((SPAN - 8, TILE), F32)], axis=0).T
+        square = stat[:, 0:1]
+        root = lax.rsqrt(square * unit[0, 0] + EPSILON)
+        hidden = x_ref[...].astype(F32)
+        branch = ysum[z].astype(F32)
+        normed_grad = xsum[z].astype(F32) + dxc[...]
+        for d in range(nz - 1):
+            branch = branch + yz[d].astype(F32)
+            normed_grad = normed_grad + xz[d].astype(F32)
+        y_out[...] = (hidden + root * branch).astype(BF16)
+        inverse = lax.rsqrt(jnp.mean(hidden * hidden, axis=1, keepdims=True) + EPSILON)
+        unitary = hidden * inverse
+        gain_grad = jnp.sum(normed_grad * unitary, axis=0, keepdims=True)
+        scaled = normed_grad * gain[0:1, :]
+        middle = jnp.mean(scaled * unitary, axis=1, keepdims=True)
+        dx_out[...] = (g_ref[...].astype(F32) + inverse * (scaled - unitary * middle)).astype(BF16)
+        parbuf[...] = parp[...]
+        for i in range(MODEL // TILE):
+            parbuf[i : i + 1, :] = gain_grad[:, tile_of(i)]
+        small = [
+            go(remote(parbuf, pard.at[k - 1], pd_s.at[k], pd_r.at[k], device)) for k, device, _ in lines
+        ]
+        for copy in small:
+            copy.wait_recv()
+        total = parbuf[...]
+        for k in range(nd - 1):
+            total = total + pard[k]
+        par_out[me] = total
+        last = [
+            go(remote(par_out.at[me], par_out.at[me], pg_s.at[j], pg_r.at[j], self.target(step)[0]))
+            for j, step in enumerate(steps)
+        ]
+        for j, step in enumerate(steps):
+            device, _ = self.target(step)
+            here = par_out.at[self.source(step)]
+            remote(here, here, pg_s.at[j], pg_r.at[j], device).wait_recv()
+            got = dw_out.at[self.source(step)]
+            remote(got, got, wz_s.at[j], wz_r.at[j], device).wait_recv()
+        for copy in started:
+            copy.wait_send()
+
+    def reduce(self, unit, yp, dxp, dwp, dwop, dwcp, parp, x, g, dxc, st, gain):
+        nd, nz, nm, rows = self.nd, self.nz, self.nm, self.rows_in
+        wide = 2 * nd * TILE
+        block = (SPAN, MODEL)
+        return pl.pallas_call(
+            self.reduce_kernel,
+            out_shape=[
+                jax.ShapeDtypeStruct(block, BF16),
+                jax.ShapeDtypeStruct(block, BF16),
+                jax.ShapeDtypeStruct((nm, rows, wide), BF16),
+                jax.ShapeDtypeStruct((TILE, MODEL), F32),
+                jax.ShapeDtypeStruct((rows, COMMON), F32),
+                jax.ShapeDtypeStruct((nm, *parp.shape), F32),
+            ],
+            in_specs=[SM] + [VM] * 11,
+            out_specs=[VM] * 6,
+            scratch_shapes=[
+                pltpu.VMEM((nz, *block), BF16),
+                pltpu.VMEM((nz, *block), BF16),
+                pltpu.VMEM((nz, *block), BF16),
+                pltpu.VMEM((nz, *block), BF16),
+                pltpu.VMEM((nz - 1, *block), BF16),
+                pltpu.VMEM((nz - 1, *block), BF16),
+                pltpu.VMEM((nd - 1, nm * rows, wide), BF16),
+                pltpu.VMEM((nd - 1, TILE, MODEL), BF16),
+                pltpu.VMEM((nd - 1, rows, COMMON), BF16),
+                pltpu.VMEM((nm * rows, wide), BF16),
+                pltpu.VMEM((nd - 1, *parp.shape), F32),
+                pltpu.VMEM(parp.shape, F32),
+                DMA, DMA, DMA, DMA,
+                DMA((nz,)), DMA((nz,)), DMA((nz,)), DMA((nz,)),
+                DMA((nd,)), DMA((nd,)), DMA((nd,)), DMA((nd,)), DMA((nd,)), DMA((nd,)),
+                DMA((nm,)), DMA((nm,)), DMA((nd,)), DMA((nd,)), DMA((nm,)), DMA((nm,)),
+            ],
+            compiler_params=pltpu.CompilerParams(
+                collective_id=3, has_side_effects=True, vmem_limit_bytes=60 * 2**20
+            ),
+            name="reduce",
+        )(unit, yp, dxp, dwp, dwop, dwcp, parp, x, g, dxc, st, gain)
+
+    def local(
+        self, layer_input, out_grad, norm_gain, in_weight, conv_weight, conv_bias, step_bias, log_rate,
+        skip_gain, gate_gain, out_weight, nest_level, doc_lengths,
+    ):
+        nd, nc, nz, nm, rows = self.nd, self.nc, self.nz, self.nm, self.rows_in
+        span, wide = self.span, nd * TILE
+        dp, c, z = self.place()
+        me = c * nz + z
+        docs = doc_lengths.shape[1]
+        order = jnp.arange(docs)
+        ahead = order[:, None] < order[None, :]
+        starts = jnp.sum(jnp.where(ahead, doc_lengths[0][:, None], 0), axis=0, keepdims=True)
+        starts = starts.astype(jnp.int32)
+        active = jnp.right_shift(HEADS, 3 - nest_level[0])
+        unit = (1.0 / (active * HEAD_DIM).astype(F32)).reshape(1, 1)
+        x = layer_input.reshape(SPAN, MODEL)
+        g = out_grad.reshape(SPAN, MODEL)
+        wm = in_weight[:, : 2 * INNER].reshape(rows, 2 * nd, nm, TILE)
+        wm = jnp.transpose(wm, (2, 0, 1, 3)).reshape(nm, rows, 2 * wide)
+        wc = jnp.pad(in_weight[:, 2 * INNER :], ((0, 0), (0, COMMON - (EXTENT - 2 * INNER))))
+        own_conv = conv_bias.shape[0]
+        conv_pack = jnp.concatenate([conv_bias, conv_weight.reshape(-1)])
+        par = jnp.concatenate(
+            [
+                jnp.pad(norm_gain, (0, TILE - rows)),
+                gate_gain,
+                jnp.pad(conv_pack, (0, 6 * TILE - conv_pack.shape[0])),
+            ]
+        ).reshape(8, TILE)
+        xall, gall, wall, wcall, woall, parall = self.gather(x, par, g, wm, wc, out_weight)
+        by_owner = jnp.swapaxes(parall, 0, 1)
+        gain = by_owner[:, :, 0, :rows].reshape(1, MODEL)
+        gate_mine = lax.dynamic_index_in_dim(parall, me, 0, keepdims=False)[:, 1, :].reshape(wide)
+        conv_all = by_owner[:, :, 2:, :].reshape(nd * nm, 6 * TILE)
+        bias_all = conv_all[:, :own_conv].reshape(CONV)
+        taps_all = conv_all[:, own_conv : own_conv * (1 + KW)].reshape(CONV, KW)
+
+        def my_channels(values):
+            main = values[:INNER].reshape(nd, nm, TILE, *values.shape[1:])
+            main = lax.dynamic_index_in_dim(main, me, 1, keepdims=False)
+            return jnp.concatenate([main.reshape(wide, *values.shape[1:]), values[INNER:]], axis=0)
+
+        bias = my_channels(bias_all).reshape(1, -1)
+        taps = jnp.pad(my_channels(taps_all).T, ((0, 8 - KW), (0, 0)))
+        per = HEADS // (nd * nm)
+
+        def my_heads(values):
+            return lax.dynamic_index_in_dim(values.reshape(nd, nm, per), me, 1, keepdims=False).reshape(-1)
+
+        numbers = my_heads(jnp.arange(HEADS))
+        mine = nd * per
+        sel = (jnp.arange(TILE)[:, None] == jnp.pad(numbers, (0, TILE - mine), constant_values=-1)[None, :])
+        sel = sel.astype(BF16)
+        lane_pad = lambda v: jnp.pad(v, (0, TILE - mine))
+        hp = jnp.stack([lane_pad(my_heads(step_bias)), lane_pad(my_heads(-jnp.exp(log_rate)))])
+        hp = jnp.pad(hp, ((0, 6), (0, 0)))
+        mask = (numbers < active).astype(F32)
+        chp = jnp.stack(
+            [jnp.repeat(my_heads(skip_gain), HEAD_DIM), jnp.repeat(mask, HEAD_DIM), gate_mine]
+        )
+        chp = jnp.pad(chp, ((0, 5), (0, 0)))
+        xflat = xall.reshape(span, MODEL)
+        gflat = gall.reshape(span, MODEL)
+        wflat = wall.reshape(MODEL, 2 * wide)
+        wcflat = wcall.reshape(MODEL, COMMON)
+        woflat = woall.reshape(wide, MODEL)
+        projm = jnp.dot(xflat, wflat, preferred_element_type=F32).astype(BF16)
+        projc = jnp.dot(xflat, wcflat, preferred_element_type=F32).astype(BF16)
+        pre_sig, pre_bc, o, sin, step, cum, dg, y, st = self.forward(
+            docs, starts, projm, projc, gflat, woflat, taps, bias, sel, hp, chp
+        )
+        st = self.stats(st)
+        dproj, dcom, normed_out, sums, heads = self.backward(
+            docs, starts, unit, projm, pre_sig, pre_bc, o, sin, step, cum, dg, st, taps, sel, hp, chp
+        )
+        dcall, bc_sums = self.common(docs, starts, dcom, pre_bc, projc, taps)
+        dxp = lax.dot_general(dproj, wflat, (((1,), (1,)), ((), ())), preferred_element_type=F32)
+        dxp = dxp.astype(BF16).reshape(nm, SPAN, MODEL)
+        dwp = lax.dot_general(xflat, dproj, (((0,), (0,)), ((), ())), preferred_element_type=F32)
+        dwp = dwp.astype(BF16).reshape(nd, nm * rows, 2 * wide)
+        dwop = lax.dot_general(normed_out, gflat, (((0,), (0,)), ((), ())), preferred_element_type=F32)
+        dwop = dwop.astype(BF16).reshape(nd, TILE, MODEL)
+        dc_mine = lax.dynamic_index_in_dim(dcall, me, 0, keepdims=False)
+        dxc = lax.dot_general(dc_mine, wcflat, (((1,), (1,)), ((), ())), preferred_element_type=F32)
+        x_rows = lax.dynamic_index_in_dim(xflat.reshape(span, nd, nm, rows), me, 2, keepdims=False)
+        dwcp = lax.dot_general(
+            x_rows.reshape(span, nd * rows), dcall.reshape(span, COMMON), (((0,), (0,)), ((), ())),
+            preferred_element_type=F32,
+        )
+        dwcp = dwcp.astype(BF16).reshape(nd, rows, COMMON)
+        parp = jnp.concatenate(
+            [
+                jnp.zeros((MODEL // TILE, TILE), F32),
+                sums.reshape(8 * nd, TILE),
+                bc_sums,
+                heads,
+            ]
+        )
+        y_out, dx_out, dw, dwo, dwc, pars = self.reduce(
+            unit, y.reshape(nm, SPAN, MODEL), dxp, dwp, dwop, dwcp, parp, x, g, dxc, st, gain
+        )
+        dw = jnp.transpose(dw.reshape(nm, rows, 2 * nd, TILE), (1, 2, 0, 3)).reshape(rows, 2 * INNER)
+        in_weight_grad = jnp.concatenate([dw.astype(F32), dwc[:, : EXTENT - 2 * INNER]], axis=1)
+        owner = dp * nm + me
+        gains = jnp.sum(pars[:, : MODEL // TILE], axis=0).reshape(MODEL)
+        norm_gain_grad = lax.dynamic_slice_in_dim(gains, owner * rows, rows)
+        base = MODEL // TILE
+        mains = pars[:, base : base + 8 * nd].reshape(nm, 8, nd, TILE)
+        shared = jnp.sum(pars[:, base + 8 * nd : base + 8 * nd + 16], axis=0)
+        head_sums = pars[:, base + 8 * nd + 16 :]
+        gate_gain_grad = lax.dynamic_index_in_dim(mains[me, 0], dp, 0, keepdims=False)
+        everything = jnp.transpose(mains[:, 1:], (1, 2, 0, 3)).reshape(7, INNER)
+        skip_gain_grad = jnp.sum(everything[0].reshape(HEADS, HEAD_DIM), axis=1)
+        bias_sum = jnp.concatenate([everything[1], shared[:2].reshape(-1)])
+        taps_sum = jnp.concatenate([everything[3:], shared[2:10].reshape(KW, 2 * TILE)], axis=1).T
+        conv_bias_grad = lax.dynamic_slice_in_dim(bias_sum, owner * own_conv, own_conv)
+        conv_weight_grad = lax.dynamic_slice_in_dim(taps_sum, owner * own_conv, own_conv)
+        by_head = lambda v: jnp.swapaxes(v[:, :mine].reshape(nm, nd, per), 0, 1).reshape(HEADS)
+        step_bias_grad, log_rate_grad = by_head(head_sums[:, 0]), by_head(head_sums[:, 1])
+        return (
+            y_out.reshape(1, SPAN, MODEL),
+            dx_out.reshape(1, SPAN, MODEL),
+            norm_gain_grad,
+            in_weight_grad,
+            conv_weight_grad,
+            conv_bias_grad,
+            step_bias_grad,
+            log_rate_grad,
+            skip_gain_grad,
+            gate_gain_grad,
+            dwo,
+        )
+
+
 def solution(mesh):
+    shape = dict(mesh.shape)
+    head_split = HeadSplit(shape["dp"], shape["seq"], shape["fsdp"])
     return jax.shard_map(
-        local,
+        head_split.local if head_split.fits() else token_split,
         mesh=mesh,
         in_specs=(
             P("dp", ("seq", "fsdp"), None),

time: 1080 us -> 457 us (0.42)
  waiting for transfers between devices: 437 us -> 0 us
  Pallas kernels: 0 us -> 371 us
  blocking collectives: 334 us -> 0 us
  other arithmetic: 117 us -> 10.9 us
  matrix products: 139 us -> 35.3 us
  between operations: 15.9 us -> 1.79 us
  local copies, waits for them, and re-layouts: 24.9 us -> 37.5 us
    pallas_call x0 -> x6, Pallas kernels: none -> 371 us  [the longest x1 140 us: reduce(): pl.pallas_call(self.reduce_kernel, out_shape=[jax.ShapeDtypeStruct(block,...]
    all_gather x6 -> x0, waiting for transfers between devices: 310 us -> none  [the longest x1 93.7 us: local(): lax.all_gather(in_weight, ('dp', 'seq', 'fsdp'), axis=0, tiled=True)]
    all_gather x3 -> x0, blocking collectives: 154 us -> none  [the longest x1 73.2 us: local(): lax.all_gather(conv_weight, ('dp', 'seq', 'fsdp'), axis=0, tiled=True)]
    dot_general x18 -> x7, matrix products: 139 us -> 35.3 us  [the longest x1 9.41 us: local(): projm = jnp.dot(xflat, wflat, preferred_element_type=F32).astype(BF16)]
    all_to_all x2 -> x0, blocking collectives: 101 us -> none  [the longest x1 59.6 us: local(): lax.all_to_all(normed_out.reshape(token_count, replicas, members, width_o...]
    unnamed x2 -> x0, blocking collectives: 79.2 us -> none
    reduce_scatter x2 -> x0, waiting for transfers between devices: 68.1 us -> none  [the longest x1 58.6 us: local(): lax.psum_scatter(in_new.astype(jnp.bfloat16), 'dp', scatter_dimension=0,...]
    unnamed x10 -> x0, waiting for transfers between devices: 55.1 us -> none
  transfers between devices with their start and end apart: 11 -> 0, of which waited for: 9 -> 0; matrix products, arithmetic and copies ran while one was open for 20% -> 0% of each run, Pallas kernels for 0% -> 0%
where the time goes in v1:
time: 457 us; the launch traced here: 456 us
  Pallas kernels  371 us (81%)
  local copies, waits for them, and re-layouts  37.5 us (8%)
  matrix products  35.3 us (8%)
  other arithmetic  10.9 us (2%)
    pallas_call x1, Pallas kernels, reduce(): pl.pallas_call(self.reduce_kernel, out_shape=[jax.ShapeDtypeStruct(block,...  140 us
    pallas_call x1, Pallas kernels, gather(): pl.pallas_call(self.gather_kernel, out_shape=out, in_specs=[VM, VM, ANY,...  128 us
    pallas_call x1, Pallas kernels, common(): pl.pallas_call(functools.partial(self.common_kernel, docs), out_shape=[ja...  40.1 us
    pallas_call x1, Pallas kernels, backward(): pl.pallas_call(functools.partial(self.backward_kernel, docs), grid=(nm,),...  25.6 us
    pallas_call x1, Pallas kernels, stats(): pl.pallas_call(self.stats_kernel, out_shape=jax.ShapeDtypeStruct(st.shape...  20 us
    pallas_call x1, Pallas kernels, forward(): pl.pallas_call(functools.partial(self.forward_kernel, docs), grid=(nm,),...  17 us
    dot_general x1, matrix products, local(): projm = jnp.dot(xflat, wflat, preferred_element_type=F32).astype(BF16)  9.41 us

profile of v1, /device:TPU:0, one launch (start us, length us, event | category | flops | bytes accessed | tf_op | source)
XLA Modules:
  0.0 456.1 jit_solution(13915128557419973508)
XLA Ops:
  1.3 1.2 select_reduce_fusion
  2.6 0.8 copy.45
  3.4 0.1 reshape.199
  3.5 0.8 select_maximum_fusion.3
  4.2 1.3 fusion.6.par_ref
  5.5 1.3 slice_bitcast_fusion
  6.8 0.3 copy.62
  7.1 0.1 copy.72
  7.2 1.3 reshape.203.wm_ref
  8.5 0.6 pad.37.wc_ref
  9.1 128.4 %gather.1 = (bf16[8,128,2048]{2,1,0:T(8,128)(2,1)}, bf16[8,128,2048]{2,1,0:T(8,128)(2,1)}, bf16[4,8,64,1024]{3,2,1,0:T(8,128)(2,1)}, bf16[4,8,64,384]{3,2,1,0:T(...) custom-call(bf16[128,2048]{1,0:T(8,128)(2,1)} %bitcast.136, f32[8,128]{1,0:T(8,128)} %fusion.6.par_ref, ...), custom_call_target="tpu_custom_call" | custom-call | tf_op jit(solution)/shard_map/gather/pallas_call | solution.py:571
  137.6 9.4 %convolution_convert_fusion.3.pm.pm_prev = bf16[1024,1024]{1,0:T(8,128)(2,1)} fusion(bf16[1024,2048]{1,0:T(8,128)(2,1)} %bitcast.128, bf16[2048,1024]{1,0:T(8,128)(2,1)} %bitcast.168), kind=kOutput, calls=%fused_computation.6 | convolution fusion | flops 4296015872 | bytes 10485760 | tf_op jit(solution)/shard_map/dot_general | solution.py:1280
  147.0 3.2 convolution_convert_fusion.4.pc.pc_prev.projc
  150.4 0.7 reshape.210
  151.2 1.5 slice.111
  152.7 1.0 constant_dynamic-slice_fusion.6
  153.6 0.1 copy.61
  153.7 0.6 pad.38.taps
  154.4 0.1 reshape.213
  154.5 0.6 reshape.216.bias
  155.1 0.1 reshape.223
  155.2 0.6 fusion.3.sel
  155.9 0.1 reshape.224
  156.0 0.1 reshape.226
  156.1 0.1 reshape.227
  156.3 0.6 select_maximum_fusion.2.hp
  157.1 0.1 reshape.228
  157.2 0.1 reshape.229
  157.4 0.6 select_maximum_fusion.chp
  158.1 17.0 %forward.1 = (f32[1024,512]{1,0:T(8,128)}, f32[1024,256]{1,0:T(8,128)}, f32[1024,512]{1,0:T(8,128)}, f32[8,128,512]{2,1,0:T(8,128)}, f32[1024,128]{1,0:T(8,128)}...) custom-call(s32[1,4]{1,0:T(1,128)} %bitcast.165, ...), custom_call_target="tpu_custom_call" | custom-call | tf_op jit(solution)/shard_map/forward/pallas_call | solution.py:683
  175.1 20.0 %stats.1.st = f32[8,8,128]{2,1,0:T(8,128)} custom-call(f32[8,8,128]{2,1,0:T(8,128)} %get-tuple-element.53.st), custom_call_target="tpu_custom_call" | custom-call | tf_op jit(solution)/shard_map/stats/pallas_call | solution.py:746
  195.1 25.6 %backward.1 = (bf16[1024,1024]{1,0:T(8,128)(2,1)}, bf16[1024,384]{1,0:T(8,128)(2,1)}, bf16[1024,512]{1,0:T(8,128)(2,1)}, f32[8,512]{1,0:T(8,128)}, f32[8,128]{1,0:T(8,128)}) custom-call(s32[1,4]{1,0:T(1,128)} %bitcast.166, f32[1,1]{1,0:T(1,128)} %bitcast.1.unit, bf16[1024,1024]{1,0:T(8,128)(2,1)} %convolution_convert_fusion.3.pm.pm_prev, ...), custom_call_target="tpu_custom_call" | custom-call | tf_op jit(solution)/shard_map/backward/pallas_call | solution.py:924
  220.7 7.9 %convolution_convert_fusion.1 = bf16[1024,2048]{1,0:T(8,128)(2,1)} fusion(bf16[1024,1024]{1,0:T(8,128)(2,1)} %get-tuple-element.54, bf16[2048,1024]{1,0:T(8,128)(2,1)S(1)} %bitcast.169), kind=kOutput, calls=%fused_computation.1 | convolution fusion | flops 4297064448 | bytes 10485760 | tf_op jit(solution)/shard_map/dot_general | solution.py:1290
  228.7 6.2 %convolution_convert_fusion = bf16[2048,1024]{1,0:T(8,128)(2,1)} fusion(bf16[1024,2048]{1,0:T(8,128)(2,1)S(1)} %bitcast.130, bf16[1024,1024]{1,0:T(8,128)(2,1)S(1)} %copy-done.15), kind=kOutput, calls=%fused_computation | convolution fusion | flops 4297064448 | bytes 10485760 | tf_op jit(solution)/shard_map/dot_general | solution.py:1292
  234.9 3.8 convolution_convert_fusion.2
  238.7 6.7 %copy.50 = bf16[8,128,2048]{1,0,2:T(8,128)(2,1)} copy(bf16[8,128,2048]{2,1,0:T(8,128)(2,1)} %get-tuple-element.39) | data formatting | bytes 8388608 | tf_op jit(solution)/shard_map/gather/pallas_call | solution.py:571
  245.3 7.4 %reshape_reshape.3 = bf16[1024,4,8,64]{0,3,2,1:T(8,128)(2,1)} reshape(bf16[8,128,2048]{1,0,2:T(8,128)(2,1)} %copy.50) | data formatting | bytes 8388608 | tf_op jit(solution)/shard_map/reshape;reshape | solution.py:1298
  252.7 1.1 constant_dynamic-slice_fusion
  253.8 40.1 %common.1 = (bf16[8,128,384]{2,1,0:T(8,128)(2,1)}, f32[16,128]{1,0:T(8,128)}) custom-call(s32[1,4]{1,0:T(1,128)} %bitcast.167, bf16[1024,384]{1,0:T(8,128)(2,1)} %get-tuple-element.56.dcom, f32[1024,256]{1,0:T(8,128)} %get-tuple-element.47.pre_bc, bf16[1024,384]{1,0:T(8,128)(2,1)} %convolution_convert_fusion.4.pc.pc_prev.projc, f32[8,768]{1,0:T(8,128)} %pad.38.taps), custom_call_target="tpu_custom_call" | custom-call | tf_op jit(solution)/shard_map/common/pallas_call | solution.py:1031
  293.9 2.2 convolution_convert_fusion.5
  296.1 1.4 pad_maximum_fusion.1.parp
  297.5 2.5 fusion.dxc
  300.0 0.7 reshape_squeeze.6.gain
  300.7 139.6 %reduce.13 = (bf16[128,2048]{1,0:T(8,128)(2,1)}, bf16[128,2048]{1,0:T(8,128)(2,1)}, bf16[8,64,1024]{2,1,0:T(8,128)(2,1)}, f32[128,2048]{1,0:T(8,128)}, f32[64,384]{1,0:T(8,128)}, /*index=5*/f32[8,72,128]{2,1,0:T(8,128)}) custom-call(f32[1,1]{1,0:T(1,128)} %bitcast.1.unit, bf16[8,128,2048]{2,1,0:T(8,128)(2,1)} %bitcast.125, bf16[8,128,2048]{2,1,0:T(8,128)(2,1)} %bitcast.126, ...), custom_call_target="tpu_custom_call" | custom-call | tf_op jit(solution)/shard_map/reduce/pallas_call | solution.py:1178
  440.3 0.9 slice_reduce_fusion
  441.2 0.6 dynamic_slice.57
  441.8 1.5 copy.63
  443.3 0.1 bitcast_bitcast_fusion
  443.5 1.2 copy.52
  444.7 1.2 copy.71
  445.9 1.5 pad_maximum_fusion
  447.4 1.0 slice.96
  448.6 0.7 fusion.7
  449.3 0.6 fusion.13
  449.9 0.8 fusion.15
  450.8 0.1 copy.55
  450.9 0.6 reshape.245
  451.6 0.1 copy.57
  451.7 0.6 reshape.247
  452.4 0.6 reduce_sum.39
  453.0 0.5 fusion.14
  453.5 0.8 copy.80
  454.3 0.8 copy.81
  455.1 1.0 copy.82
  (80 shorter events, 1.2 us)
Async XLA Ops:
  7.1 1.4 slice-start
  137.5 9.4 %copy-start.1 = (bf16[8,128,2048]{2,1,0:T(8,128)(2,1)S(1)}, bf16[8,128,2048]{2,1,0:T(8,128)(2,1)}, u32[]{:S(2)}) copy-start(bf16[8,128,2048]{2,1,0:T(8,128)(2,1)} %get-tuple-element.39) | copy-start | bytes 12582916
  137.6 9.4 %copy-start.3 = (bf16[4,8,64,384]{3,2,1,0:T(8,128)(2,1)S(1)}, bf16[4,8,64,384]{3,2,1,0:T(8,128)(2,1)}, u32[]{:S(2)}) copy-start(bf16[4,8,64,384]{3,2,1,0:T(8,128)(2,1)} %get-tuple-element.41) | copy-start | bytes 4718596
  147.0 3.2 copy-start.8
  151.2 4.7 %copy-start.12 = (f32[64]{0:T(128)S(1)}, f32[64]{0:T(128)}, u32[]{:S(2)}) copy-start(f32[64]{0:T(128)} %param.19) | copy-start | bytes 772
  151.2 4.8 %copy-start.17 = (f32[64]{0:T(128)S(1)}, f32[64]{0:T(128)}, u32[]{:S(2)}) copy-start(f32[64]{0:T(128)} %param.20) | copy-start | bytes 772
  151.2 5.9 %copy-start.13 = (f32[64]{0:T(128)S(1)}, f32[64]{0:T(128)}, u32[]{:S(2)}) copy-start(f32[64]{0:T(128)} %param.21) | copy-start | bytes 772
  195.1 25.6 %copy-start.14 = (bf16[4,8,64,1024]{3,2,1,0:T(8,128)(2,1)S(1)}, bf16[4,8,64,1024]{3,2,1,0:T(8,128)(2,1)}, u32[]{:S(2)}) copy-start(bf16[4,8,64,1024]{3,2,1,0:T(8,128)(2,1)} %get-tuple-element.40) | copy-start | bytes 12582916
  220.7 7.9 %copy-start.2 = (bf16[8,128,2048]{2,1,0:T(8,128)(2,1)S(1)}, bf16[8,128,2048]{2,1,0:T(8,128)(2,1)}, u32[]{:S(2)}) copy-start(bf16[8,128,2048]{2,1,0:T(8,128)(2,1)} %get-tuple-element.39) | copy-start | bytes 12582916
  220.7 7.9 %copy-start.15 = (bf16[1024,1024]{1,0:T(8,128)(2,1)S(1)}, bf16[1024,1024]{1,0:T(8,128)(2,1)}, u32[]{:S(2)}) copy-start(bf16[1024,1024]{1,0:T(8,128)(2,1)} %get-tuple-element.54) | copy-start | bytes 6291460
  228.6 6.3 %copy-start = (bf16[8,128,2048]{2,1,0:T(8,128)(2,1)S(1)}, bf16[8,128,2048]{2,1,0:T(8,128)(2,1)}, u32[]{:S(2)}) copy-start(bf16[8,128,2048]{2,1,0:T(8,128)(2,1)} %get-tuple-element.42) | copy-start | bytes 12582916
  228.6 6.3 %copy-start.16 = (bf16[1024,512]{1,0:T(8,128)(2,1)S(1)}, bf16[1024,512]{1,0:T(8,128)(2,1)}, u32[]{:S(2)}) copy-start(bf16[1024,512]{1,0:T(8,128)(2,1)} %get-tuple-element.55) | copy-start | bytes 3145732
  253.8 42.3 %copy-start.10 = (f32[8,512]{1,0:T(8,128)S(1)}, f32[8,512]{1,0:T(8,128)}, u32[]{:S(2)}) copy-start(f32[8,512]{1,0:T(8,128)} %get-tuple-element.58) | copy-start | bytes 49156
  253.8 42.4 %copy-start.11 = (f32[8,128]{1,0:T(8,128)S(1)}, f32[8,128]{1,0:T(8,128)}, u32[]{:S(2)}) copy-start(f32[8,128]{1,0:T(8,128)} %get-tuple-element.60) | copy-start | bytes 12292
  253.8 43.7 %copy-start.4 = (bf16[4,8,64,384]{3,2,1,0:T(8,128)(2,1)S(1)}, bf16[4,8,64,384]{3,2,1,0:T(8,128)(2,1)}, u32[]{:S(2)}) copy-start(bf16[4,8,64,384]{3,2,1,0:T(8,128)(2,1)} %get-tuple-element.41) | copy-start | bytes 4718596
  444.7 1.2 copy-start.9
  445.9 7.6 %copy-start.7 = (bf16[128,2048]{1,0:T(8,128)(2,1)S(1)}, bf16[128,2048]{1,0:T(8,128)(2,1)}, u32[]{:S(2)}) copy-start(bf16[128,2048]{1,0:T(8,128)(2,1)} %get-tuple-element.61) | copy-start | bytes 1572868
  447.4 6.9 %copy-start.6 = (bf16[128,2048]{1,0:T(8,128)(2,1)S(1)}, bf16[128,2048]{1,0:T(8,128)(2,1)}, u32[]{:S(2)}) copy-start(bf16[128,2048]{1,0:T(8,128)(2,1)} %get-tuple-element.62) | copy-start | bytes 1572868
  447.4 7.7 %copy-start.5 = (f32[128,2048]{1,0:T(8,128)S(1)}, f32[128,2048]{1,0:T(8,128)}, u32[]{:S(2)}) copy-start(f32[128,2048]{1,0:T(8,128)} %get-tuple-element.96) | copy-start | bytes 3145732

commit v2 on v0

--- a/solution.py
+++ b/solution.py
@@ -1,6 +1,10 @@
+import functools
+
 import jax
 import jax.numpy as jnp
 from jax import lax
+from jax.experimental import pallas as pl
+from jax.experimental.pallas import tpu as pltpu
 from jax.sharding import PartitionSpec as P
 
 HEADS = 64
@@ -70,7 +74,9 @@
 
 
 def doc_begins(lengths, positions):
-    endings = jnp.cumsum(lengths, axis=1) - lengths
+    places = jnp.arange(lengths.shape[1])
+    ahead = places[:, None] < places[None, :]
+    endings = jnp.sum(jnp.where(ahead[None], lengths[:, :, None], 0), axis=1)
     reached = endings[:, None, :] <= positions[None, :, None]
     return jnp.max(jnp.where(reached, endings[:, None, :], 0), axis=2)
 
@@ -93,7 +99,9 @@
 def scan_parts(signal, key_side, query_side, rate_in, step_bias, log_rate, begins, block_start):
     step = jax.nn.softplus(rate_in + step_bias)
     log_decay = step * -jnp.exp(log_rate)
-    cumulative = jnp.cumsum(log_decay, axis=1)
+    places = jnp.arange(log_decay.shape[1])
+    lower = (places[None, :] <= places[:, None]).astype(jnp.float32)
+    cumulative = jnp.einsum("ts,bsh->bth", lower, log_decay, precision=HIGH)
     by_head = jnp.swapaxes(cumulative, 1, 2)
     indices = jnp.arange(signal.shape[1])
     same_doc = (begins[:, :, None] == begins[:, None, :]) & (
@@ -127,7 +135,7 @@
     return (earlier[0] * later[0], later[1] + later[0][:, :, None, None] * earlier[1])
 
 
-def local(
+def token_split(
     layer_input,
     out_grad,
     norm_gain,
@@ -333,9 +341,1319 @@
     )
 
 
+MESH = pl.DeviceIdType.MESH
+F32 = jnp.float32
+BF16 = jnp.bfloat16
+TILE = 128
+SPAN = 128
+MODEL = 2048
+COMMON = 384
+PAD = 16
+NEG = -1e30
+VM = pl.BlockSpec(memory_space=pltpu.VMEM)
+SM = pl.BlockSpec(memory_space=pltpu.SMEM)
+ANY = pl.BlockSpec(memory_space=pl.ANY)
+DMA = pltpu.SemaphoreType.DMA
+
+
+def remote(src, dst, sends, recvs, device):
+    return pltpu.make_async_remote_copy(
+        src_ref=src,
+        dst_ref=dst,
+        send_sem=sends,
+        recv_sem=recvs,
+        device_id=device,
+        device_id_type=MESH,
+    )
+
+
+def dot(a, b, over=((1,), (0,))):
+    return lax.dot_general(a, b, (over, ((), ())), preferred_element_type=F32)
+
+
+def exact(a, b, over=((1,), (0,))):
+    return lax.dot_general(a, b, (over, ((), ())), precision=HIGH, preferred_element_type=F32)
+
+
+def begin_at(place, starts, docs):
+    begin = jnp.zeros_like(place)
+    for doc in range(1, docs):
+        begin = jnp.where(starts[0, doc] <= place, starts[0, doc], begin)
+    return begin
+
+
+def iota(shape, dim):
+    return lax.broadcasted_iota(jnp.int32, shape, dim)
+
+
+def silu_slope(value):
+    gate = jax.nn.sigmoid(value)
+    return gate * (1.0 + value * (1.0 - gate))
+
+
+def softplus(value):
+    return jnp.maximum(value, 0.0) + jnp.log1p(jnp.exp(-jnp.abs(value)))
+
+
+def conv_tile(extended, taps, lanes, valid):
+    total = jnp.broadcast_to(taps[KW : KW + 1, lanes], (SPAN, TILE))
+    for tap in range(KW):
+        back = KW - 1 - tap
+        moved = extended if back == 0 else pltpu.roll(extended, back, 0)
+        total = total + jnp.where(valid[tap], moved[PAD:], 0.0) * taps[tap : tap + 1, lanes]
+    return total
+
+
+def tile_of(index):
+    return slice(index * TILE, (index + 1) * TILE)
+
+
+def rows_of(index, size=SPAN):
+    return pl.ds(pl.multiple_of(index * size, size), size)
+
+
+def head_col(values, head):
+    return jnp.broadcast_to(values[:, head : head + 1], (SPAN, TILE))
+
+
+def lane_sum(values):
+    return jnp.broadcast_to(jnp.sum(values, axis=1, keepdims=True), values.shape)
+
+
+class Line:
+    def __init__(self, place, sizes, block, sems):
+        self.dp, self.c, self.z = place
+        self.nc, self.nz = sizes
+        self.block = block
+        self.right_s, self.right_r, self.left_s, self.left_r, self.core_s, self.core_r = sems
+
+    def right(self, s):
+        block = self.block(self.c, self.z - s)
+        to = (self.dp, self.c, lax.rem(self.z + 1, self.nz))
+        return remote(block, block, self.right_s.at[s], self.right_r.at[s], to)
+
+    def left(self, s):
+        block = self.block(self.c, self.z + s)
+        to = (self.dp, self.c, lax.rem(self.z + self.nz - 1, self.nz))
+        return remote(block, block, self.left_s.at[s], self.left_r.at[s], to)
+
+    def core(self, z):
+        block = self.block(self.c, z)
+        to = (self.dp, self.nc - 1 - self.c, self.z)
+        return remote(block, block, self.core_s.at[z], self.core_r.at[z], to)
+
+    def across(self):
+        return (self.dp, self.nc - 1 - self.c, self.z)
+
+    def begin(self):
+        pl.when(self.z < self.nz - 1)(lambda: self.right(0).start())
+        pl.when(self.z > 0)(lambda: self.left(0).start())
+        self.core(self.z).start()
+
+    def step(self, s):
+        z, nz = self.z, self.nz
+
+        @pl.when(z >= s)
+        def _():
+            block = self.block(self.c, z - s)
+            remote(block, block, self.right_s.at[s - 1], self.right_r.at[s - 1], self.across()).wait_recv()
+            if s < nz - 1:
+                pl.when(z < nz - 1)(lambda: self.right(s).start())
+            self.core(z - s).start()
+
+        @pl.when(z + s < nz)
+        def _():
+            block = self.block(self.c, z + s)
+            remote(block, block, self.left_s.at[s - 1], self.left_r.at[s - 1], self.across()).wait_recv()
+            if s < nz - 1:
+                pl.when(z > 0)(lambda: self.left(s).start())
+            self.core(z + s).start()
+
+    def arrive(self):
+        for z in range(self.nz):
+            block = self.block(self.nc - 1 - self.c, z)
+            to = (self.dp, self.nc - 1 - self.c, self.z)
+            remote(block, block, self.core_s.at[z], self.core_r.at[z], to).wait_recv()
+
+    def end(self):
+        z, nz = self.z, self.nz
+        for s in range(nz - 1):
+            pl.when((z >= s) & (z < nz - 1))(lambda s=s: self.right(s).wait_send())
+            pl.when((z + s < nz) & (z > 0))(lambda s=s: self.left(s).wait_send())
+        for s in range(nz):
+            self.core(jnp.int32(s)).wait_send()
+
+
+class Sum:
+    def __init__(self, place, sizes, part, came, total, heard, sems):
+        self.dp, self.c, self.z = place
+        self.nc, self.nz = sizes
+        self.part, self.came, self.total, self.heard = part, came, total, heard
+        self.core_s, self.core_r, self.right_s, self.right_r, self.left_s, self.left_r = sems
+
+    def core(self, t):
+        to = (self.dp, self.nc - 1 - self.c, self.z)
+        src = self.part.at[(self.nc - 1 - self.c) * self.nz + t]
+        return remote(src, self.came.at[t], self.core_s.at[t], self.core_r.at[t], to)
+
+    def right(self, t):
+        to = (self.dp, self.c, lax.rem(self.z + 1, self.nz))
+        return remote(self.total.at[t], self.heard.at[t], self.right_s.at[t], self.right_r.at[t], to)
+
+    def left(self, t):
+        to = (self.dp, self.c, lax.rem(self.z + self.nz - 1, self.nz))
+        return remote(self.total.at[t], self.heard.at[self.nz + t], self.left_s.at[t], self.left_r.at[t], to)
+
+    def add_core(self, t):
+        self.core(t).wait_recv()
+
+        def add(r, _):
+            at = rows_of(r, 16)
+            self.total[t, at, :] = (
+                self.part[self.c * self.nz + t, at, :].astype(F32) + self.came[t, at, :].astype(F32)
+            ).astype(BF16)
+            return 0
+
+        lax.fori_loop(0, SPAN // 16, add, 0)
+
+    def add(self, t, slot):
+        def add(r, _):
+            at = rows_of(r, 16)
+            self.total[t, at, :] = (
+                self.total[t, at, :].astype(F32) + self.heard[slot, at, :].astype(F32)
+            ).astype(BF16)
+            return 0
+
+        lax.fori_loop(0, SPAN // 16, add, 0)
+
+    def begin(self):
+        z, nz = self.z, self.nz
+        for k in range(nz - 1):
+            pl.when(z == 0)(lambda k=k: self.right(nz - 1 - k).start())
+            pl.when(z == nz - 1)(lambda k=k: self.left(k).start())
+
+    def relay(self, hops, k):
+        z, nz = self.z, self.nz
+        if nz - 1 - k <= hops:
+            return
+
+        @pl.when(z == hops)
+        def _():
+            t = nz - 1 - k
+            self.right(t).wait_recv()
+            self.add(t, t)
+            self.right(t).start()
+
+        @pl.when(z == nz - 1 - hops)
+        def _():
+            self.left(k).wait_recv()
+            self.add(k, nz + k)
+            self.left(k).start()
+
+    def arrive(self):
+        z, nz = self.z, self.nz
+        for t in range(nz):
+            pl.when((z == t) & (z > 0))(lambda t=t: self.right(t).wait_recv())
+            pl.when((z == t) & (z < nz - 1))(lambda t=t: self.left(t).wait_recv())
+
+    def own(self, rows):
+        z, nz = self.z, self.nz
+        value = self.total[z, rows, :].astype(F32)
+        left = self.heard[z, rows, :].astype(F32)
+        right = self.heard[nz + z, rows, :].astype(F32)
+        value = value + jnp.where(z > 0, left, 0.0)
+        return value + jnp.where(z < nz - 1, right, 0.0)
+
+    def end(self):
+        for t in range(self.nz):
+            self.core(t).wait_send()
+            pl.when(self.z < t)(lambda t=t: self.right(t).wait_send())
+            pl.when(self.z > t)(lambda t=t: self.left(t).wait_send())
+
+
+class Square:
+    def __init__(self, place, block, size, sems):
+        dp, c, z = place
+        self.dp, self.dx, self.dy = dp, dp + 1 - 2 * lax.rem(dp, 2), lax.rem(dp + 2, 4)
+        self.diag = lax.rem(self.dx + 2, 4)
+        self.x, self.y = (self.dx, c, z), (self.dy, c, z)
+        self.block = block
+        self.half = size // 2
+        self.sems = sems
+
+    def copy(self, way, owner, piece, first, rows, to):
+        block = self.block(owner, piece, first, rows)
+        sends, recvs = self.sems
+        return remote(block, block, sends.at[way, piece], recvs.at[way, piece], to)
+
+    def whole(self, way, owner, piece):
+        return self.copy(way, owner, piece, 0, 2 * self.half, self.x if way == 0 else self.y)
+
+    def part(self, way, owner, piece):
+        return self.copy(way, owner, piece, 0 if way == 2 else self.half, self.half, self.y if way == 2 else self.x)
+
+    def begin(self, piece):
+        self.whole(0, self.dp, piece).start()
+        self.whole(1, self.dp, piece).start()
+
+    def step(self, piece):
+        self.whole(0, self.dx, piece).wait_recv()
+        self.part(2, self.dx, piece).start()
+        self.whole(1, self.dy, piece).wait_recv()
+        self.part(3, self.dy, piece).start()
+
+    def arrive(self, piece):
+        self.part(2, self.diag, piece).wait_recv()
+        self.part(3, self.diag, piece).wait_recv()
+
+    def end(self, piece):
+        self.whole(0, self.dp, piece).wait_send()
+        self.whole(1, self.dp, piece).wait_send()
+        self.part(2, self.dx, piece).wait_send()
+        self.part(3, self.dy, piece).wait_send()
+
+
+class SquareSum:
+    def __init__(self, place, part, once, twice, gone, sems, pieces):
+        dp, c, z = place
+        self.dp, self.dx, self.dy = dp, dp + 1 - 2 * lax.rem(dp, 2), lax.rem(dp + 2, 4)
+        self.diag = lax.rem(self.dx + 2, 4)
+        self.x, self.y = (self.dx, c, z), (self.dy, c, z)
+        self.part, self.once, self.twice, self.gone = part, once, twice, gone
+        self.s1, self.r1, self.s2, self.r2 = sems
+        self.pieces = pieces
+        self.rows = part.shape[1] // pieces
+        self.half = part.shape[2] // 2
+        self.halves = (slice(0, self.half), slice(self.half, 2 * self.half))
+
+    def first(self, p, side, k):
+        owner = ((self.dx, self.diag), (self.dy, self.diag))[side][k]
+        at = pl.ds(p * self.rows, self.rows)
+        slot = 2 * side + k
+        return remote(
+            self.part.at[owner, at, self.halves[side]], self.once.at[slot, at, :],
+            self.s1.at[p, slot], self.r1.at[p, slot], (self.x, self.y)[side],
+        )
+
+    def second(self, p, side):
+        at = pl.ds(p * self.rows, self.rows)
+        return remote(
+            self.gone.at[side, at, :], self.twice.at[side, at, :], self.s2.at[p, side], self.r2.at[p, side],
+            (self.y, self.x)[side],
+        )
+
+    def begin_x(self, p):
+        self.first(p, 0, 1).start()
+        self.first(p, 0, 0).start()
+
+    def begin_y(self, p):
+        self.first(p, 1, 1).start()
+        self.first(p, 1, 0).start()
+
+    def each(self, p, body):
+        def step(r, _):
+            body(pl.ds(pl.multiple_of(p * self.rows + r * 16, 16), 16))
+            return 0
+
+        lax.fori_loop(0, self.rows // 16, step, 0)
+
+    def pass_on(self, p):
+        for side in range(2):
+            self.first(p, side, 1).wait_recv()
+            owner = (self.dy, self.dx)[side]
+
+            def body(at, side=side, owner=owner):
+                self.gone[side, at, :] = (
+                    self.part[owner, at, self.halves[side]].astype(F32)
+                    + self.once[2 * side + 1, at, :].astype(F32)
+                ).astype(BF16)
+
+            self.each(p, body)
+            self.second(p, side).start()
+
+    def finish(self, p, out):
+        for side in range(2):
+            self.first(p, side, 0).wait_recv()
+            self.second(p, side).wait_recv()
+
+            def body(at, side=side):
+                out[at, self.halves[side]] = (
+                    self.part[self.dp, at, self.halves[side]].astype(F32)
+                    + self.once[2 * side, at, :].astype(F32)
+                    + self.twice[side, at, :].astype(F32)
+                ).astype(out.dtype)
+
+            self.each(p, body)
+
+    def end(self):
+        for p in range(self.pieces):
+            for side in range(2):
+                self.first(p, side, 0).wait_send()
+                self.first(p, side, 1).wait_send()
+                self.second(p, side).wait_send()
+
+
+class HeadSplit:
+    def __init__(self, nd, nc, nz):
+        self.nd, self.nc, self.nz = nd, nc, nz
+        self.nm = nc * nz
+        self.span = self.nm * SPAN
+        self.rows_in = MODEL // (nd * self.nm)
+        self.wide = nd * TILE
+        self.per = HEADS // (nd * self.nm)
+
+    def fits(self):
+        return (
+            INNER == self.nd * self.nm * TILE and self.nd == 4 and self.nc == 2 and self.rows_in % 32 == 0
+        )
+
+    def place(self):
+        return lax.axis_index("dp"), lax.axis_index("seq"), lax.axis_index("fsdp")
+
+    def group_steps(self):
+        return [(e, d) for d in range(self.nz) for e in range(self.nc) if e or d]
+
+    def target(self, step):
+        dp, c, z = self.place()
+        ct, zt = lax.rem(c + step[0], self.nc), lax.rem(z + step[1], self.nz)
+        return (dp, ct, zt), ct * self.nz + zt
+
+    def source(self, step):
+        dp, c, z = self.place()
+        cs, zs = lax.rem(c + self.nc - step[0], self.nc), lax.rem(z + self.nz - step[1], self.nz)
+        return cs * self.nz + zs
+
+    def barrier(self):
+        dp, c, z = self.place()
+        sem = pltpu.get_barrier_semaphore()
+        for step in self.group_steps():
+            pl.semaphore_signal(sem, inc=1, device_id=self.target(step)[0], device_id_type=MESH)
+        for k in range(1, self.nd):
+            pl.semaphore_signal(
+                sem, inc=1, device_id=(lax.rem(dp + k, self.nd), c, z), device_id_type=MESH
+            )
+        pl.semaphore_wait(sem, self.nm - 1 + self.nd - 1)
+
+    def first_kernel(
+        self, docs, starts, unit, x_ref, par_ref, head_ref, g_ref, wm_ref, wc_ref, wo_ref,
+        y_out, x_out, g_out, w_out, wc_out, dproj, dcom, normed_out, sums, heads, pre_bc, projc, taps, gain_out, st,
+        xall, gall, wall, wcall, woall, parbuf, parall, every_par, projm, pre_sig, o, states, step_s, cum_s,
+        dg, scaled, sel, hp, chp, state, dnext, heard_st, ypart, ycame, ytotal, yheard,
+        pd_s, pd_r, pg_s, pg_r, wz_s, wz_r, cz_s, cz_r, wq_s, wq_r, cq_s, cq_r, oq_s, oq_r, cc_s, cc_r,
+        xr_s, xr_r, xl_s, xl_r, xc_s, xc_r, gr_s, gr_r, gl_s, gl_r, gc_s, gc_r,
+        st_s, st_r, yc_s, yc_r, yr_s, yr_r, yl_s, yl_r, loc,
+    ):
+        nd, nc, nz, nm = self.nd, self.nc, self.nz, self.nm
+        rows, wide = self.rows_in, self.wide
+        where = dp, c, z = self.place()
+        me = c * nz + z
+        sizes = (nc, nz)
+        steps = self.group_steps()
+        other = (dp, nc - 1 - c, z)
+        lines = [(k, (lax.rem(dp + k, nd), c, z), lax.rem(dp + nd - k, nd)) for k in range(1, nd)]
+        started = []
+
+        def go(copy):
+            copy.start()
+            started.append(copy)
+            return copy
+
+        def w_block(owner, m, first=0, count=rows):
+            at = pl.multiple_of((owner * nm + m) * rows + first, rows // 2)
+            return wall.at[pl.ds(at, count), :]
+
+        def c_block(owner, m, first=0, count=rows):
+            at = pl.multiple_of((owner * nm + m) * rows + first, rows // 2)
+            return wcall.at[pl.ds(at, count), :]
+
+        w_from = [me] + [self.source(step) for step in steps]
+        c_from = [c * nz + lax.rem(z + nz - d, nz) for d in range(nz)]
+        w_square = Square(
+            where, lambda owner, j, first, count: w_block(owner, w_from[j], first, count), rows, (wq_s, wq_r)
+        )
+        c_square = Square(
+            where, lambda owner, j, first, count: c_block(owner, c_from[j], first, count), rows, (cq_s, cq_r)
+        )
+        o_square = Square(
+            where,
+            lambda owner, j, first, count: woall.at[
+                pl.ds(pl.multiple_of(owner * TILE + first, TILE // 2), count), :
+            ],
+            TILE,
+            (oq_s, oq_r),
+        )
+        x_line = Line(where, sizes, lambda a, b: xall.at[rows_of(a * nz + b), :], (xr_s, xr_r, xl_s, xl_r, xc_s, xc_r))
+        g_line = Line(where, sizes, lambda a, b: gall.at[rows_of(a * nz + b), :], (gr_s, gr_r, gl_s, gl_r, gc_s, gc_r))
+        y_sum = Sum(where, sizes, ypart, ycame, ytotal, yheard, (yc_s, yc_r, yr_s, yr_r, yl_s, yl_r))
+
+        st[...] = jnp.zeros_like(st)
+        parbuf[dp] = par_ref[...]
+        own = [
+            pltpu.make_async_copy(wm_ref.at[me], w_block(dp, me), loc.at[0]),
+            pltpu.make_async_copy(wc_ref, c_block(dp, me), loc.at[1]),
+            pltpu.make_async_copy(wo_ref, woall.at[rows_of(dp), :], loc.at[2]),
+            pltpu.make_async_copy(g_ref, gall.at[rows_of(me), :], loc.at[3]),
+        ]
+        for copy in own:
+            copy.start()
+        self.barrier()
+        for k, device, _ in lines:
+            go(remote(parbuf.at[dp], parbuf.at[dp], pd_s.at[k], pd_r.at[k], device))
+        for j, step in enumerate(steps):
+            device, there = self.target(step)
+            go(remote(wm_ref.at[there], w_block(dp, me), wz_s.at[j], wz_r.at[j], device))
+            if step[0] == 0:
+                go(remote(wc_ref, c_block(dp, me), cz_s.at[step[1]], cz_r.at[step[1]], device))
+        for copy in own[:3]:
+            copy.wait()
+        o_square.begin(0)
+        w_square.begin(0)
+        c_square.begin(0)
+        for k, device, frm in lines:
+            remote(parbuf.at[frm], parbuf.at[frm], pd_s.at[k], pd_r.at[k], device).wait_recv()
+        parall[me] = parbuf[...]
+        for j, step in enumerate(steps):
+            device, _ = self.target(step)
+            go(remote(parbuf, parall.at[me], pg_s.at[j], pg_r.at[j], device))
+        for j, step in enumerate(steps):
+            device, _ = self.target(step)
+            remote(parbuf, parall.at[self.source(step)], pg_s.at[j], pg_r.at[j], device).wait_recv()
+        owners = [(first // nm, first % nm) for first in range(nd * nm)]
+        gain = jnp.concatenate([parall[m, d][5:6, :rows] for d, m in owners], axis=1)
+        gain_out[...] = jnp.broadcast_to(gain, (8, MODEL))
+        hidden = x_ref[...].astype(F32)
+        inverse = lax.rsqrt(jnp.mean(hidden * hidden, axis=1, keepdims=True) + EPSILON)
+        xall[rows_of(me), :] = (hidden * inverse * gain).astype(BF16)
+        x_line.begin()
+
+        for j, step in enumerate(steps):
+            device, _ = self.target(step)
+            block = w_block(dp, w_from[j + 1])
+            remote(block, block, wz_s.at[j], wz_r.at[j], device).wait_recv()
+            w_square.begin(j + 1)
+            if step[0] == 0:
+                d = step[1]
+                block = c_block(dp, c_from[d])
+                remote(block, block, cz_s.at[d], cz_r.at[d], device).wait_recv()
+                c_square.begin(d)
+            if j == 2:
+                o_square.step(0)
+                w_square.step(0)
+                c_square.step(0)
+        own_conv = CONV // (nd * nm)
+        every_par[...] = jnp.concatenate([parall[m, d][:, :own_conv] for d, m in owners], axis=1)
+        for i in range(nd):
+            at = pl.ds(pl.multiple_of((i * nm + me) * TILE, TILE), TILE)
+            taps[:, tile_of(i)] = every_par[:, at]
+        taps[:, wide:] = every_par[:, INNER : INNER + 2 * TILE]
+        head, lane = iota((TILE, TILE), 0), iota((TILE, TILE), 1)
+        step_of = nm * self.per
+        chosen = (head == lax.div(lane, self.per) * step_of + self.per * me + lax.rem(lane, self.per)) & (
+            lane < nd * self.per
+        )
+        sel[...] = chosen.astype(BF16)
+        hp[...] = exact(head_ref[...], chosen.astype(F32))
+        for i in range(nd):
+            chosen = head == i * step_of + self.per * me + lax.div(lane, HEAD_DIM)
+            spread = exact(head_ref[...], chosen.astype(F32))
+            chp[0:2, tile_of(i)] = spread[2:4, :]
+            chp[2:3, tile_of(i)] = parbuf[i][6:7, :TILE]
+        x_line.step(1)
+        for j in range(1, 4):
+            w_square.step(j)
+        for j in range(1, nz):
+            c_square.step(j)
+        x_line.step(2)
+        for j in range(4, nm):
+            w_square.step(j)
+        x_line.step(3)
+        own[3].wait()
+        g_line.begin()
+        for j in range(nz):
+            c_square.arrive(j)
+        for i in range(nd):
+            at = pl.ds(pl.multiple_of((i * nm + c * nz) * rows, rows), nz * rows)
+            go(remote(wcall.at[at, :], wcall.at[at, :], cc_s.at[i], cc_r.at[i], other))
+        x_line.arrive()
+        for j in range(nm):
+            w_square.arrive(j)
+        for i in range(nd):
+            at = pl.ds(pl.multiple_of((i * nm + (nc - 1 - c) * nz) * rows, rows), nz * rows)
+            remote(wcall.at[at, :], wcall.at[at, :], cc_s.at[i], cc_r.at[i], other).wait_recv()
+        outs = [
+            pltpu.make_async_copy(xall, x_out, loc.at[4]),
+            pltpu.make_async_copy(wall, w_out, loc.at[5]),
+            pltpu.make_async_copy(wcall, wc_out, loc.at[6]),
+        ]
+        for copy in outs:
+            copy.start()
+
+        projm[0:PAD, :] = jnp.zeros((PAD, 2 * wide), BF16)
+        projc[0:PAD, :] = jnp.zeros((PAD, COMMON), BF16)
+        projc[PAD:, :] = dot(xall[...], wcall[...]).astype(BF16)
+
+        def project(n, _):
+            at = rows_of(n, 256)
+            projm[PAD:, at] = dot(xall[...], wall[:, at]).astype(BF16)
+            pl.when(n == 2)(lambda: g_line.step(1))
+            return 0
+
+        lax.fori_loop(0, 2 * wide // 256, project, 0)
+        state[...] = jnp.zeros_like(state)
+
+        def forward(i, _):
+            self.forward_chunk(
+                i, docs, starts, projm, projc, taps, sel, hp, chp,
+                pre_sig, pre_bc, o, states, step_s, cum_s, scaled, st, state,
+            )
+            pl.when(i == 2)(lambda: g_line.step(2))
+            pl.when(i == 6)(lambda: g_line.step(3))
+            return 0
+
+        lax.fori_loop(0, nm, forward, 0)
+
+        o_square.arrive(0)
+
+        def branch(n, _):
+            turn = lax.rem(n + (nc - 1 - c) * nz, nm)
+            ypart[turn] = dot(scaled[rows_of(turn), :], woall[...]).astype(BF16)
+            return 0
+
+        lax.fori_loop(0, nz, branch, 0)
+        for t in range(nz):
+            y_sum.core(t).start()
+        lax.fori_loop(nz, nm, branch, 0)
+        for t in range(nz):
+            y_sum.add_core(t)
+        y_sum.begin()
+
+        g_line.arrive()
+        out = pltpu.make_async_copy(gall, g_out, loc.at[7])
+        out.start()
+        outs.append(out)
+        lanes_at = iota((SPAN, TILE), 1)
+
+        def gate_grad(n, _):
+            at = rows_of(n, 256)
+            grad = dot(gall[at, :], woall[...], ((1,), (1,)))
+            dg[at, :] = grad
+            for half in range(2):
+                product = jnp.zeros((SPAN, TILE), F32)
+                for i in range(nd):
+                    mine = scaled[pl.ds(pl.multiple_of(n * 256 + half * SPAN, SPAN), SPAN), tile_of(i)]
+                    product = product + mine.astype(F32) * grad[half * SPAN : (half + 1) * SPAN, tile_of(i)]
+                st[2 * n + half, 1:2, :] = jnp.where(lanes_at == 0, lane_sum(product), 0.0).T[0:1, :]
+            return 0
+
+        lax.fori_loop(0, nm // 2, gate_grad, 0)
+        sent = []
+        for j, step in enumerate(steps):
+            device, _ = self.target(step)
+            sent.append(go(remote(st, heard_st.at[j], st_s.at[j], st_r.at[j], device)))
+
+        totals = st[...]
+        for j, copy in enumerate(sent):
+            copy.wait_recv()
+            totals = totals + heard_st[j]
+        for copy in sent:
+            copy.wait_send()
+        st[...] = totals
+
+        dnext[...] = jnp.zeros_like(dnext)
+        state[...] = jnp.zeros_like(state)
+        sums[...] = jnp.zeros_like(sums)
+        heads[...] = jnp.zeros_like(heads)
+
+        def backward(n, _):
+            self.backward_chunk(
+                nm - 1 - n, docs, starts, unit, projm, pre_sig, pre_bc, o, states, step_s, cum_s, dg, st, taps, sel,
+                hp, chp, dproj, dcom, normed_out, sums, heads, state, dnext,
+            )
+            pl.when(n == 1)(lambda: y_sum.relay(1, 0))
+
+            @pl.when(n == 4)
+            def _():
+                y_sum.relay(1, 1)
+                y_sum.relay(2, 0)
+
+            return 0
+
+        lax.fori_loop(0, nm, backward, 0)
+        y_sum.arrive()
+        stat = jnp.concatenate([st[me], jnp.zeros((SPAN - 8, TILE), F32)], axis=0).T
+        root = lax.rsqrt(stat[:, 0:1] * unit[0, 0] + EPSILON)
+        y_out[...] = (x_ref[...].astype(F32) + root * y_sum.own(slice(None))).astype(BF16)
+        for copy in outs:
+            copy.wait()
+        for copy in started:
+            if not any(copy is s for s in sent):
+                copy.wait_send()
+        for j in range(nm):
+            w_square.end(j)
+        for j in range(nz):
+            c_square.end(j)
+        o_square.end(0)
+        x_line.end()
+        g_line.end()
+        y_sum.end()
+
+    def forward_chunk(
+        self, chunk, docs, starts, projm, projc, taps, sel, hp, chp,
+        pre_sig, pre_bc, o, states, step_s, cum_s, scaled, st, state,
+    ):
+        nd, wide = self.nd, self.wide
+        first = chunk * SPAN
+        here = rows_of(chunk)
+        lead = pl.ds(pl.multiple_of(chunk * SPAN, SPAN), SPAN + PAD)
+        body = pl.ds(pl.multiple_of(chunk * SPAN + PAD, PAD), SPAN)
+        lane = iota((SPAN, TILE), 1)
+        row = iota((SPAN, TILE), 0)
+        low = lane < HEAD_DIM
+        begin_t = begin_at(first + row, starts, docs)
+        begin_s = begin_at(first + lane, starts, docs)
+        valid = [first + row - (KW - 1 - tap) >= begin_t for tap in range(KW)]
+        sides = []
+        for i in range(2):
+            lanes = tile_of(i)
+            value = conv_tile(projc[lead, lanes].astype(F32), taps, tile_of(nd + i), valid)
+            pre_bc[here, lanes] = value
+            sides.append((value * jax.nn.sigmoid(value)).astype(BF16))
+        key_side, query_side = sides
+        rate = dot(projc[body, 2 * TILE :], sel[...])
+        step = softplus(rate + hp[0:1, :])
+        log_decay = step * hp[1:2, :]
+        cum = exact((lane <= row).astype(F32), log_decay)
+        step_s[here, :] = step
+        cum_s[here, :] = cum
+        cum_t = cum.T
+        shut = jnp.where((begin_t == begin_s) & (lane <= row), 0.0, NEG)
+        inherits = (begin_t < first).astype(F32)
+        begin_last = begin_at(jnp.full((SPAN, TILE), first + SPAN - 1, jnp.int32), starts, docs)
+        last_same = (begin_t == begin_last).astype(F32)
+        meet = dot(query_side, key_side, ((1,), (1,)))
+        before = state[...]
+        states[chunk] = before
+        carried_out = dot(query_side, before.astype(BF16))
+        squares = jnp.zeros((SPAN, TILE), F32)
+        for i in range(nd):
+            lanes = tile_of(i)
+            pre = conv_tile(projm[lead, tile_of(nd + i)].astype(F32), taps, lanes, valid)
+            pre_sig[here, lanes] = pre
+            signal = pre * jax.nn.sigmoid(pre)
+            cums = [head_col(cum, 2 * i), head_col(cum, 2 * i + 1)]
+            stepx = jnp.where(low, head_col(step, 2 * i), head_col(step, 2 * i + 1))
+            cumx = jnp.where(low, cums[0], cums[1])
+            fed = stepx * signal
+            fed_low = fed.astype(BF16)
+            local = []
+            for e in range(2):
+                head = 2 * i + e
+                kernel = jnp.exp(cums[e] - cum_t[head : head + 1, :] + shut)
+                local.append(dot((kernel * meet).astype(BF16), fed_low))
+            entry = jnp.exp(cumx) * inherits
+            out = jnp.where(low, local[0], local[1]) + entry * carried_out[:, lanes]
+            o[here, lanes] = out
+            last = cumx[SPAN - 1 : SPAN, :]
+            tail = jnp.exp((last - cumx) * last_same) * last_same
+            state[:, lanes] = entry[SPAN - 1 : SPAN, :] * before[:, lanes] + dot(
+                key_side, (tail * fed).astype(BF16), ((0,), (0,))
+            )
+            mixed = (out + chp[0:1, lanes] * signal) * chp[1:2, lanes]
+            gate_in = projm[body, lanes].astype(F32)
+            gated = mixed * (gate_in * jax.nn.sigmoid(gate_in))
+            squares = squares + gated * gated
+            scaled[here, lanes] = (gated * chp[2:3, lanes]).astype(BF16)
+        st[chunk, 0:1, :] = jnp.where(lane == 0, lane_sum(squares), 0.0).T[0:1, :]
+
+    def backward_chunk(
+        self, chunk, docs, starts, unit, projm, pre_sig, pre_bc, o, states, step_s, cum_s, dg, st, taps, sel,
+        hp, chp, dproj, dcom, normed_out, sums, heads, dstate, dnext,
+    ):
+        nd = self.nd
+        first = chunk * SPAN
+        here = rows_of(chunk)
+        lead = pl.ds(pl.multiple_of(chunk * SPAN, SPAN), SPAN + PAD)
+        body = pl.ds(pl.multiple_of(chunk * SPAN + PAD, PAD), SPAN)
+        lane = iota((SPAN, TILE), 1)
+        row = iota((SPAN, TILE), 0)
+        low = lane < HEAD_DIM
+        begin_t = begin_at(first + row, starts, docs)
+        begin_s = begin_at(first + lane, starts, docs)
+        shut = jnp.where((begin_t == begin_s) & (lane <= row), 0.0, NEG)
+        inherits = (begin_t < first).astype(F32)
+        begin_last = begin_at(jnp.full((SPAN, TILE), first + SPAN - 1, jnp.int32), starts, docs)
+        last_same = (begin_t == begin_last).astype(F32)
+        lower = (lane <= row).astype(F32)
+        key_pre, query_pre = pre_bc[here, :TILE], pre_bc[here, TILE:]
+        key_side = (key_pre * jax.nn.sigmoid(key_pre)).astype(BF16)
+        query_side = (query_pre * jax.nn.sigmoid(query_pre)).astype(BF16)
+        meet = dot(query_side, key_side, ((1,), (1,)))
+        step, cum = step_s[here, :], cum_s[here, :]
+        cum_t = cum.T
+        stat = jnp.concatenate([st[chunk], jnp.zeros((SPAN - 8, TILE), F32)], axis=0).T
+        square, cross = head_col(stat, 0), head_col(stat, 1)
+        root = lax.rsqrt(square * unit[0, 0] + EPSILON)
+        pull = root * root * root * cross * unit[0, 0]
+        before = states[chunk]
+        before_low = before.astype(BF16)
+        after = dstate[...]
+        after_low = after.astype(BF16)
+        carried_out = dot(query_side, before_low)
+        from_state = dot(key_side, after_low)
+        meet_grad = jnp.zeros((SPAN, SPAN), F32)
+        cum_cols = jnp.zeros((SPAN, TILE), F32)
+        cum_rows = jnp.zeros((8, SPAN), F32)
+        step_cols = jnp.zeros((SPAN, TILE), F32)
+        entered, tails = [], []
+        head_rows = iota((8, SPAN), 0)
+        next_rows = first + iota((SPAN + PAD, TILE), 0)
+        next_begin = begin_at(next_rows, starts, docs)
+        valid = [next_rows - (KW - 1 - tap) >= next_begin for tap in range(KW)]
+        tail_row = row == SPAN - 1
+        for i in range(nd):
+            lanes = tile_of(i)
+            pre = pre_sig[here, lanes]
+            gate_of = jax.nn.sigmoid(pre)
+            signal = pre * gate_of
+            gate_in = projm[body, lanes].astype(F32)
+            gate_sig = jax.nn.sigmoid(gate_in)
+            opened = gate_in * gate_sig
+            mask = chp[1:2, lanes]
+            mixed = (o[here, lanes] + chp[0:1, lanes] * signal) * mask
+            gated = mixed * opened
+            grad = dg[here, lanes]
+            gain = chp[2:3, lanes]
+            normed_out[here, lanes] = (gated * root * gain).astype(BF16)
+            sums[0:1, lanes] += jnp.sum(grad * gated * root, axis=0, keepdims=True)
+            gated_grad = root * grad * gain - gated * pull
+            mixed_grad = gated_grad * opened * mask
+            dproj[here, lanes] = (
+                gated_grad * mixed * (gate_sig * (1.0 + gate_in * (1.0 - gate_sig)))
+            ).astype(BF16)
+            sums[1:2, lanes] += jnp.sum(mixed_grad * signal, axis=0, keepdims=True)
+            cums = [head_col(cum, 2 * i), head_col(cum, 2 * i + 1)]
+            stepx = jnp.where(low, head_col(step, 2 * i), head_col(step, 2 * i + 1))
+            cumx = jnp.where(low, cums[0], cums[1])
+            fed = stepx * signal
+            fed_low = fed.astype(BF16)
+            out_grad = mixed_grad
+            out_low = out_grad.astype(BF16)
+            entry = jnp.exp(cumx) * inherits
+            last = cumx[SPAN - 1 : SPAN, :]
+            tail = jnp.exp((last - cumx) * last_same) * last_same
+            backs = []
+            for e in range(2):
+                head = 2 * i + e
+                kernel = jnp.exp(cums[e] - cum_t[head : head + 1, :] + shut)
+                mix = kernel * meet
+                half = low if e == 0 else jnp.logical_not(low)
+                mix_grad = dot(jnp.where(half, out_grad, 0.0).astype(BF16), fed_low, ((1,), (1,)))
+                meet_grad = meet_grad + kernel * mix_grad
+                weight = mix * mix_grad
+                cum_cols = cum_cols + jnp.where(lane == head, lane_sum(weight), 0.0)
+                cum_rows = cum_rows + jnp.where(
+                    head_rows == head, jnp.broadcast_to(jnp.sum(weight, axis=0, keepdims=True), (8, SPAN)), 0.0
+                )
+                backs.append(dot(mix.astype(BF16), out_low, ((0,), (0,))))
+            entry_grad = entry * out_grad
+            tail_fed = tail * fed
+            entered.append(entry_grad.astype(BF16))
+            tails.append(tail_fed.astype(BF16))
+            fed_grad = jnp.where(low, backs[0], backs[1]) + tail * from_state[:, lanes]
+            moved_in = entry_grad * carried_out[:, lanes]
+            moved_out = tail_fed * from_state[:, lanes]
+            direct = fed_grad * signal
+            end = entry[SPAN - 1 : SPAN, :]
+            kept = jnp.sum(after[:, lanes] * before[:, lanes], axis=0, keepdims=True) * end
+            at_end = jnp.sum(moved_out, axis=0, keepdims=True) + kept
+            local = moved_in - moved_out + jnp.where(tail_row, at_end, 0.0)
+            for e in range(2):
+                half = low if e == 0 else jnp.logical_not(low)
+                place = lane == 2 * i + e
+                cum_cols = cum_cols + jnp.where(place, lane_sum(jnp.where(half, local, 0.0)), 0.0)
+                step_cols = step_cols + jnp.where(place, lane_sum(jnp.where(half, direct, 0.0)), 0.0)
+            dstate[:, lanes] = end * after[:, lanes] + dot(query_side, entry_grad.astype(BF16), ((0,), (0,)))
+            signal_grad = stepx * fed_grad + chp[0:1, lanes] * mixed_grad
+            pre_grad = signal_grad * (gate_of * (1.0 + pre * (1.0 - gate_of)))
+            sums[2:3, lanes] += jnp.sum(pre_grad, axis=0, keepdims=True)
+            later = jnp.concatenate([pre_grad, dnext[:, lanes]], axis=0)
+            dnext[:, lanes] = pre_grad[0:PAD, :]
+            cols = tile_of(nd + i)
+            ext = projm[lead, cols].astype(F32)
+            back_grad = jnp.zeros((SPAN, TILE), F32)
+            for tap in range(KW):
+                back = KW - 1 - tap
+                masked = jnp.where(valid[tap], later, 0.0)
+                moved = ext if back == 0 else pltpu.roll(ext, back, 0)
+                sums[4 + tap : 5 + tap, lanes] += jnp.sum(masked[:SPAN] * moved[PAD:], axis=0, keepdims=True)
+                ahead = masked if back == 0 else pltpu.roll(masked, SPAN + PAD - back, 0)
+                back_grad = back_grad + ahead[:SPAN] * taps[tap : tap + 1, lanes]
+            dproj[here, cols] = back_grad.astype(BF16)
+        meet_low = meet_grad.astype(BF16)
+        state_rows = ((1,), (1,))
+        query_grad = dot(meet_low, key_side) + dot(jnp.concatenate(entered, axis=1), before_low, state_rows)
+        key_grad = dot(meet_low, query_side, ((0,), (0,))) + dot(
+            jnp.concatenate(tails, axis=1), after_low, state_rows
+        )
+        dcom[here, :TILE] = key_grad.astype(BF16)
+        dcom[here, TILE : 2 * TILE] = query_grad.astype(BF16)
+        rows_t = jnp.concatenate([cum_rows, jnp.zeros((SPAN - 8, SPAN), F32)], axis=0).T
+        decay_grad = exact(lower, cum_cols - rows_t, ((0,), (0,)))
+        log_decay = step * hp[1:2, :]
+        slope = 1.0 - jnp.exp(-step)
+        rate_grad = (step_cols + decay_grad * hp[1:2, :]) * slope
+        heads[0:1, :] += jnp.sum(rate_grad, axis=0, keepdims=True)
+        heads[1:2, :] += jnp.sum(decay_grad * log_decay, axis=0, keepdims=True)
+        dcom[here, 2 * TILE :] = dot(rate_grad.astype(BF16), sel[...], ((1,), (1,))).astype(BF16)
+
+    def first(self, docs, starts, unit, x, par, heads, g, wm, wc, wo):
+        nd, nz, nm, rows, span, wide = self.nd, self.nz, self.nm, self.rows_in, self.span, self.wide
+        like = jax.ShapeDtypeStruct
+        block = (SPAN, MODEL)
+        return pl.pallas_call(
+            functools.partial(self.first_kernel, docs),
+            out_shape=[
+                like(block, BF16),
+                like((span, MODEL), BF16),
+                like((span, MODEL), BF16),
+                like((MODEL, 2 * wide), BF16),
+                like((MODEL, COMMON), BF16),
+                like((span, 2 * wide), BF16),
+                like((span, COMMON), BF16),
+                like((span, wide), BF16),
+                like((8, wide), F32),
+                like((8, TILE), F32),
+                like((span, 2 * TILE), F32),
+                like((PAD + span, COMMON), BF16),
+                like((8, wide + 2 * TILE), F32),
+                like((8, MODEL), F32),
+                like((nm, 8, TILE), F32),
+            ],
+            in_specs=[SM, SM, VM, VM, VM, ANY, ANY, ANY, ANY],
+            out_specs=[VM, ANY, ANY, ANY, ANY] + [VM] * 10,
+            scratch_shapes=[
+                pltpu.VMEM((span, MODEL), BF16),
+                pltpu.VMEM((span, MODEL), BF16),
+                pltpu.VMEM((MODEL, 2 * wide), BF16),
+                pltpu.VMEM((MODEL, COMMON), BF16),
+                pltpu.VMEM((wide, MODEL), BF16),
+                pltpu.VMEM((nd, 8, 2 * TILE), F32),
+                pltpu.VMEM((nm, nd, 8, 2 * TILE), F32),
+                pltpu.VMEM((8, CONV), F32),
+                pltpu.VMEM((PAD + span, 2 * wide), BF16),
+                pltpu.VMEM((span, wide), F32),
+                pltpu.VMEM((span, wide), F32),
+                pltpu.VMEM((nm, STATE, wide), F32),
+                pltpu.VMEM((span, TILE), F32),
+                pltpu.VMEM((span, TILE), F32),
+                pltpu.VMEM((span, wide), F32),
+                pltpu.VMEM((span, wide), BF16),
+                pltpu.VMEM((TILE, TILE), BF16),
+                pltpu.VMEM((8, TILE), F32),
+                pltpu.VMEM((8, wide), F32),
+                pltpu.VMEM((STATE, wide), F32),
+                pltpu.VMEM((PAD, wide), F32),
+                pltpu.VMEM((nm - 1, nm, 8, TILE), F32),
+                pltpu.VMEM((nm, *block), BF16),
+                pltpu.VMEM((nz, *block), BF16),
+                pltpu.VMEM((nz, *block), BF16),
+                pltpu.VMEM((2 * nz, *block), BF16),
+                DMA((nd,)), DMA((nd,)), DMA((nm,)), DMA((nm,)),
+                DMA((nm,)), DMA((nm,)), DMA((nz,)), DMA((nz,)),
+                DMA((4, nm)), DMA((4, nm)), DMA((4, nz)), DMA((4, nz)), DMA((4, 1)), DMA((4, 1)),
+                DMA((nd,)), DMA((nd,)),
+                DMA((nz,)), DMA((nz,)), DMA((nz,)), DMA((nz,)), DMA((nz,)), DMA((nz,)),
+                DMA((nz,)), DMA((nz,)), DMA((nz,)), DMA((nz,)), DMA((nz,)), DMA((nz,)),
+                DMA((nm,)), DMA((nm,)),
+                DMA((nz,)), DMA((nz,)), DMA((nz,)), DMA((nz,)), DMA((nz,)), DMA((nz,)),
+                DMA((8,)),
+            ],
+            compiler_params=pltpu.CompilerParams(
+                collective_id=0, has_side_effects=True, vmem_limit_bytes=62 * 2**20
+            ),
+            name="first",
+        )(starts, unit, x, par, heads, g, wm, wc, wo)
+
+    def second_kernel(
+        self, docs, starts, dproj, dcom, normed_out, sums, heads, pre_bc, projc, taps, gain, x_ref, g_ref,
+        x_in, g_in, w_in, wc_in,
+        dx_out, dw_out, dwc_out, dwo_out, par_out,
+        xall, gall, wall, wcall, xpart, xcame, xtotal, xheard,
+        padded, ccame, ctotal, cheard, every, dxc, x_rows, wcpart, wccame,
+        wpart, w1, w2, wgo, wsum, opart, o1, o2, ogo, pard, parbuf,
+        xc_s, xc_r, xr_s, xr_r, xl_s, xl_r, cc_s, cc_r, cz_s, cz_r, ez_s, ez_r, ec_s, ec_r,
+        w1_s, w1_r, w2_s, w2_r, o1_s, o1_r, o2_s, o2_r, wz_s, wz_r, wcd_s, wcd_r, pd_s, pd_r, pg_s, pg_r, loc,
+    ):
+        nd, nc, nz, nm = self.nd, self.nc, self.nz, self.nm
+        rows, wide, span = self.rows_in, self.wide, self.span
+        where = dp, c, z = self.place()
+        me = c * nz + z
+        sizes = (nc, nz)
+        steps = self.group_steps()
+        other = (dp, nc - 1 - c, z)
+        long = SPAN + PAD
+        started = []
+
+        def go(copy):
+            copy.start()
+            started.append(copy)
+            return copy
+
+        loads = [
+            pltpu.make_async_copy(w_in, wall, loc.at[0]),
+            pltpu.make_async_copy(x_in, xall, loc.at[1]),
+            pltpu.make_async_copy(wc_in, wcall, loc.at[2]),
+            pltpu.make_async_copy(g_in, gall, loc.at[3]),
+        ]
+        for load in loads:
+            load.start()
+        padded[0:span, :] = dcom[...]
+        padded[span:, :] = jnp.zeros((PAD, COMMON), BF16)
+        self.barrier()
+        x_sum = Sum(where, sizes, xpart, xcame, xtotal, xheard, (xc_s, xc_r, xr_s, xr_r, xl_s, xl_r))
+        w_sum = SquareSum(where, wpart, w1, w2, wgo, (w1_s, w1_r, w2_s, w2_r), 2)
+        o_sum = SquareSum(where, opart, o1, o2, ogo, (o1_s, o1_r, o2_s, o2_r), 1)
+
+        def c_rows(m):
+            return pl.ds(pl.multiple_of(m * SPAN, SPAN), long)
+
+        ccopies = [
+            go(remote(padded.at[c_rows((nc - 1 - c) * nz + t), :], ccame.at[t], cc_s.at[t], cc_r.at[t], other))
+            for t in range(nz)
+        ]
+        loads[0].wait()
+
+        def input_grad(n, _):
+            at = rows_of(n, 256)
+            base = rows_of(nc - 1 - c, nz * SPAN)
+            part = dot(dproj[base, :], wall[at, :], ((1,), (1,))).astype(BF16)
+            for t in range(nz):
+                xpart[(nc - 1 - c) * nz + t, :, at] = part[t * SPAN : (t + 1) * SPAN, :]
+            return 0
+
+        lax.fori_loop(0, MODEL // 256, input_grad, 0)
+        for t in range(nz):
+            x_sum.core(t).start()
+        for t in range(nz):
+            ccopies[t].wait_recv()
+            ctotal[t] = (padded[c_rows(c * nz + t), :].astype(F32) + ccame[t].astype(F32)).astype(BF16)
+        for d in range(1, nz):
+            to = lax.rem(z + d, nz)
+            go(remote(ctotal.at[to], cheard.at[d - 1], cz_s.at[d], cz_r.at[d], (dp, c, to)))
+
+        def own_grad(n, _):
+            at = rows_of(n, 256)
+            base = rows_of(c, nz * SPAN)
+            part = dot(dproj[base, :], wall[at, :], ((1,), (1,))).astype(BF16)
+            for t in range(nz):
+                xpart[c * nz + t, :, at] = part[t * SPAN : (t + 1) * SPAN, :]
+            return 0
+
+        lax.fori_loop(0, MODEL // 256, own_grad, 0)
+        for t in range(nz):
+            x_sum.add_core(t)
+        x_sum.begin()
+
+        total = ctotal[z].astype(F32)
+        for d in range(1, nz):
+            remote(cheard.at[d - 1], cheard.at[d - 1], cz_s.at[d], cz_r.at[d], other).wait_recv()
+            total = total + cheard[d - 1].astype(F32)
+        base = pl.multiple_of(me * SPAN, SPAN)
+        after = pl.multiple_of(lax.rem(me + 1, nm) * SPAN, SPAN)
+        places = base + iota((long, TILE), 0)
+        begin = begin_at(places, starts, docs)
+        inside = places < span
+        counts = MODEL // TILE + 8 * nd
+        parbuf[counts : counts + 16, :] = jnp.zeros((16, TILE), F32)
+        for i in range(2):
+            lanes = tile_of(i)
+            pre = jnp.concatenate([pre_bc[pl.ds(base, SPAN), lanes], pre_bc[pl.ds(after, PAD), lanes]], axis=0)
+            later = jnp.where(inside, total[:, lanes] * silu_slope(pre), 0.0)
+            ext = projc[pl.ds(base, long), lanes].astype(F32)
+            parbuf[counts + i : counts + i + 1, :] = jnp.sum(later[:SPAN], axis=0, keepdims=True)
+            back_grad = jnp.zeros((SPAN, TILE), F32)
+            for tap in range(KW):
+                back = KW - 1 - tap
+                masked = jnp.where(places - back >= begin, later, 0.0)
+                moved = ext if back == 0 else pltpu.roll(ext, back, 0)
+                at = counts + 2 + 2 * tap + i
+                parbuf[at : at + 1, :] = jnp.sum(masked[:SPAN] * moved[PAD:], axis=0, keepdims=True)
+                ahead = masked if back == 0 else pltpu.roll(masked, long - back, 0)
+                back_grad = back_grad + ahead[:SPAN] * taps[tap : tap + 1, tile_of(nd + i)]
+            every[me, :, lanes] = back_grad.astype(BF16)
+        every[me, :, 2 * TILE :] = total[:SPAN, 2 * TILE :].astype(BF16)
+        mine = every.at[me]
+        for d in range(1, nz):
+            go(remote(mine, mine, ez_s.at[d], ez_r.at[d], (dp, c, lax.rem(z + d, nz))))
+        go(remote(mine, mine, ec_s.at[0], ec_r.at[0], other))
+
+        loads[1].wait()
+
+        def weight_grad(owner):
+            def piece(n, _):
+                at = pl.ds(pl.multiple_of(owner * (nm * rows) + n * 256, 256), 256)
+                wpart[owner, rows_of(n, 256), :] = dot(xall[:, at], dproj[...], ((0,), (0,))).astype(BF16)
+                return 0
+
+            lax.fori_loop(0, nm * rows // 256, piece, 0)
+
+        weight_grad(w_sum.diag)
+        weight_grad(w_sum.dx)
+        for p in range(2):
+            w_sum.begin_x(p)
+        weight_grad(w_sum.dy)
+        for p in range(2):
+            w_sum.begin_y(p)
+        x_sum.relay(1, 0)
+        weight_grad(dp)
+        loads[2].wait()
+        dxc[...] = dot(every[me], wcall[...], ((1,), (1,)))
+        loads[3].wait()
+
+        def out_grad(n, _):
+            at = rows_of(n, 512)
+            part = dot(normed_out[...], gall[:, at], ((0,), (0,))).astype(BF16)
+            for i in range(nd):
+                opart[i, :, at] = part[tile_of(i), :]
+            return 0
+
+        lax.fori_loop(0, MODEL // 512, out_grad, 0)
+        o_sum.begin_x(0)
+        o_sum.begin_y(0)
+        for d in range(1, nz):
+            block = every.at[c * nz + lax.rem(z + nz - d, nz)]
+            remote(block, block, ez_s.at[d], ez_r.at[d], other).wait_recv()
+            go(remote(block, block, ec_s.at[d], ec_r.at[d], other))
+        w_sum.pass_on(0)
+        x_sum.relay(1, 1)
+        x_sum.relay(2, 0)
+        for i in range(nd):
+            pair = pl.ds(pl.multiple_of(i * (nm * rows) + (me // 2) * (2 * rows), 2 * rows), 2 * rows)
+            both = xall[:, pair]
+            x_rows[:, i * rows : (i + 1) * rows] = jnp.where(
+                lax.rem(me, 2) == 0, both[:, :rows].astype(F32), both[:, rows:].astype(F32)
+            ).astype(BF16)
+        for d in range(nz):
+            block = every.at[(nc - 1 - c) * nz + lax.rem(z + nz - d, nz)]
+            remote(block, block, ec_s.at[d], ec_r.at[d], other).wait_recv()
+        shared = dot(x_rows[...], every[...].reshape(span, COMMON), ((0,), (0,))).astype(BF16)
+        for i in range(nd):
+            wcpart[i] = shared[i * rows : (i + 1) * rows, :]
+        lines = [(k, (lax.rem(dp + k, nd), c, z), lax.rem(dp + k, nd)) for k in range(1, nd)]
+        wc_copies = [
+            go(remote(wcpart.at[to], wccame.at[k - 1], wcd_s.at[k], wcd_r.at[k], device)) for k, device, to in lines
+        ]
+        w_sum.pass_on(1)
+
+        def send_rows(p):
+            half = nm // 2
+            for j in range(half):
+                there = p * half + j
+                block = wsum.at[there * rows : (there + 1) * rows, :]
+                ct, zt = there // nz, there % nz
+
+                @pl.when(there != me)
+                def _():
+                    remote(block, dw_out.at[me], wz_s.at[there], wz_r.at[me], (dp, ct, zt)).start()
+
+                @pl.when(there == me)
+                def _():
+                    dw_out[there] = block[...]
+
+        w_sum.finish(0, wsum)
+        send_rows(0)
+        o_sum.pass_on(0)
+
+        x_sum.arrive()
+        hidden = x_ref[...].astype(F32)
+        normed_grad = x_sum.own(slice(None)) + dxc[...]
+        inverse = lax.rsqrt(jnp.mean(hidden * hidden, axis=1, keepdims=True) + EPSILON)
+        unitary = hidden * inverse
+        gain_grad = jnp.sum(normed_grad * unitary, axis=0, keepdims=True)
+        grad_scaled = normed_grad * gain[0:1, :]
+        middle = jnp.mean(grad_scaled * unitary, axis=1, keepdims=True)
+        dx_out[...] = (g_ref[...].astype(F32) + inverse * (grad_scaled - unitary * middle)).astype(BF16)
+        base_row = MODEL // TILE
+        for i in range(base_row):
+            parbuf[i : i + 1, :] = gain_grad[:, tile_of(i)]
+        for r in range(8):
+            for i in range(nd):
+                parbuf[base_row + r * nd + i : base_row + r * nd + i + 1, :] = sums[r : r + 1, tile_of(i)]
+        parbuf[counts + 16 :, :] = heads[...]
+        small = [
+            go(remote(parbuf, pard.at[k - 1], pd_s.at[k], pd_r.at[k], device)) for k, device, _ in lines
+        ]
+        w_sum.finish(1, wsum)
+        send_rows(1)
+        for copy in small:
+            copy.wait_recv()
+        total = parbuf[...]
+        for k in range(nd - 1):
+            total = total + pard[k]
+        par_out[me] = total
+        for j, step in enumerate(steps):
+            go(remote(par_out.at[me], par_out.at[me], pg_s.at[j], pg_r.at[j], self.target(step)[0]))
+        o_sum.finish(0, dwo_out)
+        for copy in wc_copies:
+            copy.wait_recv()
+        total = wcpart[dp].astype(F32)
+        for k in range(nd - 1):
+            total = total + wccame[k].astype(F32)
+        dwc_out[...] = total
+        for j, step in enumerate(steps):
+            here = par_out.at[self.source(step)]
+            remote(here, here, pg_s.at[j], pg_r.at[j], other).wait_recv()
+        for m in range(nm):
+            got = dw_out.at[m]
+
+            @pl.when(m != me)
+            def _():
+                remote(got, got, wz_s.at[m], wz_r.at[m], other).wait_recv()
+                remote(got, got, wz_s.at[m], wz_r.at[m], other).wait_send()
+
+        for copy in started:
+            copy.wait_send()
+        x_sum.end()
+        w_sum.end()
+        o_sum.end()
+
+    def second(self, docs, starts, dproj, dcom, normed_out, sums, heads, pre_bc, projc, taps, gain, x, g, xall, gall, w, wc):
+        nd, nz, nm, rows, span, wide = self.nd, self.nz, self.nm, self.rows_in, self.span, self.wide
+        like = jax.ShapeDtypeStruct
+        block = (SPAN, MODEL)
+        npar = MODEL // TILE + 8 * nd + 16 + 8
+        long = SPAN + PAD
+        return pl.pallas_call(
+            functools.partial(self.second_kernel, docs),
+            out_shape=[
+                like(block, BF16),
+                like((nm, rows, 2 * wide), BF16),
+                like((rows, COMMON), F32),
+                like((TILE, MODEL), F32),
+                like((nm, npar, TILE), F32),
+            ],
+            in_specs=[SM] + [VM] * 11 + [ANY] * 4,
+            out_specs=[VM] * 5,
+            scratch_shapes=[
+                pltpu.VMEM((span, MODEL), BF16),
+                pltpu.VMEM((span, MODEL), BF16),
+                pltpu.VMEM((MODEL, 2 * wide), BF16),
+                pltpu.VMEM((MODEL, COMMON), BF16),
+                pltpu.VMEM((nm, *block), BF16),
+                pltpu.VMEM((nz, *block), BF16),
+                pltpu.VMEM((nz, *block), BF16),
+                pltpu.VMEM((2 * nz, *block), BF16),
+                pltpu.VMEM((span + PAD, COMMON), BF16),
+                pltpu.VMEM((nz, long, COMMON), BF16),
+                pltpu.VMEM((nz, long, COMMON), BF16),
+                pltpu.VMEM((nz - 1, long, COMMON), BF16),
+                pltpu.VMEM((nm, SPAN, COMMON), BF16),
+                pltpu.VMEM(block, F32),
+                pltpu.VMEM((span, nd * rows), BF16),
+                pltpu.VMEM((nd, rows, COMMON), BF16),
+                pltpu.VMEM((nd - 1, rows, COMMON), BF16),
+                pltpu.VMEM((nd, nm * rows, 2 * wide), BF16),
+                pltpu.VMEM((4, nm * rows, wide), BF16),
+                pltpu.VMEM((2, nm * rows, wide), BF16),
+                pltpu.VMEM((2, nm * rows, wide), BF16),
+                pltpu.VMEM((nm * rows, 2 * wide), BF16),
+                pltpu.VMEM((nd, TILE, MODEL), BF16),
+                pltpu.VMEM((4, TILE, MODEL // 2), BF16),
+                pltpu.VMEM((2, TILE, MODEL // 2), BF16),
+                pltpu.VMEM((2, TILE, MODEL // 2), BF16),
+                pltpu.VMEM((nd - 1, npar, TILE), F32),
+                pltpu.VMEM((npar, TILE), F32),
+                DMA((nz,)), DMA((nz,)), DMA((nz,)), DMA((nz,)), DMA((nz,)), DMA((nz,)),
+                DMA((nz,)), DMA((nz,)), DMA((nz,)), DMA((nz,)), DMA((nz,)), DMA((nz,)), DMA((nz,)), DMA((nz,)),
+                DMA((2, 4)), DMA((2, 4)), DMA((2, 2)), DMA((2, 2)),
+                DMA((1, 4)), DMA((1, 4)), DMA((1, 2)), DMA((1, 2)),
+                DMA((nm,)), DMA((nm,)), DMA((nd,)), DMA((nd,)), DMA((nd,)), DMA((nd,)),
+                DMA((nm,)), DMA((nm,)), DMA((4,)),
+            ],
+            compiler_params=pltpu.CompilerParams(
+                collective_id=1, has_side_effects=True, vmem_limit_bytes=62 * 2**20
+            ),
+            name="second",
+        )(starts, dproj, dcom, normed_out, sums, heads, pre_bc, projc, taps, gain, x, g, xall, gall, w, wc)
+
+    def local(
+        self, layer_input, out_grad, norm_gain, in_weight, conv_weight, conv_bias, step_bias, log_rate,
+        skip_gain, gate_gain, out_weight, nest_level, doc_lengths,
+    ):
+        nd, nz, nm, rows, wide = self.nd, self.nz, self.nm, self.rows_in, self.wide
+        dp, c, z = self.place()
+        me = c * nz + z
+        docs = doc_lengths.shape[1]
+        order = jnp.arange(docs)
+        ahead = order[:, None] < order[None, :]
+        starts = jnp.sum(jnp.where(ahead, doc_lengths[0][:, None], 0), axis=0, keepdims=True)
+        starts = starts.astype(jnp.int32)
+        active = jnp.right_shift(HEADS, 3 - nest_level[0])
+        unit = (1.0 / (active * HEAD_DIM).astype(F32)).reshape(1, 1)
+        x = layer_input.reshape(SPAN, MODEL)
+        g = out_grad.reshape(SPAN, MODEL)
+        wm = in_weight[:, : 2 * INNER].reshape(rows, 2 * nd, nm, TILE)
+        wm = jnp.transpose(wm, (2, 0, 1, 3)).reshape(nm, rows, 2 * wide)
+        wc = jnp.pad(in_weight[:, 2 * INNER :], ((0, 0), (0, COMMON - (EXTENT - 2 * INNER))))
+        own_conv = conv_bias.shape[0]
+        widen = lambda v: jnp.pad(v, ((0, 0), (0, 2 * TILE - v.shape[1])))
+        par = jnp.concatenate(
+            [
+                widen(conv_weight.T),
+                widen(conv_bias[None]),
+                widen(norm_gain[None]),
+                widen(gate_gain[None]),
+                jnp.zeros((1, 2 * TILE), F32),
+            ]
+        )
+        mask = (jnp.arange(HEADS) < active).astype(F32)
+        head_in = jnp.stack([step_bias, -jnp.exp(log_rate), skip_gain, mask])
+        head_in = jnp.pad(head_in, ((0, 4), (0, TILE - HEADS)))
+        (
+            y_out, xall, gall, w, wc_all, dproj, dcom, normed_out, sums, heads, pre_bc, projc, taps, gain, _,
+        ) = self.first(docs, starts, unit, x, par, head_in, g, wm, wc, out_weight)
+        dx_out, dw, dwc, dwo, pars = self.second(
+            docs, starts, dproj, dcom, normed_out, sums, heads, pre_bc, projc, taps, gain, x, g, xall, gall, w, wc_all
+        )
+        dw = jnp.transpose(dw.reshape(nm, rows, 2 * nd, TILE), (1, 2, 0, 3)).reshape(rows, 2 * INNER)
+        in_weight_grad = jnp.concatenate([dw.astype(F32), dwc[:, : EXTENT - 2 * INNER]], axis=1)
+        owner = dp * nm + me
+        gains = jnp.sum(pars[:, : MODEL // TILE], axis=0).reshape(MODEL)
+        norm_gain_grad = lax.dynamic_slice_in_dim(gains, owner * rows, rows)
+        base = MODEL // TILE
+        mains = pars[:, base : base + 8 * nd].reshape(nm, 8, nd, TILE)
+        shared = jnp.sum(pars[:, base + 8 * nd : base + 8 * nd + 16], axis=0)
+        head_sums = pars[:, base + 8 * nd + 16 :]
+        gate_gain_grad = lax.dynamic_index_in_dim(mains[me, 0], dp, 0, keepdims=False)
+        everything = jnp.transpose(mains[:, 1:], (1, 2, 0, 3)).reshape(7, INNER)
+        skip_gain_grad = jnp.sum(everything[0].reshape(HEADS, HEAD_DIM), axis=1)
+        bias_sum = jnp.concatenate([everything[1], shared[:2].reshape(-1)])
+        taps_sum = jnp.concatenate([everything[3:], shared[2:10].reshape(KW, 2 * TILE)], axis=1).T
+        conv_bias_grad = lax.dynamic_slice_in_dim(bias_sum, owner * own_conv, own_conv)
+        conv_weight_grad = lax.dynamic_slice_in_dim(taps_sum, owner * own_conv, own_conv)
+        mine = nd * self.per
+        by_head = lambda v: jnp.swapaxes(v[:, :mine].reshape(nm, nd, self.per), 0, 1).reshape(HEADS)
+        step_bias_grad, log_rate_grad = by_head(head_sums[:, 0]), by_head(head_sums[:, 1])
+        return (
+            y_out.reshape(1, SPAN, MODEL),
+            dx_out.reshape(1, SPAN, MODEL),
+            norm_gain_grad,
+            in_weight_grad,
+            conv_weight_grad,
+            conv_bias_grad,
+            step_bias_grad,
+            log_rate_grad,
+            skip_gain_grad,
+            gate_gain_grad,
+            dwo,
+        )
+
+
 def solution(mesh):
+    shape = dict(mesh.shape)
+    head_split = HeadSplit(shape["dp"], shape["seq"], shape["fsdp"])
     return jax.shard_map(
-        local,
+        head_split.local if head_split.fits() else token_split,
         mesh=mesh,
         in_specs=(
             P("dp", ("seq", "fsdp"), None),

time: 1080 us -> 329 us (0.30)
  waiting for transfers between devices: 437 us -> 0 us
  blocking collectives: 334 us -> 0 us
  Pallas kernels: 0 us -> 301 us
  matrix products: 139 us -> 0 us
  other arithmetic: 117 us -> 7.54 us
  between operations: 15.9 us -> 1.51 us
    all_gather x6 -> x0, waiting for transfers between devices: 310 us -> none  [the longest x1 93.7 us: local(): lax.all_gather(in_weight, ('dp', 'seq', 'fsdp'), axis=0, tiled=True)]
    pallas_call x0 -> x2, Pallas kernels: none -> 301 us  [the longest x1 199 us: first(): pl.pallas_call(functools.partial(self.first_kernel, docs), out_shape=[lik...]
    all_gather x3 -> x0, blocking collectives: 154 us -> none  [the longest x1 73.2 us: local(): lax.all_gather(conv_weight, ('dp', 'seq', 'fsdp'), axis=0, tiled=True)]
    dot_general x18 -> x0, matrix products: 139 us -> none  [the longest x3 24.7 us: scan_parts(): local_out = jnp.einsum('bhts,bshp->bthp', mixing, signal, precision=HIGH)]
    all_to_all x2 -> x0, blocking collectives: 101 us -> none  [the longest x1 59.6 us: local(): lax.all_to_all(normed_out.reshape(token_count, replicas, members, width_o...]
    unnamed x2 -> x0, blocking collectives: 79.2 us -> none
    reduce_scatter x2 -> x0, waiting for transfers between devices: 68.1 us -> none  [the longest x1 58.6 us: local(): lax.psum_scatter(in_new.astype(jnp.bfloat16), 'dp', scatter_dimension=0,...]
    unnamed x10 -> x0, waiting for transfers between devices: 55.1 us -> none
  transfers between devices with their start and end apart: 11 -> 0, of which waited for: 9 -> 0; matrix products, arithmetic and copies ran while one was open for 20% -> 0% of each run, Pallas kernels for 0% -> 0%
where the time goes in v2:
time: 329 us
  Pallas kernels  301 us (91%)
  local copies, waits for them, and re-layouts  18.2 us (6%)
  other arithmetic  7.54 us (2%)
    pallas_call x1, Pallas kernels, first(): pl.pallas_call(functools.partial(self.first_kernel, docs), out_shape=[lik...  199 us
    pallas_call x1, Pallas kernels, second(): pl.pallas_call(functools.partial(self.second_kernel, docs), out_shape=[li...  102 us
    unnamed x18, local copies, waits for them, and re-layouts  6.87 us

profile of v2, /device:TPU:0, one launch (start us, length us, event | category | flops | bytes accessed | tf_op | source)
XLA Modules:
  0.0 328.7 jit_solution(4831748509892271129)
XLA Ops:
  0.6 1.2 select_reduce_fusion
  2.6 0.7 pad.24
  3.3 0.7 pad.25
  4.0 0.7 pad.26
  4.6 0.7 pad.27
  5.3 0.6 concatenate.12.par_ref
  5.9 0.7 negate_bitcast_fusion
  6.6 1.3 select_maximum_fusion.head_ref
  7.8 1.3 slice_bitcast_fusion
  9.1 0.3 copy.46
  9.4 0.0 slice-start
  9.4 0.1 copy.55
  9.6 1.3 reshape.100.wm_ref
  10.9 0.0 slice-done
  10.9 0.6 pad.29.wc_ref
  11.5 199.1 %first.1 = (bf16[128,2048]{1,0:T(8,128)(2,1)}, bf16[1024,2048]{1,0:T(8,128)(2,1)}, bf16[1024,2048]{1,0:T(8,128)(2,1)}, bf16[2048,1024]{1,0:T(8,128)(2,1)}, bf16[...) custom-call(s32[1,4]{1,0:T(1,128)} %bitcast.95, ...), custom_call_target="tpu_custom_call" | custom-call | tf_op jit(solution)/shard_map/first/pallas_call | solution.py:1213
  210.6 102.3 %second.1 = (bf16[128,2048]{1,0:T(8,128)(2,1)}, bf16[8,64,1024]{2,1,0:T(8,128)(2,1)}, f32[64,384]{1,0:T(8,128)}, f32[128,2048]{1,0:T(8,128)}, f32[8,72,128]{2,1,0:T(8,128)}) custom-call(s32[1,4]{1,0:T(1,128)} %bitcast.96, bf16[1024,1024]{1,0:T(8,128)(2,1)} %get-tuple-element.31.dproj, bf16[1024,384]{1,0:T(8,128)(2,1)} %get-tuple-element.32.dcom, ...), custom_call_target="tpu_custom_call" | custom-call | tf_op jit(solution)/shard_map/second/pallas_call | solution.py:1526
  312.9 0.9 slice_reduce_fusion
  313.8 0.6 dynamic_slice.14
  314.4 1.5 copy.47
  315.9 0.1 bitcast_bitcast_fusion
  316.1 1.2 copy.39
  317.3 0.0 copy-start.3
  317.3 1.2 copy.54
  318.5 0.0 copy-done.3
  318.5 0.0 copy-start.1
  318.5 1.5 pad_maximum_fusion
  320.0 0.0 copy-start.2
  320.0 0.0 copy-start
  320.0 1.0 slice.60
  321.2 0.7 fusion.1
  321.9 0.6 fusion.2
  322.5 0.8 fusion.4
  323.3 0.1 copy.41
  323.4 0.1 copy.42
  323.5 0.6 reshape.108
  324.1 0.1 copy.43
  324.2 0.1 copy.44
  324.3 0.6 reshape.110
  324.9 0.1 reshape_squeeze.3
  325.0 0.6 reduce_sum.39
  325.6 0.5 fusion.3
  326.1 0.0 copy-done.1
  326.1 0.8 copy.62
  326.9 0.0 copy-done.2
  326.9 0.8 copy.63
  327.7 0.0 copy-done
  327.7 1.0 copy.64
  (10 shorter events, 0.1 us)
Async XLA Ops:
  9.4 1.4 slice-start
  317.3 1.2 copy-start.3
  318.5 7.6 %copy-start.1 = (bf16[128,2048]{1,0:T(8,128)(2,1)S(1)}, bf16[128,2048]{1,0:T(8,128)(2,1)}, u32[]{:S(2)}) copy-start(bf16[128,2048]{1,0:T(8,128)(2,1)} %get-tuple-element.30) | copy-start | bytes 1572868
  320.0 6.9 %copy-start.2 = (bf16[128,2048]{1,0:T(8,128)(2,1)S(1)}, bf16[128,2048]{1,0:T(8,128)(2,1)}, u32[]{:S(2)}) copy-start(bf16[128,2048]{1,0:T(8,128)(2,1)} %get-tuple-element.44) | copy-start | bytes 1572868
  320.0 7.7 %copy-start = (f32[128,2048]{1,0:T(8,128)S(1)}, f32[128,2048]{1,0:T(8,128)}, u32[]{:S(2)}) copy-start(f32[128,2048]{1,0:T(8,128)} %get-tuple-element.76) | copy-start | bytes 3145732

commit v3 on v2

--- a/solution.py
+++ b/solution.py
@@ -350,6 +350,7 @@
 COMMON = 384
 PAD = 16
 NEG = -1e30
+SLOTS = (1, 4)
 VM = pl.BlockSpec(memory_space=pltpu.VMEM)
 SM = pl.BlockSpec(memory_space=pltpu.SMEM)
 ANY = pl.BlockSpec(memory_space=pl.ANY)
@@ -528,26 +529,35 @@
 
     def begin(self):
         z, nz = self.z, self.nz
-        for k in range(nz - 1):
-            pl.when(z == 0)(lambda k=k: self.right(nz - 1 - k).start())
-            pl.when(z == nz - 1)(lambda k=k: self.left(k).start())
-
-    def relay(self, hops, k):
+        pl.when(z == 0)(lambda: self.right(nz - 1).start())
+        pl.when(z == nz - 1)(lambda: self.left(0).start())
+
+    def slot(self, k):
         z, nz = self.z, self.nz
-        if nz - 1 - k <= hops:
-            return
-
-        @pl.when(z == hops)
+        for hop in range(1, k + 1):
+            t = nz - 1 - (k - hop)
+            if t > hop:
+
+                @pl.when(z == hop)
+                def _(t=t):
+                    self.right(t).wait_recv()
+                    self.add(t, t)
+                    self.right(t).start()
+
+                @pl.when(z == nz - 1 - hop)
+                def _(u=nz - 1 - t):
+                    self.left(u).wait_recv()
+                    self.add(u, nz + u)
+                    self.left(u).start()
+
+        @pl.when(z == 0)
         def _():
-            t = nz - 1 - k
-            self.right(t).wait_recv()
-            self.add(t, t)
-            self.right(t).start()
-
-        @pl.when(z == nz - 1 - hops)
+            self.right(nz - k).wait_send()
+            self.right(nz - 1 - k).start()
+
+        @pl.when(z == nz - 1)
         def _():
-            self.left(k).wait_recv()
-            self.add(k, nz + k)
+            self.left(k - 1).wait_send()
             self.left(k).start()
 
     def arrive(self):
@@ -567,8 +577,14 @@
     def end(self):
         for t in range(self.nz):
             self.core(t).wait_send()
-            pl.when(self.z < t)(lambda t=t: self.right(t).wait_send())
-            pl.when(self.z > t)(lambda t=t: self.left(t).wait_send())
+            if t > 1:
+                pl.when((self.z < t) & (self.z > 0))(lambda t=t: self.right(t).wait_send())
+            else:
+                pl.when(self.z < t)(lambda t=t: self.right(t).wait_send())
+            if t < self.nz - 2:
+                pl.when((self.z > t) & (self.z < self.nz - 1))(lambda t=t: self.left(t).wait_send())
+            else:
+                pl.when(self.z > t)(lambda t=t: self.left(t).wait_send())
 
 
 class Square:
@@ -623,23 +639,24 @@
         self.s1, self.r1, self.s2, self.r2 = sems
         self.pieces = pieces
         self.rows = part.shape[1] // pieces
-        self.half = part.shape[2] // 2
-        self.halves = (slice(0, self.half), slice(self.half, 2 * self.half))
+        cut = (part.shape[2] // TILE + 1) // 2 * TILE
+        self.halves = (slice(0, cut), slice(cut, part.shape[2]))
+        self.widths = (cut, part.shape[2] - cut)
 
     def first(self, p, side, k):
         owner = ((self.dx, self.diag), (self.dy, self.diag))[side][k]
         at = pl.ds(p * self.rows, self.rows)
         slot = 2 * side + k
         return remote(
-            self.part.at[owner, at, self.halves[side]], self.once.at[slot, at, :],
+            self.part.at[owner, at, self.halves[side]], self.once.at[slot, at, : self.widths[side]],
             self.s1.at[p, slot], self.r1.at[p, slot], (self.x, self.y)[side],
         )
 
     def second(self, p, side):
         at = pl.ds(p * self.rows, self.rows)
         return remote(
-            self.gone.at[side, at, :], self.twice.at[side, at, :], self.s2.at[p, side], self.r2.at[p, side],
-            (self.y, self.x)[side],
+            self.gone.at[side, at, : self.widths[side]], self.twice.at[side, at, : self.widths[side]],
+            self.s2.at[p, side], self.r2.at[p, side], (self.y, self.x)[side],
         )
 
     def begin_x(self, p):
@@ -663,9 +680,9 @@
             owner = (self.dy, self.dx)[side]
 
             def body(at, side=side, owner=owner):
-                self.gone[side, at, :] = (
+                self.gone[side, at, : self.widths[side]] = (
                     self.part[owner, at, self.halves[side]].astype(F32)
-                    + self.once[2 * side + 1, at, :].astype(F32)
+                    + self.once[2 * side + 1, at, : self.widths[side]].astype(F32)
                 ).astype(BF16)
 
             self.each(p, body)
@@ -679,8 +696,8 @@
             def body(at, side=side):
                 out[at, self.halves[side]] = (
                     self.part[self.dp, at, self.halves[side]].astype(F32)
-                    + self.once[2 * side, at, :].astype(F32)
-                    + self.twice[side, at, :].astype(F32)
+                    + self.once[2 * side, at, : self.widths[side]].astype(F32)
+                    + self.twice[side, at, : self.widths[side]].astype(F32)
                 ).astype(out.dtype)
 
             self.each(p, body)
@@ -736,9 +753,9 @@
 
     def first_kernel(
         self, docs, starts, unit, x_ref, par_ref, head_ref, g_ref, wm_ref, wc_ref, wo_ref,
-        y_out, x_out, g_out, w_out, wc_out, dproj, dcom, normed_out, sums, heads, pre_bc, projc, taps, gain_out, st,
+        y_out, x_out, g_out, w_out, wc_out, dproj, dcom, normed_out, sums, heads, gain_out,
         xall, gall, wall, wcall, woall, parbuf, parall, every_par, projm, pre_sig, o, states, step_s, cum_s,
-        dg, scaled, sel, hp, chp, state, dnext, heard_st, ypart, ycame, ytotal, yheard,
+        dg, scaled, sel, hp, chp, state, dnext, heard_st, st, pre_bc, projc, taps, ypart, ycame, ytotal, yheard,
         pd_s, pd_r, pg_s, pg_r, wz_s, wz_r, cz_s, cz_r, wq_s, wq_r, cq_s, cq_r, oq_s, oq_r, cc_s, cc_r,
         xr_s, xr_r, xl_s, xl_r, xc_s, xc_r, gr_s, gr_r, gl_s, gl_r, gc_s, gc_r,
         st_s, st_r, yc_s, yc_r, yr_s, yr_r, yl_s, yl_r, loc,
@@ -942,7 +959,7 @@
                 for i in range(nd):
                     mine = scaled[pl.ds(pl.multiple_of(n * 256 + half * SPAN, SPAN), SPAN), tile_of(i)]
                     product = product + mine.astype(F32) * grad[half * SPAN : (half + 1) * SPAN, tile_of(i)]
-                st[2 * n + half, 1:2, :] = jnp.where(lanes_at == 0, lane_sum(product), 0.0).T[0:1, :]
+                st[1, pl.ds(2 * n + half, 1), :] = lane_sum(product).T[0:1, :]
             return 0
 
         lax.fori_loop(0, nm // 2, gate_grad, 0)
@@ -967,20 +984,15 @@
         def backward(n, _):
             self.backward_chunk(
                 nm - 1 - n, docs, starts, unit, projm, pre_sig, pre_bc, o, states, step_s, cum_s, dg, st, taps, sel,
-                hp, chp, dproj, dcom, normed_out, sums, heads, state, dnext,
+                hp, chp, dproj, dcom, normed_out, sums, heads, state, dnext, projc,
             )
-            pl.when(n == 1)(lambda: y_sum.relay(1, 0))
-
-            @pl.when(n == 4)
-            def _():
-                y_sum.relay(1, 1)
-                y_sum.relay(2, 0)
-
+            for k in range(1, nz - 1):
+                pl.when(n == SLOTS[k - 1])(lambda k=k: y_sum.slot(k))
             return 0
 
         lax.fori_loop(0, nm, backward, 0)
         y_sum.arrive()
-        stat = jnp.concatenate([st[me], jnp.zeros((SPAN - 8, TILE), F32)], axis=0).T
+        stat = jnp.broadcast_to(st[0, pl.ds(me, 1), :], (SPAN, TILE)).T
         root = lax.rsqrt(stat[:, 0:1] * unit[0, 0] + EPSILON)
         y_out[...] = (x_ref[...].astype(F32) + root * y_sum.own(slice(None))).astype(BF16)
         for copy in outs:
@@ -1063,11 +1075,11 @@
             gated = mixed * (gate_in * jax.nn.sigmoid(gate_in))
             squares = squares + gated * gated
             scaled[here, lanes] = (gated * chp[2:3, lanes]).astype(BF16)
-        st[chunk, 0:1, :] = jnp.where(lane == 0, lane_sum(squares), 0.0).T[0:1, :]
+        st[0, pl.ds(chunk, 1), :] = lane_sum(squares).T[0:1, :]
 
     def backward_chunk(
         self, chunk, docs, starts, unit, projm, pre_sig, pre_bc, o, states, step_s, cum_s, dg, st, taps, sel,
-        hp, chp, dproj, dcom, normed_out, sums, heads, dstate, dnext,
+        hp, chp, dproj, dcom, normed_out, sums, heads, dstate, dnext, projc,
     ):
         nd = self.nd
         first = chunk * SPAN
@@ -1090,8 +1102,8 @@
         meet = dot(query_side, key_side, ((1,), (1,)))
         step, cum = step_s[here, :], cum_s[here, :]
         cum_t = cum.T
-        stat = jnp.concatenate([st[chunk], jnp.zeros((SPAN - 8, TILE), F32)], axis=0).T
-        square, cross = head_col(stat, 0), head_col(stat, 1)
+        square = jnp.broadcast_to(st[0, pl.ds(chunk, 1), :], (SPAN, TILE)).T
+        cross = jnp.broadcast_to(st[1, pl.ds(chunk, 1), :], (SPAN, TILE)).T
         root = lax.rsqrt(square * unit[0, 0] + EPSILON)
         pull = root * root * root * cross * unit[0, 0]
         before = states[chunk]
@@ -1110,6 +1122,21 @@
         next_begin = begin_at(next_rows, starts, docs)
         valid = [next_rows - (KW - 1 - tap) >= next_begin for tap in range(KW)]
         tail_row = row == SPAN - 1
+
+        def conv_back(pre_grad, ext, lanes):
+            sums[2:3, lanes] += jnp.sum(pre_grad, axis=0, keepdims=True)
+            later = jnp.concatenate([pre_grad, dnext[:, lanes]], axis=0)
+            dnext[:, lanes] = pre_grad[0:PAD, :]
+            back_grad = jnp.zeros((SPAN, TILE), F32)
+            for tap in range(KW):
+                back = KW - 1 - tap
+                masked = jnp.where(valid[tap], later, 0.0)
+                moved = ext if back == 0 else pltpu.roll(ext, back, 0)
+                sums[4 + tap : 5 + tap, lanes] += jnp.sum(masked[:SPAN] * moved[PAD:], axis=0, keepdims=True)
+                ahead = masked if back == 0 else pltpu.roll(masked, SPAN + PAD - back, 0)
+                back_grad = back_grad + ahead[:SPAN] * taps[tap : tap + 1, lanes]
+            return back_grad
+
         for i in range(nd):
             lanes = tile_of(i)
             pre = pre_sig[here, lanes]
@@ -1175,28 +1202,17 @@
             dstate[:, lanes] = end * after[:, lanes] + dot(query_side, entry_grad.astype(BF16), ((0,), (0,)))
             signal_grad = stepx * fed_grad + chp[0:1, lanes] * mixed_grad
             pre_grad = signal_grad * (gate_of * (1.0 + pre * (1.0 - gate_of)))
-            sums[2:3, lanes] += jnp.sum(pre_grad, axis=0, keepdims=True)
-            later = jnp.concatenate([pre_grad, dnext[:, lanes]], axis=0)
-            dnext[:, lanes] = pre_grad[0:PAD, :]
             cols = tile_of(nd + i)
-            ext = projm[lead, cols].astype(F32)
-            back_grad = jnp.zeros((SPAN, TILE), F32)
-            for tap in range(KW):
-                back = KW - 1 - tap
-                masked = jnp.where(valid[tap], later, 0.0)
-                moved = ext if back == 0 else pltpu.roll(ext, back, 0)
-                sums[4 + tap : 5 + tap, lanes] += jnp.sum(masked[:SPAN] * moved[PAD:], axis=0, keepdims=True)
-                ahead = masked if back == 0 else pltpu.roll(masked, SPAN + PAD - back, 0)
-                back_grad = back_grad + ahead[:SPAN] * taps[tap : tap + 1, lanes]
-            dproj[here, cols] = back_grad.astype(BF16)
+            dproj[here, cols] = conv_back(pre_grad, projm[lead, cols].astype(F32), lanes).astype(BF16)
         meet_low = meet_grad.astype(BF16)
         state_rows = ((1,), (1,))
         query_grad = dot(meet_low, key_side) + dot(jnp.concatenate(entered, axis=1), before_low, state_rows)
         key_grad = dot(meet_low, query_side, ((0,), (0,))) + dot(
             jnp.concatenate(tails, axis=1), after_low, state_rows
         )
-        dcom[here, :TILE] = key_grad.astype(BF16)
-        dcom[here, TILE : 2 * TILE] = query_grad.astype(BF16)
+        for i, (side_grad, side_pre) in enumerate(((key_grad, key_pre), (query_grad, query_pre))):
+            back_grad = conv_back(side_grad * silu_slope(side_pre), projc[lead, tile_of(i)].astype(F32), tile_of(nd + i))
+            dcom[here, tile_of(i)] = back_grad.astype(BF16)
         rows_t = jnp.concatenate([cum_rows, jnp.zeros((SPAN - 8, SPAN), F32)], axis=0).T
         decay_grad = exact(lower, cum_cols - rows_t, ((0,), (0,)))
         log_decay = step * hp[1:2, :]
@@ -1221,16 +1237,12 @@
                 like((span, 2 * wide), BF16),
                 like((span, COMMON), BF16),
                 like((span, wide), BF16),
-                like((8, wide), F32),
+                like((8, wide + 2 * TILE), F32),
                 like((8, TILE), F32),
-                like((span, 2 * TILE), F32),
-                like((PAD + span, COMMON), BF16),
-                like((8, wide + 2 * TILE), F32),
                 like((8, MODEL), F32),
-                like((nm, 8, TILE), F32),
             ],
             in_specs=[SM, SM, VM, VM, VM, ANY, ANY, ANY, ANY],
-            out_specs=[VM, ANY, ANY, ANY, ANY] + [VM] * 10,
+            out_specs=[VM, ANY, ANY, ANY, ANY] + [VM] * 6,
             scratch_shapes=[
                 pltpu.VMEM((span, MODEL), BF16),
                 pltpu.VMEM((span, MODEL), BF16),
@@ -1252,8 +1264,12 @@
                 pltpu.VMEM((8, TILE), F32),
                 pltpu.VMEM((8, wide), F32),
                 pltpu.VMEM((STATE, wide), F32),
-                pltpu.VMEM((PAD, wide), F32),
-                pltpu.VMEM((nm - 1, nm, 8, TILE), F32),
+                pltpu.VMEM((PAD, wide + 2 * TILE), F32),
+                pltpu.VMEM((nm - 1, 2, nm, TILE), F32),
+                pltpu.VMEM((2, nm, TILE), F32),
+                pltpu.VMEM((span, 2 * TILE), F32),
+                pltpu.VMEM((PAD + span, COMMON), BF16),
+                pltpu.VMEM((8, wide + 2 * TILE), F32),
                 pltpu.VMEM((nm, *block), BF16),
                 pltpu.VMEM((nz, *block), BF16),
                 pltpu.VMEM((nz, *block), BF16),
@@ -1275,14 +1291,13 @@
         )(starts, unit, x, par, heads, g, wm, wc, wo)
 
     def second_kernel(
-        self, docs, starts, dproj, dcom, normed_out, sums, heads, pre_bc, projc, taps, gain, x_ref, g_ref,
-        x_in, g_in, w_in, wc_in,
+        self, dproj, dcom, normed_out, sums, heads, gain, x_ref, g_ref, x_in, g_in, w_in, wc_in,
         dx_out, dw_out, dwc_out, dwo_out, par_out,
         xall, gall, wall, wcall, xpart, xcame, xtotal, xheard,
-        padded, ccame, ctotal, cheard, every, dxc, x_rows, wcpart, wccame,
+        cpart, ccame, csum, c1, c2, cgo, crows, cheard,
         wpart, w1, w2, wgo, wsum, opart, o1, o2, ogo, pard, parbuf,
-        xc_s, xc_r, xr_s, xr_r, xl_s, xl_r, cc_s, cc_r, cz_s, cz_r, ez_s, ez_r, ec_s, ec_r,
-        w1_s, w1_r, w2_s, w2_r, o1_s, o1_r, o2_s, o2_r, wz_s, wz_r, wcd_s, wcd_r, pd_s, pd_r, pg_s, pg_r, loc,
+        xc_s, xc_r, xr_s, xr_r, xl_s, xl_r, cc_s, cc_r, c1_s, c1_r, c2_s, c2_r, cz_s, cz_r,
+        w1_s, w1_r, w2_s, w2_r, o1_s, o1_r, o2_s, o2_r, wz_s, wz_r, pd_s, pd_r, pg_s, pg_r, loc,
     ):
         nd, nc, nz, nm = self.nd, self.nc, self.nz, self.nm
         rows, wide, span = self.rows_in, self.wide, self.span
@@ -1291,7 +1306,7 @@
         sizes = (nc, nz)
         steps = self.group_steps()
         other = (dp, nc - 1 - c, z)
-        long = SPAN + PAD
+        lines = [(k, (lax.rem(dp + k, nd), c, z), lax.rem(dp + k, nd)) for k in range(1, nd)]
         started = []
 
         def go(copy):
@@ -1301,93 +1316,42 @@
 
         loads = [
             pltpu.make_async_copy(w_in, wall, loc.at[0]),
-            pltpu.make_async_copy(x_in, xall, loc.at[1]),
-            pltpu.make_async_copy(wc_in, wcall, loc.at[2]),
+            pltpu.make_async_copy(wc_in, wcall, loc.at[1]),
+            pltpu.make_async_copy(x_in, xall, loc.at[2]),
             pltpu.make_async_copy(g_in, gall, loc.at[3]),
         ]
         for load in loads:
             load.start()
-        padded[0:span, :] = dcom[...]
-        padded[span:, :] = jnp.zeros((PAD, COMMON), BF16)
         self.barrier()
         x_sum = Sum(where, sizes, xpart, xcame, xtotal, xheard, (xc_s, xc_r, xr_s, xr_r, xl_s, xl_r))
         w_sum = SquareSum(where, wpart, w1, w2, wgo, (w1_s, w1_r, w2_s, w2_r), 2)
         o_sum = SquareSum(where, opart, o1, o2, ogo, (o1_s, o1_r, o2_s, o2_r), 1)
-
-        def c_rows(m):
-            return pl.ds(pl.multiple_of(m * SPAN, SPAN), long)
-
-        ccopies = [
-            go(remote(padded.at[c_rows((nc - 1 - c) * nz + t), :], ccame.at[t], cc_s.at[t], cc_r.at[t], other))
-            for t in range(nz)
-        ]
+        c_sum = SquareSum(where, csum, c1, c2, cgo, (c1_s, c1_r, c2_s, c2_r), 1)
         loads[0].wait()
-
-        def input_grad(n, _):
-            at = rows_of(n, 256)
-            base = rows_of(nc - 1 - c, nz * SPAN)
-            part = dot(dproj[base, :], wall[at, :], ((1,), (1,))).astype(BF16)
-            for t in range(nz):
-                xpart[(nc - 1 - c) * nz + t, :, at] = part[t * SPAN : (t + 1) * SPAN, :]
-            return 0
-
-        lax.fori_loop(0, MODEL // 256, input_grad, 0)
+        loads[1].wait()
+
+        def input_grad(core):
+            base = rows_of(core, nz * SPAN)
+
+            def piece(n, _):
+                at = rows_of(n, 256)
+                part = dot(dproj[base, :], wall[at, :], ((1,), (1,)))
+                part = (part + dot(dcom[base, :], wcall[at, :], ((1,), (1,)))).astype(BF16)
+                for t in range(nz):
+                    xpart[core * nz + t, :, at] = part[t * SPAN : (t + 1) * SPAN, :]
+                return 0
+
+            lax.fori_loop(0, MODEL // 256, piece, 0)
+
+        input_grad(nc - 1 - c)
         for t in range(nz):
             x_sum.core(t).start()
-        for t in range(nz):
-            ccopies[t].wait_recv()
-            ctotal[t] = (padded[c_rows(c * nz + t), :].astype(F32) + ccame[t].astype(F32)).astype(BF16)
-        for d in range(1, nz):
-            to = lax.rem(z + d, nz)
-            go(remote(ctotal.at[to], cheard.at[d - 1], cz_s.at[d], cz_r.at[d], (dp, c, to)))
-
-        def own_grad(n, _):
-            at = rows_of(n, 256)
-            base = rows_of(c, nz * SPAN)
-            part = dot(dproj[base, :], wall[at, :], ((1,), (1,))).astype(BF16)
-            for t in range(nz):
-                xpart[c * nz + t, :, at] = part[t * SPAN : (t + 1) * SPAN, :]
-            return 0
-
-        lax.fori_loop(0, MODEL // 256, own_grad, 0)
+        input_grad(c)
         for t in range(nz):
             x_sum.add_core(t)
         x_sum.begin()
 
-        total = ctotal[z].astype(F32)
-        for d in range(1, nz):
-            remote(cheard.at[d - 1], cheard.at[d - 1], cz_s.at[d], cz_r.at[d], other).wait_recv()
-            total = total + cheard[d - 1].astype(F32)
-        base = pl.multiple_of(me * SPAN, SPAN)
-        after = pl.multiple_of(lax.rem(me + 1, nm) * SPAN, SPAN)
-        places = base + iota((long, TILE), 0)
-        begin = begin_at(places, starts, docs)
-        inside = places < span
-        counts = MODEL // TILE + 8 * nd
-        parbuf[counts : counts + 16, :] = jnp.zeros((16, TILE), F32)
-        for i in range(2):
-            lanes = tile_of(i)
-            pre = jnp.concatenate([pre_bc[pl.ds(base, SPAN), lanes], pre_bc[pl.ds(after, PAD), lanes]], axis=0)
-            later = jnp.where(inside, total[:, lanes] * silu_slope(pre), 0.0)
-            ext = projc[pl.ds(base, long), lanes].astype(F32)
-            parbuf[counts + i : counts + i + 1, :] = jnp.sum(later[:SPAN], axis=0, keepdims=True)
-            back_grad = jnp.zeros((SPAN, TILE), F32)
-            for tap in range(KW):
-                back = KW - 1 - tap
-                masked = jnp.where(places - back >= begin, later, 0.0)
-                moved = ext if back == 0 else pltpu.roll(ext, back, 0)
-                at = counts + 2 + 2 * tap + i
-                parbuf[at : at + 1, :] = jnp.sum(masked[:SPAN] * moved[PAD:], axis=0, keepdims=True)
-                ahead = masked if back == 0 else pltpu.roll(masked, long - back, 0)
-                back_grad = back_grad + ahead[:SPAN] * taps[tap : tap + 1, tile_of(nd + i)]
-            every[me, :, lanes] = back_grad.astype(BF16)
-        every[me, :, 2 * TILE :] = total[:SPAN, 2 * TILE :].astype(BF16)
-        mine = every.at[me]
-        for d in range(1, nz):
-            go(remote(mine, mine, ez_s.at[d], ez_r.at[d], (dp, c, lax.rem(z + d, nz))))
-        go(remote(mine, mine, ec_s.at[0], ec_r.at[0], other))
-
-        loads[1].wait()
+        loads[2].wait()
 
         def weight_grad(owner):
             def piece(n, _):
@@ -1404,10 +1368,18 @@
         weight_grad(w_sum.dy)
         for p in range(2):
             w_sum.begin_y(p)
-        x_sum.relay(1, 0)
         weight_grad(dp)
-        loads[2].wait()
-        dxc[...] = dot(every[me], wcall[...], ((1,), (1,)))
+
+        def shared_grad(n, _):
+            at = rows_of(n, 256)
+            cpart[n] = dot(xall[:, at], dcom[...], ((0,), (0,))).astype(BF16)
+            return 0
+
+        lax.fori_loop(0, nd * nc, shared_grad, 0)
+        ccopies = [
+            go(remote(cpart.at[i * nc + nc - 1 - c], ccame.at[i], cc_s.at[i], cc_r.at[i], other)) for i in range(nd)
+        ]
+        x_sum.slot(1)
         loads[3].wait()
 
         def out_grad(n, _):
@@ -1418,31 +1390,15 @@
             return 0
 
         lax.fori_loop(0, MODEL // 512, out_grad, 0)
+        for i in range(nd):
+            ccopies[i].wait_recv()
+            csum[i] = (cpart[i * nc + c].astype(F32) + ccame[i].astype(F32)).astype(BF16)
+        c_sum.begin_x(0)
+        c_sum.begin_y(0)
         o_sum.begin_x(0)
         o_sum.begin_y(0)
-        for d in range(1, nz):
-            block = every.at[c * nz + lax.rem(z + nz - d, nz)]
-            remote(block, block, ez_s.at[d], ez_r.at[d], other).wait_recv()
-            go(remote(block, block, ec_s.at[d], ec_r.at[d], other))
         w_sum.pass_on(0)
-        x_sum.relay(1, 1)
-        x_sum.relay(2, 0)
-        for i in range(nd):
-            pair = pl.ds(pl.multiple_of(i * (nm * rows) + (me // 2) * (2 * rows), 2 * rows), 2 * rows)
-            both = xall[:, pair]
-            x_rows[:, i * rows : (i + 1) * rows] = jnp.where(
-                lax.rem(me, 2) == 0, both[:, :rows].astype(F32), both[:, rows:].astype(F32)
-            ).astype(BF16)
-        for d in range(nz):
-            block = every.at[(nc - 1 - c) * nz + lax.rem(z + nz - d, nz)]
-            remote(block, block, ec_s.at[d], ec_r.at[d], other).wait_recv()
-        shared = dot(x_rows[...], every[...].reshape(span, COMMON), ((0,), (0,))).astype(BF16)
-        for i in range(nd):
-            wcpart[i] = shared[i * rows : (i + 1) * rows, :]
-        lines = [(k, (lax.rem(dp + k, nd), c, z), lax.rem(dp + k, nd)) for k in range(1, nd)]
-        wc_copies = [
-            go(remote(wcpart.at[to], wccame.at[k - 1], wcd_s.at[k], wcd_r.at[k], device)) for k, device, to in lines
-        ]
+        x_sum.slot(2)
         w_sum.pass_on(1)
 
         def send_rows(p):
@@ -1462,11 +1418,12 @@
 
         w_sum.finish(0, wsum)
         send_rows(0)
+        c_sum.pass_on(0)
         o_sum.pass_on(0)
 
         x_sum.arrive()
         hidden = x_ref[...].astype(F32)
-        normed_grad = x_sum.own(slice(None)) + dxc[...]
+        normed_grad = x_sum.own(slice(None))
         inverse = lax.rsqrt(jnp.mean(hidden * hidden, axis=1, keepdims=True) + EPSILON)
         unitary = hidden * inverse
         gain_grad = jnp.sum(normed_grad * unitary, axis=0, keepdims=True)
@@ -1476,15 +1433,21 @@
         base_row = MODEL // TILE
         for i in range(base_row):
             parbuf[i : i + 1, :] = gain_grad[:, tile_of(i)]
+        count = nd + 2
         for r in range(8):
-            for i in range(nd):
-                parbuf[base_row + r * nd + i : base_row + r * nd + i + 1, :] = sums[r : r + 1, tile_of(i)]
-        parbuf[counts + 16 :, :] = heads[...]
+            for i in range(count):
+                at = base_row + r * count + i
+                parbuf[at : at + 1, :] = sums[r : r + 1, tile_of(i)]
+        parbuf[base_row + 8 * count :, :] = heads[...]
         small = [
             go(remote(parbuf, pard.at[k - 1], pd_s.at[k], pd_r.at[k], device)) for k, device, _ in lines
         ]
         w_sum.finish(1, wsum)
         send_rows(1)
+        c_sum.finish(0, crows)
+        for d in range(1, nz):
+            to = lax.rem(z + d, nz)
+            go(remote(crows.at[rows_of(to, rows), :], cheard.at[d - 1], cz_s.at[d], cz_r.at[d], (dp, c, to)))
         for copy in small:
             copy.wait_recv()
         total = parbuf[...]
@@ -1494,11 +1457,10 @@
         for j, step in enumerate(steps):
             go(remote(par_out.at[me], par_out.at[me], pg_s.at[j], pg_r.at[j], self.target(step)[0]))
         o_sum.finish(0, dwo_out)
-        for copy in wc_copies:
-            copy.wait_recv()
-        total = wcpart[dp].astype(F32)
-        for k in range(nd - 1):
-            total = total + wccame[k].astype(F32)
+        total = crows[rows_of(z, rows), :].astype(F32)
+        for d in range(1, nz):
+            remote(cheard.at[d - 1], cheard.at[d - 1], cz_s.at[d], cz_r.at[d], other).wait_recv()
+            total = total + cheard[d - 1].astype(F32)
         dwc_out[...] = total
         for j, step in enumerate(steps):
             here = par_out.at[self.source(step)]
@@ -1516,15 +1478,15 @@
         x_sum.end()
         w_sum.end()
         o_sum.end()
-
-    def second(self, docs, starts, dproj, dcom, normed_out, sums, heads, pre_bc, projc, taps, gain, x, g, xall, gall, w, wc):
-        nd, nz, nm, rows, span, wide = self.nd, self.nz, self.nm, self.rows_in, self.span, self.wide
+        c_sum.end()
+
+    def second(self, dproj, dcom, normed_out, sums, heads, gain, x, g, xall, gall, w, wc):
+        nd, nc, nz, nm, rows, span, wide = self.nd, self.nc, self.nz, self.nm, self.rows_in, self.span, self.wide
         like = jax.ShapeDtypeStruct
         block = (SPAN, MODEL)
-        npar = MODEL // TILE + 8 * nd + 16 + 8
-        long = SPAN + PAD
+        npar = MODEL // TILE + 8 * (nd + 2) + 8
         return pl.pallas_call(
-            functools.partial(self.second_kernel, docs),
+            self.second_kernel,
             out_shape=[
                 like(block, BF16),
                 like((nm, rows, 2 * wide), BF16),
@@ -1532,7 +1494,7 @@
                 like((TILE, MODEL), F32),
                 like((nm, npar, TILE), F32),
             ],
-            in_specs=[SM] + [VM] * 11 + [ANY] * 4,
+            in_specs=[VM] * 8 + [ANY] * 4,
             out_specs=[VM] * 5,
             scratch_shapes=[
                 pltpu.VMEM((span, MODEL), BF16),
@@ -1543,15 +1505,14 @@
                 pltpu.VMEM((nz, *block), BF16),
                 pltpu.VMEM((nz, *block), BF16),
                 pltpu.VMEM((2 * nz, *block), BF16),
-                pltpu.VMEM((span + PAD, COMMON), BF16),
-                pltpu.VMEM((nz, long, COMMON), BF16),
-                pltpu.VMEM((nz, long, COMMON), BF16),
-                pltpu.VMEM((nz - 1, long, COMMON), BF16),
-                pltpu.VMEM((nm, SPAN, COMMON), BF16),
-                pltpu.VMEM(block, F32),
-                pltpu.VMEM((span, nd * rows), BF16),
-                pltpu.VMEM((nd, rows, COMMON), BF16),
-                pltpu.VMEM((nd - 1, rows, COMMON), BF16),
+                pltpu.VMEM((nd * nc, nz * rows, COMMON), BF16),
+                pltpu.VMEM((nd, nz * rows, COMMON), BF16),
+                pltpu.VMEM((nd, nz * rows, COMMON), BF16),
+                pltpu.VMEM((4, nz * rows, 2 * TILE), BF16),
+                pltpu.VMEM((2, nz * rows, 2 * TILE), BF16),
+                pltpu.VMEM((2, nz * rows, 2 * TILE), BF16),
+                pltpu.VMEM((nz * rows, COMMON), BF16),
+                pltpu.VMEM((nz - 1, rows, COMMON), BF16),
                 pltpu.VMEM((nd, nm * rows, 2 * wide), BF16),
                 pltpu.VMEM((4, nm * rows, wide), BF16),
                 pltpu.VMEM((2, nm * rows, wide), BF16),
@@ -1564,17 +1525,17 @@
                 pltpu.VMEM((nd - 1, npar, TILE), F32),
                 pltpu.VMEM((npar, TILE), F32),
                 DMA((nz,)), DMA((nz,)), DMA((nz,)), DMA((nz,)), DMA((nz,)), DMA((nz,)),
-                DMA((nz,)), DMA((nz,)), DMA((nz,)), DMA((nz,)), DMA((nz,)), DMA((nz,)), DMA((nz,)), DMA((nz,)),
+                DMA((nd,)), DMA((nd,)), DMA((1, 4)), DMA((1, 4)), DMA((1, 2)), DMA((1, 2)), DMA((nz,)), DMA((nz,)),
                 DMA((2, 4)), DMA((2, 4)), DMA((2, 2)), DMA((2, 2)),
                 DMA((1, 4)), DMA((1, 4)), DMA((1, 2)), DMA((1, 2)),
-                DMA((nm,)), DMA((nm,)), DMA((nd,)), DMA((nd,)), DMA((nd,)), DMA((nd,)),
+                DMA((nm,)), DMA((nm,)), DMA((nd,)), DMA((nd,)),
                 DMA((nm,)), DMA((nm,)), DMA((4,)),
             ],
             compiler_params=pltpu.CompilerParams(
                 collective_id=1, has_side_effects=True, vmem_limit_bytes=62 * 2**20
             ),
             name="second",
-        )(starts, dproj, dcom, normed_out, sums, heads, pre_bc, projc, taps, gain, x, g, xall, gall, w, wc)
+        )(dproj, dcom, normed_out, sums, heads, gain, x, g, xall, gall, w, wc)
 
     def local(
         self, layer_input, out_grad, norm_gain, in_weight, conv_weight, conv_bias, step_bias, log_rate,
@@ -1609,11 +1570,11 @@
         mask = (jnp.arange(HEADS) < active).astype(F32)
         head_in = jnp.stack([step_bias, -jnp.exp(log_rate), skip_gain, mask])
         head_in = jnp.pad(head_in, ((0, 4), (0, TILE - HEADS)))
-        (
-            y_out, xall, gall, w, wc_all, dproj, dcom, normed_out, sums, heads, pre_bc, projc, taps, gain, _,
-        ) = self.first(docs, starts, unit, x, par, head_in, g, wm, wc, out_weight)
+        y_out, xall, gall, w, wc_all, dproj, dcom, normed_out, sums, heads, gain = self.first(
+            docs, starts, unit, x, par, head_in, g, wm, wc, out_weight
+        )
         dx_out, dw, dwc, dwo, pars = self.second(
-            docs, starts, dproj, dcom, normed_out, sums, heads, pre_bc, projc, taps, gain, x, g, xall, gall, w, wc_all
+            dproj, dcom, normed_out, sums, heads, gain, x, g, xall, gall, w, wc_all
         )
         dw = jnp.transpose(dw.reshape(nm, rows, 2 * nd, TILE), (1, 2, 0, 3)).reshape(rows, 2 * INNER)
         in_weight_grad = jnp.concatenate([dw.astype(F32), dwc[:, : EXTENT - 2 * INNER]], axis=1)
@@ -1621,14 +1582,15 @@
         gains = jnp.sum(pars[:, : MODEL // TILE], axis=0).reshape(MODEL)
         norm_gain_grad = lax.dynamic_slice_in_dim(gains, owner * rows, rows)
         base = MODEL // TILE
-        mains = pars[:, base : base + 8 * nd].reshape(nm, 8, nd, TILE)
-        shared = jnp.sum(pars[:, base + 8 * nd : base + 8 * nd + 16], axis=0)
-        head_sums = pars[:, base + 8 * nd + 16 :]
+        per_row = pars[:, base : base + 8 * (nd + 2)].reshape(nm, 8, nd + 2, TILE)
+        mains = per_row[:, :, :nd]
+        shared = jnp.sum(per_row[:, :, nd:], axis=0).reshape(8, 2 * TILE)
+        head_sums = pars[:, base + 8 * (nd + 2) :]
         gate_gain_grad = lax.dynamic_index_in_dim(mains[me, 0], dp, 0, keepdims=False)
         everything = jnp.transpose(mains[:, 1:], (1, 2, 0, 3)).reshape(7, INNER)
         skip_gain_grad = jnp.sum(everything[0].reshape(HEADS, HEAD_DIM), axis=1)
-        bias_sum = jnp.concatenate([everything[1], shared[:2].reshape(-1)])
-        taps_sum = jnp.concatenate([everything[3:], shared[2:10].reshape(KW, 2 * TILE)], axis=1).T
+        bias_sum = jnp.concatenate([everything[1], shared[2]])
+        taps_sum = jnp.concatenate([everything[3:], shared[4:]], axis=1).T
         conv_bias_grad = lax.dynamic_slice_in_dim(bias_sum, owner * own_conv, own_conv)
         conv_weight_grad = lax.dynamic_slice_in_dim(taps_sum, owner * own_conv, own_conv)
         mine = nd * self.per

time: 329 us -> 300 us (0.912)
  Pallas kernels: 301 us -> 274 us
    pallas_call x1, Pallas kernels: 199 us -> 173 us  [first(): pl.pallas_call(functools.partial(self.first_kernel, docs), out_shape=[lik...]
    unnamed x18 -> x21, local copies, waits for them, and re-layouts: 6.87 us -> 6.87 us
where the time goes in v3:
time: 300 us; the launch traced here: 299 us
  Pallas kernels  274 us (91%)
  local copies, waits for them, and re-layouts  16.5 us (6%)
  other arithmetic  7.53 us (3%)
    pallas_call x1, Pallas kernels, first(): pl.pallas_call(functools.partial(self.first_kernel, docs), out_shape=[lik...  173 us
    pallas_call x1, Pallas kernels, second(): pl.pallas_call(self.second_kernel, out_shape=[like(block, BF16), like((nm...  100 us
    unnamed x21, local copies, waits for them, and re-layouts  6.87 us

profile of v3, /device:TPU:0, one launch (start us, length us, event | category | flops | bytes accessed | tf_op | source)
XLA Modules:
  0.0 299.3 jit_solution(8033203917510160324)
XLA Ops:
  0.6 1.2 select_reduce_fusion
  2.6 0.7 pad.24
  3.3 0.7 pad.25
  4.0 0.7 pad.26
  4.6 0.7 pad.27
  5.3 0.6 concatenate.12.par_ref
  5.9 0.7 negate_bitcast_fusion
  6.6 1.3 select_maximum_fusion.head_ref
  7.8 1.3 slice_bitcast_fusion
  9.1 0.3 copy.45
  9.4 0.0 slice-start
  9.4 0.1 copy.55
  9.6 1.3 reshape.98.wm_ref
  10.9 0.0 slice-done
  10.9 0.6 pad.29.wc_ref
  11.5 173.5 %first.1 = (bf16[128,2048]{1,0:T(8,128)(2,1)}, bf16[1024,2048]{1,0:T(8,128)(2,1)}, bf16[1024,2048]{1,0:T(8,128)(2,1)}, bf16[2048,1024]{1,0:T(8,128)(2,1)}, bf16[...) custom-call(s32[1,4]{1,0:T(1,128)} %bitcast.100, ...), custom_call_target="tpu_custom_call" | custom-call | tf_op jit(solution)/shard_map/first/pallas_call | solution.py:1229
  184.9 100.4 %second.1 = (bf16[128,2048]{1,0:T(8,128)(2,1)}, bf16[8,64,1024]{2,1,0:T(8,128)(2,1)}, f32[64,384]{1,0:T(8,128)}, f32[128,2048]{1,0:T(8,128)}, f32[8,72,128]{2,1,0:T(8,128)}) custom-call(bf16[1024,1024]{1,0:T(8,128)(2,1)} %get-tuple-element.28.dproj, bf16[1024,384]{1,0:T(8,128)(2,1)} %get-tuple-element.29.dcom, ...), custom_call_target="tpu_custom_call" | custom-call | tf_op jit(solution)/shard_map/second/pallas_call | solution.py:1488
  285.3 0.9 slice_reduce_fusion.1
  286.2 0.6 dynamic_slice.14
  286.8 1.5 copy.46
  288.3 0.1 bitcast_bitcast_fusion
  288.4 1.2 copy.39
  289.6 0.0 copy-start.4
  289.6 1.2 copy.54
  290.8 0.0 copy-done.4
  290.9 0.0 copy-start.3
  290.9 1.5 pad_maximum_fusion
  292.4 0.0 copy-start.1
  292.4 0.0 copy-start.2
  292.4 0.0 copy-start
  292.4 0.0 copy-done.3
  292.4 0.1 copy.40
  292.6 0.7 fusion.1
  293.3 0.6 fusion.2
  294.0 0.1 copy.41
  294.0 0.1 copy.42
  294.1 0.6 reshape.104
  294.7 0.1 copy.43
  294.8 0.1 copy.44
  294.9 0.6 reshape.106
  295.5 0.1 reshape_squeeze.3
  295.6 0.6 reduce_sum.39
  296.3 0.5 fusion.3
  296.8 0.0 copy-done.1
  296.8 0.8 copy.62
  297.6 0.0 copy-done.2
  297.6 0.8 copy.63
  298.4 0.0 copy-done
  298.4 1.0 copy.64
  (13 shorter events, 0.1 us)
Async XLA Ops:
  9.4 1.4 slice-start
  289.6 1.2 copy-start.4
  290.9 1.5 copy-start.3
  292.4 4.4 %copy-start.1 = (bf16[128,2048]{1,0:T(8,128)(2,1)S(1)}, bf16[128,2048]{1,0:T(8,128)(2,1)}, u32[]{:S(2)}) copy-start(bf16[128,2048]{1,0:T(8,128)(2,1)} %get-tuple-element.27) | copy-start | bytes 1572868
  292.4 5.2 %copy-start.2 = (bf16[128,2048]{1,0:T(8,128)(2,1)S(1)}, bf16[128,2048]{1,0:T(8,128)(2,1)}, u32[]{:S(2)}) copy-start(bf16[128,2048]{1,0:T(8,128)(2,1)} %get-tuple-element.38) | copy-start | bytes 1572868
  292.4 6.0 %copy-start = (f32[128,2048]{1,0:T(8,128)S(1)}, f32[128,2048]{1,0:T(8,128)}, u32[]{:S(2)}) copy-start(f32[128,2048]{1,0:T(8,128)} %get-tuple-element.68) | copy-start | bytes 3145732

commit v4 on v3

--- a/solution.py
+++ b/solution.py
@@ -379,7 +379,7 @@
 def begin_at(place, starts, docs):
     begin = jnp.zeros_like(place)
     for doc in range(1, docs):
-        begin = jnp.where(starts[0, doc] <= place, starts[0, doc], begin)
+        begin = jnp.where(starts[doc] <= place, starts[doc], begin)
     return begin
 
 
@@ -501,9 +501,10 @@
         to = (self.dp, self.c, lax.rem(self.z + 1, self.nz))
         return remote(self.total.at[t], self.heard.at[t], self.right_s.at[t], self.right_r.at[t], to)
 
-    def left(self, t):
+    def left(self, t, stops):
+        slot = self.nz if stops else t
         to = (self.dp, self.c, lax.rem(self.z + self.nz - 1, self.nz))
-        return remote(self.total.at[t], self.heard.at[self.nz + t], self.left_s.at[t], self.left_r.at[t], to)
+        return remote(self.total.at[t], self.heard.at[slot], self.left_s.at[t], self.left_r.at[t], to)
 
     def add_core(self, t):
         self.core(t).wait_recv()
@@ -530,7 +531,7 @@
     def begin(self):
         z, nz = self.z, self.nz
         pl.when(z == 0)(lambda: self.right(nz - 1).start())
-        pl.when(z == nz - 1)(lambda: self.left(0).start())
+        pl.when(z == nz - 1)(lambda: self.left(0, nz == 2).start())
 
     def slot(self, k):
         z, nz = self.z, self.nz
@@ -545,10 +546,10 @@
                     self.right(t).start()
 
                 @pl.when(z == nz - 1 - hop)
-                def _(u=nz - 1 - t):
-                    self.left(u).wait_recv()
-                    self.add(u, nz + u)
-                    self.left(u).start()
+                def _(u=nz - 1 - t, hop=hop):
+                    self.left(u, False).wait_recv()
+                    self.add(u, u)
+                    self.left(u, u == nz - 2 - hop).start()
 
         @pl.when(z == 0)
         def _():
@@ -557,34 +558,34 @@
 
         @pl.when(z == nz - 1)
         def _():
-            self.left(k - 1).wait_send()
-            self.left(k).start()
+            self.left(k - 1, False).wait_send()
+            self.left(k, k == nz - 2).start()
 
     def arrive(self):
         z, nz = self.z, self.nz
         for t in range(nz):
             pl.when((z == t) & (z > 0))(lambda t=t: self.right(t).wait_recv())
-            pl.when((z == t) & (z < nz - 1))(lambda t=t: self.left(t).wait_recv())
+            pl.when((z == t) & (z < nz - 1))(lambda t=t: self.left(t, True).wait_recv())
 
     def own(self, rows):
         z, nz = self.z, self.nz
         value = self.total[z, rows, :].astype(F32)
         left = self.heard[z, rows, :].astype(F32)
-        right = self.heard[nz + z, rows, :].astype(F32)
+        right = self.heard[nz, rows, :].astype(F32)
         value = value + jnp.where(z > 0, left, 0.0)
         return value + jnp.where(z < nz - 1, right, 0.0)
 
-    def end(self):
+    def end_core(self):
         for t in range(self.nz):
             self.core(t).wait_send()
-            if t > 1:
-                pl.when((self.z < t) & (self.z > 0))(lambda t=t: self.right(t).wait_send())
-            else:
-                pl.when(self.z < t)(lambda t=t: self.right(t).wait_send())
-            if t < self.nz - 2:
-                pl.when((self.z > t) & (self.z < self.nz - 1))(lambda t=t: self.left(t).wait_send())
-            else:
-                pl.when(self.z > t)(lambda t=t: self.left(t).wait_send())
+
+    def end(self):
+        z, nz = self.z, self.nz
+        for t in range(nz):
+            right = (z < t) if t == 1 else (z < t) & (z > 0)
+            left = (z > t) if t == nz - 2 else (z > t) & (z < nz - 1)
+            pl.when(right)(lambda t=t: self.right(t).wait_send())
+            pl.when(left)(lambda t=t: self.left(t, False).wait_send())
 
 
 class Square:
@@ -630,32 +631,39 @@
 
 
 class SquareSum:
-    def __init__(self, place, part, once, twice, gone, sems, pieces):
+    def __init__(self, place, part, once, twice, gone, sems, pieces, index=lambda owner: owner, base=None):
         dp, c, z = place
         self.dp, self.dx, self.dy = dp, dp + 1 - 2 * lax.rem(dp, 2), lax.rem(dp + 2, 4)
         self.diag = lax.rem(self.dx + 2, 4)
         self.x, self.y = (self.dx, c, z), (self.dy, c, z)
         self.part, self.once, self.twice, self.gone = part, once, twice, gone
         self.s1, self.r1, self.s2, self.r2 = sems
-        self.pieces = pieces
+        self.pieces, self.index, self.base = pieces, index, base
         self.rows = part.shape[1] // pieces
         cut = (part.shape[2] // TILE + 1) // 2 * TILE
         self.halves = (slice(0, cut), slice(cut, part.shape[2]))
         self.widths = (cut, part.shape[2] - cut)
+
+    def heard(self, slot, start, size):
+        width = self.widths[slot // 2]
+        if self.base is None:
+            return self.once.at[slot, pl.ds(start, size), :width]
+        at = pl.multiple_of(self.base + slot * self.part.shape[1] + start, 16)
+        return self.once.at[pl.ds(at, size), :width]
 
     def first(self, p, side, k):
         owner = ((self.dx, self.diag), (self.dy, self.diag))[side][k]
         at = pl.ds(p * self.rows, self.rows)
         slot = 2 * side + k
         return remote(
-            self.part.at[owner, at, self.halves[side]], self.once.at[slot, at, : self.widths[side]],
+            self.part.at[self.index(owner), at, self.halves[side]], self.heard(slot, p * self.rows, self.rows),
             self.s1.at[p, slot], self.r1.at[p, slot], (self.x, self.y)[side],
         )
 
     def second(self, p, side):
         at = pl.ds(p * self.rows, self.rows)
         return remote(
-            self.gone.at[side, at, : self.widths[side]], self.twice.at[side, at, : self.widths[side]],
+            self.gone.at[at, self.halves[side]], self.twice.at[side, at, : self.widths[side]],
             self.s2.at[p, side], self.r2.at[p, side], (self.y, self.x)[side],
         )
 
@@ -669,7 +677,8 @@
 
     def each(self, p, body):
         def step(r, _):
-            body(pl.ds(pl.multiple_of(p * self.rows + r * 16, 16), 16))
+            start = pl.multiple_of(p * self.rows + r * 16, 16)
+            body(pl.ds(start, 16), start)
             return 0
 
         lax.fori_loop(0, self.rows // 16, step, 0)
@@ -679,10 +688,10 @@
             self.first(p, side, 1).wait_recv()
             owner = (self.dy, self.dx)[side]
 
-            def body(at, side=side, owner=owner):
-                self.gone[side, at, : self.widths[side]] = (
-                    self.part[owner, at, self.halves[side]].astype(F32)
-                    + self.once[2 * side + 1, at, : self.widths[side]].astype(F32)
+            def body(at, start, side=side, owner=owner):
+                self.gone[at, self.halves[side]] = (
+                    self.part[self.index(owner), at, self.halves[side]].astype(F32)
+                    + self.heard(2 * side + 1, start, 16)[...].astype(F32)
                 ).astype(BF16)
 
             self.each(p, body)
@@ -693,10 +702,10 @@
             self.first(p, side, 0).wait_recv()
             self.second(p, side).wait_recv()
 
-            def body(at, side=side):
+            def body(at, start, side=side):
                 out[at, self.halves[side]] = (
-                    self.part[self.dp, at, self.halves[side]].astype(F32)
-                    + self.once[2 * side, at, : self.widths[side]].astype(F32)
+                    self.part[self.index(self.dp), at, self.halves[side]].astype(F32)
+                    + self.heard(2 * side, start, 16)[...].astype(F32)
                     + self.twice[side, at, : self.widths[side]].astype(F32)
                 ).astype(out.dtype)
 
@@ -751,14 +760,18 @@
             )
         pl.semaphore_wait(sem, self.nm - 1 + self.nd - 1)
 
-    def first_kernel(
-        self, docs, starts, unit, x_ref, par_ref, head_ref, g_ref, wm_ref, wc_ref, wo_ref,
-        y_out, x_out, g_out, w_out, wc_out, dproj, dcom, normed_out, sums, heads, gain_out,
-        xall, gall, wall, wcall, woall, parbuf, parall, every_par, projm, pre_sig, o, states, step_s, cum_s,
-        dg, scaled, sel, hp, chp, state, dnext, heard_st, st, pre_bc, projc, taps, ypart, ycame, ytotal, yheard,
+    def kernel(
+        self, docs, lengths, level, x_ref, tap_ref, bias_ref, norm_ref, gain_ref, step_ref, rate_ref, skip_ref, in_ref, g_ref, wo_ref,
+        y_out, dx_out, dw_out, dwc_out, dwo_out, par_out,
+        xall, gall, wall, wcall, woall, wm_ref, wc_ref, head_ref, parbuf_, parall, every_par, projm, pre_sig, o, states,
+        step_s, cum_s, dg, scaled, sel, hp, chp, state, dnext, heard_st, st, pre_bc, projc, taps,
+        ypart, ycame, ytotal, yheard, xheard, dcom, sums, heads, gain_out,
+        cpart, c1, c2, crows, cheard, w1, w2, o2, pard, parbuf,
         pd_s, pd_r, pg_s, pg_r, wz_s, wz_r, cz_s, cz_r, wq_s, wq_r, cq_s, cq_r, oq_s, oq_r, cc_s, cc_r,
         xr_s, xr_r, xl_s, xl_r, xc_s, xc_r, gr_s, gr_r, gl_s, gl_r, gc_s, gc_r,
-        st_s, st_r, yc_s, yc_r, yr_s, yr_r, yl_s, yl_r, loc,
+        st_s, st_r, yc_s, yc_r, yr_s, yr_r, yl_s, yl_r,
+        uc_s, uc_r, ur_s, ur_r, ul_s, ul_r, sc_s, sc_r, c1_s, c1_r, c2_s, c2_r, sz_s, sz_r,
+        w1_s, w1_r, w2_s, w2_r, o1_s, o1_r, o2_s, o2_r, vz_s, vz_r, qd_s, qd_r, qg_s, qg_r, loc,
     ):
         nd, nc, nz, nm = self.nd, self.nc, self.nz, self.nm
         rows, wide = self.rows_in, self.wide
@@ -776,8 +789,8 @@
             return copy
 
         def w_block(owner, m, first=0, count=rows):
-            at = pl.multiple_of((owner * nm + m) * rows + first, rows // 2)
-            return wall.at[pl.ds(at, count), :]
+            at = pl.multiple_of(m * rows + first, rows // 2)
+            return wall.at[owner, pl.ds(at, count), :]
 
         def c_block(owner, m, first=0, count=rows):
             at = pl.multiple_of((owner * nm + m) * rows + first, rows // 2)
@@ -793,9 +806,7 @@
         )
         o_square = Square(
             where,
-            lambda owner, j, first, count: woall.at[
-                pl.ds(pl.multiple_of(owner * TILE + first, TILE // 2), count), :
-            ],
+            lambda owner, j, first, count: woall.at[owner, pl.ds(first, count), :],
             TILE,
             (oq_s, oq_r),
         )
@@ -803,22 +814,44 @@
         g_line = Line(where, sizes, lambda a, b: gall.at[rows_of(a * nz + b), :], (gr_s, gr_r, gl_s, gl_r, gc_s, gc_r))
         y_sum = Sum(where, sizes, ypart, ycame, ytotal, yheard, (yc_s, yc_r, yr_s, yr_r, yl_s, yl_r))
 
-        st[...] = jnp.zeros_like(st)
-        parbuf[dp] = par_ref[...]
+        starts = [jnp.int32(0)]
+        for doc in range(1, docs):
+            starts.append(starts[-1] + lengths[0, doc - 1])
+        active = jnp.right_shift(HEADS, 3 - level[0])
+        unit = jnp.float32(1.0 / INNER)
+        for smaller in range(3):
+            unit = jnp.where(level[0] == smaller, jnp.float32(2.0 ** (3 - smaller) / INNER), unit)
+        own_conv = CONV // (nd * nm)
+        parbuf_[dp, 0:KW, :own_conv] = tap_ref[...]
+        parbuf_[dp, KW : KW + 1, :own_conv] = bias_ref[...]
+        parbuf_[dp, 5:6, :rows] = norm_ref[...]
+        parbuf_[dp, 6:7, :TILE] = gain_ref[...]
+        head_ref[...] = jnp.zeros_like(head_ref)
+        head_ref[0:1, :HEADS] = step_ref[...]
+        head_ref[1:2, :HEADS] = -jnp.exp(rate_ref[...])
+        head_ref[2:3, :HEADS] = skip_ref[...]
+        head_ref[3:4, :] = (iota((1, TILE), 1) < active).astype(F32)
+        for m in range(nm):
+            for i in range(2 * nd):
+                wm_ref[m * rows : (m + 1) * rows, tile_of(i)] = in_ref[:, tile_of(i * nm + m)]
+        shared = EXTENT - 2 * INNER
+        wc_ref[:, 2 * TILE :] = jnp.zeros((rows, COMMON - 2 * TILE), BF16)
+        wc_ref[:, : 2 * TILE] = in_ref[:, 2 * INNER : 2 * INNER + 2 * TILE]
+        wc_ref[:, 2 * TILE : shared] = in_ref[:, 2 * INNER + 2 * TILE :]
         own = [
-            pltpu.make_async_copy(wm_ref.at[me], w_block(dp, me), loc.at[0]),
+            pltpu.make_async_copy(wm_ref.at[rows_of(me, rows), :], w_block(dp, me), loc.at[0]),
             pltpu.make_async_copy(wc_ref, c_block(dp, me), loc.at[1]),
-            pltpu.make_async_copy(wo_ref, woall.at[rows_of(dp), :], loc.at[2]),
+            pltpu.make_async_copy(wo_ref, woall.at[dp], loc.at[2]),
             pltpu.make_async_copy(g_ref, gall.at[rows_of(me), :], loc.at[3]),
         ]
         for copy in own:
             copy.start()
         self.barrier()
         for k, device, _ in lines:
-            go(remote(parbuf.at[dp], parbuf.at[dp], pd_s.at[k], pd_r.at[k], device))
+            go(remote(parbuf_.at[dp], parbuf_.at[dp], pd_s.at[k], pd_r.at[k], device))
         for j, step in enumerate(steps):
             device, there = self.target(step)
-            go(remote(wm_ref.at[there], w_block(dp, me), wz_s.at[j], wz_r.at[j], device))
+            go(remote(wm_ref.at[rows_of(there, rows), :], w_block(dp, me), wz_s.at[j], wz_r.at[j], device))
             if step[0] == 0:
                 go(remote(wc_ref, c_block(dp, me), cz_s.at[step[1]], cz_r.at[step[1]], device))
         for copy in own[:3]:
@@ -827,14 +860,14 @@
         w_square.begin(0)
         c_square.begin(0)
         for k, device, frm in lines:
-            remote(parbuf.at[frm], parbuf.at[frm], pd_s.at[k], pd_r.at[k], device).wait_recv()
-        parall[me] = parbuf[...]
+            remote(parbuf_.at[frm], parbuf_.at[frm], pd_s.at[k], pd_r.at[k], device).wait_recv()
+        parall[me] = parbuf_[...]
         for j, step in enumerate(steps):
             device, _ = self.target(step)
-            go(remote(parbuf, parall.at[me], pg_s.at[j], pg_r.at[j], device))
+            go(remote(parbuf_, parall.at[me], pg_s.at[j], pg_r.at[j], device))
         for j, step in enumerate(steps):
             device, _ = self.target(step)
-            remote(parbuf, parall.at[self.source(step)], pg_s.at[j], pg_r.at[j], device).wait_recv()
+            remote(parbuf_, parall.at[self.source(step)], pg_s.at[j], pg_r.at[j], device).wait_recv()
         owners = [(first // nm, first % nm) for first in range(nd * nm)]
         gain = jnp.concatenate([parall[m, d][5:6, :rows] for d, m in owners], axis=1)
         gain_out[...] = jnp.broadcast_to(gain, (8, MODEL))
@@ -857,7 +890,6 @@
                 o_square.step(0)
                 w_square.step(0)
                 c_square.step(0)
-        own_conv = CONV // (nd * nm)
         every_par[...] = jnp.concatenate([parall[m, d][:, :own_conv] for d, m in owners], axis=1)
         for i in range(nd):
             at = pl.ds(pl.multiple_of((i * nm + me) * TILE, TILE), TILE)
@@ -874,7 +906,7 @@
             chosen = head == i * step_of + self.per * me + lax.div(lane, HEAD_DIM)
             spread = exact(head_ref[...], chosen.astype(F32))
             chp[0:2, tile_of(i)] = spread[2:4, :]
-            chp[2:3, tile_of(i)] = parbuf[i][6:7, :TILE]
+            chp[2:3, tile_of(i)] = parbuf_[i][6:7, :TILE]
         x_line.step(1)
         for j in range(1, 4):
             w_square.step(j)
@@ -897,21 +929,13 @@
         for i in range(nd):
             at = pl.ds(pl.multiple_of((i * nm + (nc - 1 - c) * nz) * rows, rows), nz * rows)
             remote(wcall.at[at, :], wcall.at[at, :], cc_s.at[i], cc_r.at[i], other).wait_recv()
-        outs = [
-            pltpu.make_async_copy(xall, x_out, loc.at[4]),
-            pltpu.make_async_copy(wall, w_out, loc.at[5]),
-            pltpu.make_async_copy(wcall, wc_out, loc.at[6]),
-        ]
-        for copy in outs:
-            copy.start()
-
         projm[0:PAD, :] = jnp.zeros((PAD, 2 * wide), BF16)
         projc[0:PAD, :] = jnp.zeros((PAD, COMMON), BF16)
         projc[PAD:, :] = dot(xall[...], wcall[...]).astype(BF16)
 
         def project(n, _):
             at = rows_of(n, 256)
-            projm[PAD:, at] = dot(xall[...], wall[:, at]).astype(BF16)
+            projm[PAD:, at] = dot(xall[...], wall[:, :, at].reshape(MODEL, 256)).astype(BF16)
             pl.when(n == 2)(lambda: g_line.step(1))
             return 0
 
@@ -931,28 +955,31 @@
 
         o_square.arrive(0)
 
-        def branch(n, _):
-            turn = lax.rem(n + (nc - 1 - c) * nz, nm)
-            ypart[turn] = dot(scaled[rows_of(turn), :], woall[...]).astype(BF16)
-            return 0
-
-        lax.fori_loop(0, nz, branch, 0)
-        for t in range(nz):
-            y_sum.core(t).start()
-        lax.fori_loop(nz, nm, branch, 0)
-        for t in range(nz):
-            y_sum.add_core(t)
+        def branch(pair):
+            def some(n, _):
+                t = pair + lax.rem(n, 2) * (nz - 1 - 2 * pair)
+                turn = t + lax.rem(nc - 1 - c + lax.div(n, 2), nc) * nz
+                ypart[turn] = dot(scaled[rows_of(turn), :], woall[...].reshape(wide, MODEL)).astype(BF16)
+                pl.when(n < 2)(lambda: y_sum.core(t).start())
+                return 0
+
+            lax.fori_loop(0, 4, some, 0)
+
+        branch(0)
+        y_sum.add_core(0)
+        y_sum.add_core(nz - 1)
         y_sum.begin()
+        for pair in range(1, nz // 2):
+            branch(pair)
+            y_sum.add_core(pair)
+            y_sum.add_core(nz - 1 - pair)
 
         g_line.arrive()
-        out = pltpu.make_async_copy(gall, g_out, loc.at[7])
-        out.start()
-        outs.append(out)
         lanes_at = iota((SPAN, TILE), 1)
 
         def gate_grad(n, _):
             at = rows_of(n, 256)
-            grad = dot(gall[at, :], woall[...], ((1,), (1,)))
+            grad = dot(gall[at, :], woall[...].reshape(wide, MODEL), ((1,), (1,)))
             dg[at, :] = grad
             for half in range(2):
                 product = jnp.zeros((SPAN, TILE), F32)
@@ -984,22 +1011,17 @@
         def backward(n, _):
             self.backward_chunk(
                 nm - 1 - n, docs, starts, unit, projm, pre_sig, pre_bc, o, states, step_s, cum_s, dg, st, taps, sel,
-                hp, chp, dproj, dcom, normed_out, sums, heads, state, dnext, projc,
+                hp, chp, dcom, scaled, sums, heads, state, dnext, projc,
             )
             for k in range(1, nz - 1):
                 pl.when(n == SLOTS[k - 1])(lambda k=k: y_sum.slot(k))
             return 0
 
         lax.fori_loop(0, nm, backward, 0)
-        y_sum.arrive()
-        stat = jnp.broadcast_to(st[0, pl.ds(me, 1), :], (SPAN, TILE)).T
-        root = lax.rsqrt(stat[:, 0:1] * unit[0, 0] + EPSILON)
-        y_out[...] = (x_ref[...].astype(F32) + root * y_sum.own(slice(None))).astype(BF16)
-        for copy in outs:
-            copy.wait()
         for copy in started:
             if not any(copy is s for s in sent):
                 copy.wait_send()
+        started.clear()
         for j in range(nm):
             w_square.end(j)
         for j in range(nz):
@@ -1007,7 +1029,167 @@
         o_square.end(0)
         x_line.end()
         g_line.end()
+
+        x_sum = Sum(where, sizes, ypart, ycame, ytotal, xheard, (uc_s, uc_r, ur_s, ur_r, ul_s, ul_r))
+        w_sum = SquareSum(where, wall, w1, w2, projm, (w1_s, w1_r, w2_s, w2_r), 2)
+        o_sum = SquareSum(where, woall, xall, o2, xall, (o1_s, o1_r, o2_s, o2_r), 1, base=4 * TILE)
+        c_sum = SquareSum(where, cpart, c1, c2, dcom, (c1_s, c1_r, c2_s, c2_r), 1, lambda owner: owner * nc + c)
+        def input_grad(core):
+            base = rows_of(core, nz * SPAN)
+            lead = pl.ds(pl.multiple_of(core * nz * SPAN + PAD, PAD), nz * SPAN)
+
+            def piece(n, _):
+                at = rows_of(n, 256)
+                part = dot(projm[lead, :], wall[lax.div(n, 2), rows_of(lax.rem(n, 2), 256), :], ((1,), (1,)))
+                part = (part + dot(dcom[base, :], wcall[at, :], ((1,), (1,)))).astype(BF16)
+                for t in range(nz):
+                    ypart[core * nz + t, :, at] = part[t * SPAN : (t + 1) * SPAN, :]
+                return 0
+
+            lax.fori_loop(0, MODEL // 256, piece, 0)
+
+        y_sum.end_core()
+        input_grad(nc - 1 - c)
+        for t in range(nz):
+            x_sum.core(t).start()
+        input_grad(c)
+        y_sum.arrive()
+        stat = jnp.broadcast_to(st[0, pl.ds(me, 1), :], (SPAN, TILE)).T
+        root = lax.rsqrt(stat[:, 0:1] * unit + EPSILON)
+        y_out[...] = (x_ref[...].astype(F32) + root * y_sum.own(slice(None))).astype(BF16)
         y_sum.end()
+        x_sum.add_core(0)
+        x_sum.add_core(nz - 1)
+        x_sum.begin()
+        for t in range(1, nz - 1):
+            x_sum.add_core(t)
+
+        def weight_grad(owner):
+            def piece(n, _):
+                at = pl.ds(pl.multiple_of(owner * (nm * rows) + n * 256, 256), 256)
+                wall[owner, rows_of(n, 256), :] = dot(xall[:, at], projm[PAD:, :], ((0,), (0,))).astype(BF16)
+                return 0
+
+            lax.fori_loop(0, nm * rows // 256, piece, 0)
+
+        weight_grad(w_sum.diag)
+        weight_grad(w_sum.dx)
+        w_sum.begin_x(0)
+        weight_grad(w_sum.dy)
+        w_sum.begin_y(0)
+        weight_grad(dp)
+
+        def shared_grad(n, _):
+            at = rows_of(n, 256)
+            cpart[n] = dot(xall[:, at], dcom[...], ((0,), (0,))).astype(BF16)
+            return 0
+
+        lax.fori_loop(0, nd * nc, shared_grad, 0)
+        ccopies = [
+            go(remote(cpart.at[i * nc + nc - 1 - c], projc.at[rows_of(i, nz * rows), :], sc_s.at[i], sc_r.at[i], other)) for i in range(nd)
+        ]
+        x_sum.slot(1)
+
+        def out_grad(n, _):
+            at = rows_of(n, 512)
+            part = dot(scaled[...], gall[:, at], ((0,), (0,))).astype(BF16)
+            for i in range(nd):
+                woall[i, :, at] = part[tile_of(i), :]
+            return 0
+
+        lax.fori_loop(0, MODEL // 512, out_grad, 0)
+        w_sum.pass_on(0)
+        w_sum.begin_x(1)
+        w_sum.begin_y(1)
+        for i in range(nd):
+            ccopies[i].wait_recv()
+            cpart[i * nc + c] = (cpart[i * nc + c].astype(F32) + projc[rows_of(i, nz * rows), :].astype(F32)).astype(BF16)
+        x_sum.slot(2)
+
+        def send_rows(p):
+            half = nm // 2
+            for j in range(half):
+                there = p * half + j
+                block = wm_ref.at[there * rows : (there + 1) * rows, :]
+                ct, zt = there // nz, there % nz
+
+                @pl.when(there != me)
+                def _():
+                    remote(block, dw_out.at[me], vz_s.at[there], vz_r.at[me], (dp, ct, zt)).start()
+
+                @pl.when(there == me)
+                def _():
+                    dw_out[there] = block[...]
+
+        w_sum.finish(0, wm_ref)
+        send_rows(0)
+        w_sum.pass_on(1)
+        c_sum.begin_x(0)
+        c_sum.begin_y(0)
+        o_sum.begin_x(0)
+        o_sum.begin_y(0)
+
+        x_sum.arrive()
+        hidden = x_ref[...].astype(F32)
+        normed_grad = x_sum.own(slice(None))
+        inverse = lax.rsqrt(jnp.mean(hidden * hidden, axis=1, keepdims=True) + EPSILON)
+        unitary = hidden * inverse
+        gain_grad = jnp.sum(normed_grad * unitary, axis=0, keepdims=True)
+        grad_scaled = normed_grad * gain_out[0:1, :]
+        middle = jnp.mean(grad_scaled * unitary, axis=1, keepdims=True)
+        dx_out[...] = (gall[rows_of(me), :].astype(F32) + inverse * (grad_scaled - unitary * middle)).astype(BF16)
+        base_row = MODEL // TILE
+        for i in range(base_row):
+            parbuf[i : i + 1, :] = gain_grad[:, tile_of(i)]
+        count = nd + 2
+        for r in range(8):
+            for i in range(count):
+                at = base_row + r * count + i
+                parbuf[at : at + 1, :] = sums[r : r + 1, tile_of(i)]
+        parbuf[base_row + 8 * count :, :] = heads[...]
+        small = [
+            go(remote(parbuf, pard.at[k - 1], qd_s.at[k], qd_r.at[k], device)) for k, device, _ in lines
+        ]
+        w_sum.finish(1, wm_ref)
+        send_rows(1)
+        c_sum.pass_on(0)
+        o_sum.pass_on(0)
+        c_sum.finish(0, crows)
+        for d in range(1, nz):
+            to = lax.rem(z + d, nz)
+            go(remote(crows.at[rows_of(to, rows), :], cheard.at[d - 1], sz_s.at[d], sz_r.at[d], (dp, c, to)))
+        for copy in small:
+            copy.wait_recv()
+        total = parbuf[...]
+        for k in range(nd - 1):
+            total = total + pard[k]
+        par_out[me] = total
+        for j, step in enumerate(steps):
+            go(remote(par_out.at[me], par_out.at[me], qg_s.at[j], qg_r.at[j], self.target(step)[0]))
+        o_sum.finish(0, dwo_out)
+        total = crows[rows_of(z, rows), :].astype(F32)
+        for d in range(1, nz):
+            remote(cheard.at[d - 1], cheard.at[d - 1], sz_s.at[d], sz_r.at[d], other).wait_recv()
+            total = total + cheard[d - 1].astype(F32)
+        dwc_out[...] = total
+        for j, step in enumerate(steps):
+            here = par_out.at[self.source(step)]
+            remote(here, here, qg_s.at[j], qg_r.at[j], other).wait_recv()
+        for m in range(nm):
+            got = dw_out.at[m]
+
+            @pl.when(m != me)
+            def _():
+                remote(got, got, vz_s.at[m], vz_r.at[m], other).wait_recv()
+                remote(got, got, vz_s.at[m], vz_r.at[m], other).wait_send()
+
+        for copy in started:
+            copy.wait_send()
+        x_sum.end_core()
+        x_sum.end()
+        w_sum.end()
+        o_sum.end()
+        c_sum.end()
 
     def forward_chunk(
         self, chunk, docs, starts, projm, projc, taps, sel, hp, chp,
@@ -1044,8 +1226,9 @@
         last_same = (begin_t == begin_last).astype(F32)
         meet = dot(query_side, key_side, ((1,), (1,)))
         before = state[...]
-        states[chunk] = before
-        carried_out = dot(query_side, before.astype(BF16))
+        before_low = before.astype(BF16)
+        states[chunk] = before_low
+        carried_out = dot(query_side, before_low)
         squares = jnp.zeros((SPAN, TILE), F32)
         for i in range(nd):
             lanes = tile_of(i)
@@ -1079,7 +1262,7 @@
 
     def backward_chunk(
         self, chunk, docs, starts, unit, projm, pre_sig, pre_bc, o, states, step_s, cum_s, dg, st, taps, sel,
-        hp, chp, dproj, dcom, normed_out, sums, heads, dstate, dnext, projc,
+        hp, chp, dcom, normed_out, sums, heads, dstate, dnext, projc,
     ):
         nd = self.nd
         first = chunk * SPAN
@@ -1104,10 +1287,10 @@
         cum_t = cum.T
         square = jnp.broadcast_to(st[0, pl.ds(chunk, 1), :], (SPAN, TILE)).T
         cross = jnp.broadcast_to(st[1, pl.ds(chunk, 1), :], (SPAN, TILE)).T
-        root = lax.rsqrt(square * unit[0, 0] + EPSILON)
-        pull = root * root * root * cross * unit[0, 0]
-        before = states[chunk]
-        before_low = before.astype(BF16)
+        root = lax.rsqrt(square * unit + EPSILON)
+        pull = root * root * root * cross * unit
+        before_low = states[chunk]
+        before = before_low.astype(F32)
         after = dstate[...]
         after_low = after.astype(BF16)
         carried_out = dot(query_side, before_low)
@@ -1154,7 +1337,7 @@
             sums[0:1, lanes] += jnp.sum(grad * gated * root, axis=0, keepdims=True)
             gated_grad = root * grad * gain - gated * pull
             mixed_grad = gated_grad * opened * mask
-            dproj[here, lanes] = (
+            projm[body, lanes] = (
                 gated_grad * mixed * (gate_sig * (1.0 + gate_in * (1.0 - gate_sig)))
             ).astype(BF16)
             sums[1:2, lanes] += jnp.sum(mixed_grad * signal, axis=0, keepdims=True)
@@ -1203,7 +1386,7 @@
             signal_grad = stepx * fed_grad + chp[0:1, lanes] * mixed_grad
             pre_grad = signal_grad * (gate_of * (1.0 + pre * (1.0 - gate_of)))
             cols = tile_of(nd + i)
-            dproj[here, cols] = conv_back(pre_grad, projm[lead, cols].astype(F32), lanes).astype(BF16)
+            projm[body, cols] = conv_back(pre_grad, projm[lead, cols].astype(F32), lanes).astype(BF16)
         meet_low = meet_grad.astype(BF16)
         state_rows = ((1,), (1,))
         query_grad = dot(meet_low, key_side) + dot(jnp.concatenate(entered, axis=1), before_low, state_rows)
@@ -1222,320 +1405,58 @@
         heads[1:2, :] += jnp.sum(decay_grad * log_decay, axis=0, keepdims=True)
         dcom[here, 2 * TILE :] = dot(rate_grad.astype(BF16), sel[...], ((1,), (1,))).astype(BF16)
 
-    def first(self, docs, starts, unit, x, par, heads, g, wm, wc, wo):
-        nd, nz, nm, rows, span, wide = self.nd, self.nz, self.nm, self.rows_in, self.span, self.wide
-        like = jax.ShapeDtypeStruct
-        block = (SPAN, MODEL)
-        return pl.pallas_call(
-            functools.partial(self.first_kernel, docs),
-            out_shape=[
-                like(block, BF16),
-                like((span, MODEL), BF16),
-                like((span, MODEL), BF16),
-                like((MODEL, 2 * wide), BF16),
-                like((MODEL, COMMON), BF16),
-                like((span, 2 * wide), BF16),
-                like((span, COMMON), BF16),
-                like((span, wide), BF16),
-                like((8, wide + 2 * TILE), F32),
-                like((8, TILE), F32),
-                like((8, MODEL), F32),
-            ],
-            in_specs=[SM, SM, VM, VM, VM, ANY, ANY, ANY, ANY],
-            out_specs=[VM, ANY, ANY, ANY, ANY] + [VM] * 6,
-            scratch_shapes=[
-                pltpu.VMEM((span, MODEL), BF16),
-                pltpu.VMEM((span, MODEL), BF16),
-                pltpu.VMEM((MODEL, 2 * wide), BF16),
-                pltpu.VMEM((MODEL, COMMON), BF16),
-                pltpu.VMEM((wide, MODEL), BF16),
-                pltpu.VMEM((nd, 8, 2 * TILE), F32),
-                pltpu.VMEM((nm, nd, 8, 2 * TILE), F32),
-                pltpu.VMEM((8, CONV), F32),
-                pltpu.VMEM((PAD + span, 2 * wide), BF16),
-                pltpu.VMEM((span, wide), F32),
-                pltpu.VMEM((span, wide), F32),
-                pltpu.VMEM((nm, STATE, wide), F32),
-                pltpu.VMEM((span, TILE), F32),
-                pltpu.VMEM((span, TILE), F32),
-                pltpu.VMEM((span, wide), F32),
-                pltpu.VMEM((span, wide), BF16),
-                pltpu.VMEM((TILE, TILE), BF16),
-                pltpu.VMEM((8, TILE), F32),
-                pltpu.VMEM((8, wide), F32),
-                pltpu.VMEM((STATE, wide), F32),
-                pltpu.VMEM((PAD, wide + 2 * TILE), F32),
-                pltpu.VMEM((nm - 1, 2, nm, TILE), F32),
-                pltpu.VMEM((2, nm, TILE), F32),
-                pltpu.VMEM((span, 2 * TILE), F32),
-                pltpu.VMEM((PAD + span, COMMON), BF16),
-                pltpu.VMEM((8, wide + 2 * TILE), F32),
-                pltpu.VMEM((nm, *block), BF16),
-                pltpu.VMEM((nz, *block), BF16),
-                pltpu.VMEM((nz, *block), BF16),
-                pltpu.VMEM((2 * nz, *block), BF16),
-                DMA((nd,)), DMA((nd,)), DMA((nm,)), DMA((nm,)),
-                DMA((nm,)), DMA((nm,)), DMA((nz,)), DMA((nz,)),
-                DMA((4, nm)), DMA((4, nm)), DMA((4, nz)), DMA((4, nz)), DMA((4, 1)), DMA((4, 1)),
-                DMA((nd,)), DMA((nd,)),
-                DMA((nz,)), DMA((nz,)), DMA((nz,)), DMA((nz,)), DMA((nz,)), DMA((nz,)),
-                DMA((nz,)), DMA((nz,)), DMA((nz,)), DMA((nz,)), DMA((nz,)), DMA((nz,)),
-                DMA((nm,)), DMA((nm,)),
-                DMA((nz,)), DMA((nz,)), DMA((nz,)), DMA((nz,)), DMA((nz,)), DMA((nz,)),
-                DMA((8,)),
-            ],
-            compiler_params=pltpu.CompilerParams(
-                collective_id=0, has_side_effects=True, vmem_limit_bytes=62 * 2**20
-            ),
-            name="first",
-        )(starts, unit, x, par, heads, g, wm, wc, wo)
-
-    def second_kernel(
-        self, dproj, dcom, normed_out, sums, heads, gain, x_ref, g_ref, x_in, g_in, w_in, wc_in,
-        dx_out, dw_out, dwc_out, dwo_out, par_out,
-        xall, gall, wall, wcall, xpart, xcame, xtotal, xheard,
-        cpart, ccame, csum, c1, c2, cgo, crows, cheard,
-        wpart, w1, w2, wgo, wsum, opart, o1, o2, ogo, pard, parbuf,
-        xc_s, xc_r, xr_s, xr_r, xl_s, xl_r, cc_s, cc_r, c1_s, c1_r, c2_s, c2_r, cz_s, cz_r,
-        w1_s, w1_r, w2_s, w2_r, o1_s, o1_r, o2_s, o2_r, wz_s, wz_r, pd_s, pd_r, pg_s, pg_r, loc,
-    ):
-        nd, nc, nz, nm = self.nd, self.nc, self.nz, self.nm
-        rows, wide, span = self.rows_in, self.wide, self.span
-        where = dp, c, z = self.place()
-        me = c * nz + z
-        sizes = (nc, nz)
-        steps = self.group_steps()
-        other = (dp, nc - 1 - c, z)
-        lines = [(k, (lax.rem(dp + k, nd), c, z), lax.rem(dp + k, nd)) for k in range(1, nd)]
-        started = []
-
-        def go(copy):
-            copy.start()
-            started.append(copy)
-            return copy
-
-        loads = [
-            pltpu.make_async_copy(w_in, wall, loc.at[0]),
-            pltpu.make_async_copy(wc_in, wcall, loc.at[1]),
-            pltpu.make_async_copy(x_in, xall, loc.at[2]),
-            pltpu.make_async_copy(g_in, gall, loc.at[3]),
-        ]
-        for load in loads:
-            load.start()
-        self.barrier()
-        x_sum = Sum(where, sizes, xpart, xcame, xtotal, xheard, (xc_s, xc_r, xr_s, xr_r, xl_s, xl_r))
-        w_sum = SquareSum(where, wpart, w1, w2, wgo, (w1_s, w1_r, w2_s, w2_r), 2)
-        o_sum = SquareSum(where, opart, o1, o2, ogo, (o1_s, o1_r, o2_s, o2_r), 1)
-        c_sum = SquareSum(where, csum, c1, c2, cgo, (c1_s, c1_r, c2_s, c2_r), 1)
-        loads[0].wait()
-        loads[1].wait()
-
-        def input_grad(core):
-            base = rows_of(core, nz * SPAN)
-
-            def piece(n, _):
-                at = rows_of(n, 256)
-                part = dot(dproj[base, :], wall[at, :], ((1,), (1,)))
-                part = (part + dot(dcom[base, :], wcall[at, :], ((1,), (1,)))).astype(BF16)
-                for t in range(nz):
-                    xpart[core * nz + t, :, at] = part[t * SPAN : (t + 1) * SPAN, :]
-                return 0
-
-            lax.fori_loop(0, MODEL // 256, piece, 0)
-
-        input_grad(nc - 1 - c)
-        for t in range(nz):
-            x_sum.core(t).start()
-        input_grad(c)
-        for t in range(nz):
-            x_sum.add_core(t)
-        x_sum.begin()
-
-        loads[2].wait()
-
-        def weight_grad(owner):
-            def piece(n, _):
-                at = pl.ds(pl.multiple_of(owner * (nm * rows) + n * 256, 256), 256)
-                wpart[owner, rows_of(n, 256), :] = dot(xall[:, at], dproj[...], ((0,), (0,))).astype(BF16)
-                return 0
-
-            lax.fori_loop(0, nm * rows // 256, piece, 0)
-
-        weight_grad(w_sum.diag)
-        weight_grad(w_sum.dx)
-        for p in range(2):
-            w_sum.begin_x(p)
-        weight_grad(w_sum.dy)
-        for p in range(2):
-            w_sum.begin_y(p)
-        weight_grad(dp)
-
-        def shared_grad(n, _):
-            at = rows_of(n, 256)
-            cpart[n] = dot(xall[:, at], dcom[...], ((0,), (0,))).astype(BF16)
-            return 0
-
-        lax.fori_loop(0, nd * nc, shared_grad, 0)
-        ccopies = [
-            go(remote(cpart.at[i * nc + nc - 1 - c], ccame.at[i], cc_s.at[i], cc_r.at[i], other)) for i in range(nd)
-        ]
-        x_sum.slot(1)
-        loads[3].wait()
-
-        def out_grad(n, _):
-            at = rows_of(n, 512)
-            part = dot(normed_out[...], gall[:, at], ((0,), (0,))).astype(BF16)
-            for i in range(nd):
-                opart[i, :, at] = part[tile_of(i), :]
-            return 0
-
-        lax.fori_loop(0, MODEL // 512, out_grad, 0)
-        for i in range(nd):
-            ccopies[i].wait_recv()
-            csum[i] = (cpart[i * nc + c].astype(F32) + ccame[i].astype(F32)).astype(BF16)
-        c_sum.begin_x(0)
-        c_sum.begin_y(0)
-        o_sum.begin_x(0)
-        o_sum.begin_y(0)
-        w_sum.pass_on(0)
-        x_sum.slot(2)
-        w_sum.pass_on(1)
-
-        def send_rows(p):
-            half = nm // 2
-            for j in range(half):
-                there = p * half + j
-                block = wsum.at[there * rows : (there + 1) * rows, :]
-                ct, zt = there // nz, there % nz
-
-                @pl.when(there != me)
-                def _():
-                    remote(block, dw_out.at[me], wz_s.at[there], wz_r.at[me], (dp, ct, zt)).start()
-
-                @pl.when(there == me)
-                def _():
-                    dw_out[there] = block[...]
-
-        w_sum.finish(0, wsum)
-        send_rows(0)
-        c_sum.pass_on(0)
-        o_sum.pass_on(0)
-
-        x_sum.arrive()
-        hidden = x_ref[...].astype(F32)
-        normed_grad = x_sum.own(slice(None))
-        inverse = lax.rsqrt(jnp.mean(hidden * hidden, axis=1, keepdims=True) + EPSILON)
-        unitary = hidden * inverse
-        gain_grad = jnp.sum(normed_grad * unitary, axis=0, keepdims=True)
-        grad_scaled = normed_grad * gain[0:1, :]
-        middle = jnp.mean(grad_scaled * unitary, axis=1, keepdims=True)
-        dx_out[...] = (g_ref[...].astype(F32) + inverse * (grad_scaled - unitary * middle)).astype(BF16)
-        base_row = MODEL // TILE
-        for i in range(base_row):
-            parbuf[i : i + 1, :] = gain_grad[:, tile_of(i)]
-        count = nd + 2
-        for r in range(8):
-            for i in range(count):
-                at = base_row + r * count + i
-                parbuf[at : at + 1, :] = sums[r : r + 1, tile_of(i)]
-        parbuf[base_row + 8 * count :, :] = heads[...]
-        small = [
-            go(remote(parbuf, pard.at[k - 1], pd_s.at[k], pd_r.at[k], device)) for k, device, _ in lines
-        ]
-        w_sum.finish(1, wsum)
-        send_rows(1)
-        c_sum.finish(0, crows)
-        for d in range(1, nz):
-            to = lax.rem(z + d, nz)
-            go(remote(crows.at[rows_of(to, rows), :], cheard.at[d - 1], cz_s.at[d], cz_r.at[d], (dp, c, to)))
-        for copy in small:
-            copy.wait_recv()
-        total = parbuf[...]
-        for k in range(nd - 1):
-            total = total + pard[k]
-        par_out[me] = total
-        for j, step in enumerate(steps):
-            go(remote(par_out.at[me], par_out.at[me], pg_s.at[j], pg_r.at[j], self.target(step)[0]))
-        o_sum.finish(0, dwo_out)
-        total = crows[rows_of(z, rows), :].astype(F32)
-        for d in range(1, nz):
-            remote(cheard.at[d - 1], cheard.at[d - 1], cz_s.at[d], cz_r.at[d], other).wait_recv()
-            total = total + cheard[d - 1].astype(F32)
-        dwc_out[...] = total
-        for j, step in enumerate(steps):
-            here = par_out.at[self.source(step)]
-            remote(here, here, pg_s.at[j], pg_r.at[j], other).wait_recv()
-        for m in range(nm):
-            got = dw_out.at[m]
-
-            @pl.when(m != me)
-            def _():
-                remote(got, got, wz_s.at[m], wz_r.at[m], other).wait_recv()
-                remote(got, got, wz_s.at[m], wz_r.at[m], other).wait_send()
-
-        for copy in started:
-            copy.wait_send()
-        x_sum.end()
-        w_sum.end()
-        o_sum.end()
-        c_sum.end()
-
-    def second(self, dproj, dcom, normed_out, sums, heads, gain, x, g, xall, gall, w, wc):
+    def run(self, docs, *args):
         nd, nc, nz, nm, rows, span, wide = self.nd, self.nc, self.nz, self.nm, self.rows_in, self.span, self.wide
         like = jax.ShapeDtypeStruct
         block = (SPAN, MODEL)
         npar = MODEL // TILE + 8 * (nd + 2) + 8
+
+        def low(*shape):
+            return pltpu.VMEM(shape, BF16)
+
+        def full(*shape):
+            return pltpu.VMEM(shape, F32)
+
+        pair = lambda *shape: [DMA(shape), DMA(shape)]
         return pl.pallas_call(
-            self.second_kernel,
+            functools.partial(self.kernel, docs),
             out_shape=[
+                like(block, BF16),
                 like(block, BF16),
                 like((nm, rows, 2 * wide), BF16),
                 like((rows, COMMON), F32),
-                like((TILE, MODEL), F32),
+                like((TILE, MODEL), BF16),
                 like((nm, npar, TILE), F32),
             ],
-            in_specs=[VM] * 8 + [ANY] * 4,
-            out_specs=[VM] * 5,
+            in_specs=[SM, SM] + [VM] * 9 + [ANY, ANY],
+            out_specs=[VM] * 6,
             scratch_shapes=[
-                pltpu.VMEM((span, MODEL), BF16),
-                pltpu.VMEM((span, MODEL), BF16),
-                pltpu.VMEM((MODEL, 2 * wide), BF16),
-                pltpu.VMEM((MODEL, COMMON), BF16),
-                pltpu.VMEM((nm, *block), BF16),
-                pltpu.VMEM((nz, *block), BF16),
-                pltpu.VMEM((nz, *block), BF16),
-                pltpu.VMEM((2 * nz, *block), BF16),
-                pltpu.VMEM((nd * nc, nz * rows, COMMON), BF16),
-                pltpu.VMEM((nd, nz * rows, COMMON), BF16),
-                pltpu.VMEM((nd, nz * rows, COMMON), BF16),
-                pltpu.VMEM((4, nz * rows, 2 * TILE), BF16),
-                pltpu.VMEM((2, nz * rows, 2 * TILE), BF16),
-                pltpu.VMEM((2, nz * rows, 2 * TILE), BF16),
-                pltpu.VMEM((nz * rows, COMMON), BF16),
-                pltpu.VMEM((nz - 1, rows, COMMON), BF16),
-                pltpu.VMEM((nd, nm * rows, 2 * wide), BF16),
-                pltpu.VMEM((4, nm * rows, wide), BF16),
-                pltpu.VMEM((2, nm * rows, wide), BF16),
-                pltpu.VMEM((2, nm * rows, wide), BF16),
-                pltpu.VMEM((nm * rows, 2 * wide), BF16),
-                pltpu.VMEM((nd, TILE, MODEL), BF16),
-                pltpu.VMEM((4, TILE, MODEL // 2), BF16),
-                pltpu.VMEM((2, TILE, MODEL // 2), BF16),
-                pltpu.VMEM((2, TILE, MODEL // 2), BF16),
-                pltpu.VMEM((nd - 1, npar, TILE), F32),
-                pltpu.VMEM((npar, TILE), F32),
-                DMA((nz,)), DMA((nz,)), DMA((nz,)), DMA((nz,)), DMA((nz,)), DMA((nz,)),
-                DMA((nd,)), DMA((nd,)), DMA((1, 4)), DMA((1, 4)), DMA((1, 2)), DMA((1, 2)), DMA((nz,)), DMA((nz,)),
-                DMA((2, 4)), DMA((2, 4)), DMA((2, 2)), DMA((2, 2)),
-                DMA((1, 4)), DMA((1, 4)), DMA((1, 2)), DMA((1, 2)),
-                DMA((nm,)), DMA((nm,)), DMA((nd,)), DMA((nd,)),
-                DMA((nm,)), DMA((nm,)), DMA((4,)),
+                low(span, MODEL), low(span, MODEL), low(nd, nm * rows, 2 * wide), low(MODEL, COMMON),
+                low(nd, TILE, MODEL), low(nm * rows, 2 * wide), low(rows, COMMON), full(8, TILE),
+                full(nd, 8, 2 * TILE), full(nm, nd, 8, 2 * TILE), full(8, CONV), low(PAD + span, 2 * wide),
+                full(span, wide), full(span, wide), low(nm, STATE, wide),
+                full(span, TILE), full(span, TILE), full(span, wide), low(span, wide), low(TILE, TILE),
+                full(8, TILE), full(8, wide), full(STATE, wide), full(PAD, wide + 2 * TILE),
+                full(nm - 1, 2, nm, TILE), full(2, nm, TILE), full(span, 2 * TILE), low(PAD + span, COMMON),
+                full(8, wide + 2 * TILE),
+                low(nm, *block), low(nz, *block), low(nz, *block), low(nz + 1, *block), low(nz + 1, *block),
+                low(span, COMMON), full(8, wide + 2 * TILE), full(8, TILE), full(8, MODEL),
+                low(nd * nc, nz * rows, COMMON), low(4, nz * rows, 2 * TILE),
+                low(2, nz * rows, 2 * TILE), low(nz * rows, COMMON), low(nz - 1, rows, COMMON),
+                low(4, nm * rows, wide), low(2, nm * rows, wide),
+                low(2, TILE, MODEL // 2),
+                full(nd - 1, npar, TILE), full(npar, TILE),
+                *pair(nd), *pair(nm), *pair(nm), *pair(nz), *pair(4, nm), *pair(4, nz), *pair(4, 1), *pair(nd),
+                *pair(nz), *pair(nz), *pair(nz), *pair(nz), *pair(nz), *pair(nz),
+                *pair(nm), *pair(nz), *pair(nz), *pair(nz),
+                *pair(nz), *pair(nz), *pair(nz), *pair(nd), *pair(1, 4), *pair(1, 2), *pair(nz),
+                *pair(2, 4), *pair(2, 2), *pair(1, 4), *pair(1, 2), *pair(nm), *pair(nd), *pair(nm), DMA((4,)),
             ],
             compiler_params=pltpu.CompilerParams(
-                collective_id=1, has_side_effects=True, vmem_limit_bytes=62 * 2**20
+                collective_id=0, has_side_effects=True, vmem_limit_bytes=63 * 2**20
             ),
-            name="second",
-        )(dproj, dcom, normed_out, sums, heads, gain, x, g, xall, gall, w, wc)
+            name="first",
+        )(*args)
 
     def local(
         self, layer_input, out_grad, norm_gain, in_weight, conv_weight, conv_bias, step_bias, log_rate,
@@ -1545,36 +1466,12 @@
         dp, c, z = self.place()
         me = c * nz + z
         docs = doc_lengths.shape[1]
-        order = jnp.arange(docs)
-        ahead = order[:, None] < order[None, :]
-        starts = jnp.sum(jnp.where(ahead, doc_lengths[0][:, None], 0), axis=0, keepdims=True)
-        starts = starts.astype(jnp.int32)
-        active = jnp.right_shift(HEADS, 3 - nest_level[0])
-        unit = (1.0 / (active * HEAD_DIM).astype(F32)).reshape(1, 1)
         x = layer_input.reshape(SPAN, MODEL)
         g = out_grad.reshape(SPAN, MODEL)
-        wm = in_weight[:, : 2 * INNER].reshape(rows, 2 * nd, nm, TILE)
-        wm = jnp.transpose(wm, (2, 0, 1, 3)).reshape(nm, rows, 2 * wide)
-        wc = jnp.pad(in_weight[:, 2 * INNER :], ((0, 0), (0, COMMON - (EXTENT - 2 * INNER))))
         own_conv = conv_bias.shape[0]
-        widen = lambda v: jnp.pad(v, ((0, 0), (0, 2 * TILE - v.shape[1])))
-        par = jnp.concatenate(
-            [
-                widen(conv_weight.T),
-                widen(conv_bias[None]),
-                widen(norm_gain[None]),
-                widen(gate_gain[None]),
-                jnp.zeros((1, 2 * TILE), F32),
-            ]
-        )
-        mask = (jnp.arange(HEADS) < active).astype(F32)
-        head_in = jnp.stack([step_bias, -jnp.exp(log_rate), skip_gain, mask])
-        head_in = jnp.pad(head_in, ((0, 4), (0, TILE - HEADS)))
-        y_out, xall, gall, w, wc_all, dproj, dcom, normed_out, sums, heads, gain = self.first(
-            docs, starts, unit, x, par, head_in, g, wm, wc, out_weight
-        )
-        dx_out, dw, dwc, dwo, pars = self.second(
-            dproj, dcom, normed_out, sums, heads, gain, x, g, xall, gall, w, wc_all
+        y_out, dx_out, dw, dwc, dwo, pars = self.run(
+            docs, doc_lengths, nest_level, x, conv_weight.T, conv_bias[None], norm_gain[None], gate_gain[None],
+            step_bias[None], log_rate[None], skip_gain[None], in_weight, g, out_weight,
         )
         dw = jnp.transpose(dw.reshape(nm, rows, 2 * nd, TILE), (1, 2, 0, 3)).reshape(rows, 2 * INNER)
         in_weight_grad = jnp.concatenate([dw.astype(F32), dwc[:, : EXTENT - 2 * INNER]], axis=1)
@@ -1607,7 +1504,7 @@
             log_rate_grad,
             skip_gain_grad,
             gate_gain_grad,
-            dwo,
+            dwo.astype(F32),
         )
 
 

time: 300 us -> 264 us (0.88)
  Pallas kernels: 274 us -> 248 us
  local copies, waits for them, and re-layouts: 16.5 us -> 8.57 us
    pallas_call x2 -> x1, Pallas kernels: 274 us -> 248 us  [run(): pl.pallas_call(functools.partial(self.kernel, docs), out_shape=[like(bloc...]
    pad x5 -> x0, local copies, waits for them, and re-layouts: 3.32 us -> none  [the longest x4 2.7 us: local(): widen = lambda v: jnp.pad(v, ((0, 0), (0, 2 * TILE - v.shape[1])))]
    unnamed x21 -> x18, local copies, waits for them, and re-layouts: 6.87 us -> 4.35 us
where the time goes in v4:
time: 264 us; the launch traced here: 263 us
  Pallas kernels  248 us (94%)
  local copies, waits for them, and re-layouts  8.57 us (3%)
  other arithmetic  5.41 us (2%)
    pallas_call x1, Pallas kernels, run(): pl.pallas_call(functools.partial(self.kernel, docs), out_shape=[like(bloc...  248 us

profile of v4, /device:TPU:0, one launch (start us, length us, event | category | flops | bytes accessed | tf_op | source)
XLA Modules:
  0.0 263.3 jit_solution(3569990111283817889)
XLA Ops:
  1.3 247.9 %first.1 = (bf16[128,2048]{1,0:T(8,128)(2,1)}, bf16[128,2048]{1,0:T(8,128)(2,1)}, bf16[8,64,1024]{2,1,0:T(8,128)(2,1)}, f32[64,384]{1,0:T(8,128)}, bf16[128,2048]{1,0:T(8,128)(2,1)}, /*index=5*/f32[8,72,128]{2,1,0:T(8,128)}) custom-call(s32[1,4]{1,0:T(1,128)} %lengths.1, s32[1]{0:T(128)S(6)} %copy.48.level, bf16[128,2048]{1,0:T(8,128)(2,1)} %bitcast.70, ...), custom_call_target="tpu_custom_call" | custom-call | tf_op jit(solution)/shard_map/first/pallas_call | solution.py:1421
  249.2 0.9 slice_reduce_fusion.1
  250.0 0.6 dynamic_slice.14
  250.6 1.5 copy.36
  252.1 0.1 bitcast_bitcast_fusion
  252.3 1.2 copy.30
  253.5 0.0 copy-start.4
  253.5 1.2 copy.43
  254.7 0.0 copy-done.4
  254.7 0.0 copy-start.3
  254.7 1.5 pad_maximum_fusion
  256.2 0.0 copy-start
  256.2 0.0 copy-start.2
  256.2 0.0 copy-done.3
  256.2 0.0 copy-start.1
  256.3 0.1 copy.31
  256.5 0.7 fusion.1
  257.2 0.6 fusion.2
  257.8 0.1 copy.32
  257.9 0.1 copy.33
  258.0 0.6 reshape.77
  258.6 0.1 copy.34
  258.7 0.1 copy.35
  258.8 0.6 reshape.79
  259.4 0.1 reshape_squeeze.3
  259.5 0.6 reduce_sum.29
  260.1 0.5 fusion.3
  260.6 0.0 copy-done
  260.6 1.1 convert_element_type.19
  261.7 0.0 copy-done.2
  261.7 0.8 copy.49
  262.5 0.0 copy-done.1
  262.5 0.8 copy.50
  (11 shorter events, 0.1 us)
Async XLA Ops:
  253.5 1.2 copy-start.4
  254.7 1.5 copy-start.3
  256.2 4.4 %copy-start = (bf16[128,2048]{1,0:T(8,128)(2,1)S(1)}, bf16[128,2048]{1,0:T(8,128)(2,1)}, u32[]{:S(2)}) copy-start(bf16[128,2048]{1,0:T(8,128)(2,1)} %get-tuple-element.22) | copy-start | bytes 1572868
  256.2 5.5 %copy-start.2 = (bf16[128,2048]{1,0:T(8,128)(2,1)S(1)}, bf16[128,2048]{1,0:T(8,128)(2,1)}, u32[]{:S(2)}) copy-start(bf16[128,2048]{1,0:T(8,128)(2,1)} %get-tuple-element.17) | copy-start | bytes 1572868
  256.2 6.3 %copy-start.1 = (bf16[128,2048]{1,0:T(8,128)(2,1)S(1)}, bf16[128,2048]{1,0:T(8,128)(2,1)}, u32[]{:S(2)}) copy-start(bf16[128,2048]{1,0:T(8,128)(2,1)} %get-tuple-element.18) | copy-start | bytes 1572868

commit v5 on v4

--- a/solution.py
+++ b/solution.py
@@ -1141,12 +1141,17 @@
         base_row = MODEL // TILE
         for i in range(base_row):
             parbuf[i : i + 1, :] = gain_grad[:, tile_of(i)]
-        count = nd + 2
-        for r in range(8):
-            for i in range(count):
-                at = base_row + r * count + i
-                parbuf[at : at + 1, :] = sums[r : r + 1, tile_of(i)]
-        parbuf[base_row + 8 * count :, :] = heads[...]
+        for i in range(nd + 2):
+            parbuf[base_row + 8 * i : base_row + 8 * i + 8, :] = sums[:, tile_of(i)]
+        lane_at = iota((1, TILE), 1)
+        skip_row = jnp.zeros((1, TILE), F32)
+        for i in range(nd):
+            both = sums[1:2, tile_of(i)]
+            for e in range(2):
+                part = jnp.where(lax.div(lane_at, HEAD_DIM) == e, both, 0.0)
+                skip_row = skip_row + jnp.where(lane_at == 2 * i + e, lane_sum(part), 0.0)
+        heads[2:3, :] = skip_row
+        parbuf[base_row + 8 * (nd + 2) :, :] = exact(heads[...], sel[...].astype(F32), ((1,), (1,)))
         small = [
             go(remote(parbuf, pard.at[k - 1], qd_s.at[k], qd_r.at[k], device)) for k, device, _ in lines
         ]
@@ -1458,53 +1463,96 @@
             name="first",
         )(*args)
 
+    def finish_kernel(
+        self, y, dx, dw, dwc, dwo, pars,
+        y_out, dx_out, norm_out, in_out, tap_out, bias_out, step_out, rate_out, skip_out, gain_out, out_out, every, narrow,
+    ):
+        nd, nm, rows = self.nd, self.nm, self.rows_in
+        dp, c, z = self.place()
+        owner = dp * nm + c * self.nz + z
+        own_conv = CONV // (nd * nm)
+        base_row = MODEL // TILE
+        y_out[...] = y[...]
+        dx_out[...] = dx[...]
+        out_out[...] = dwo[...].astype(F32)
+        for m in range(nm):
+            for i in range(2 * nd):
+                in_out[:, tile_of(i * nm + m)] = dw[m, :, tile_of(i)].astype(F32)
+        in_out[:, 2 * INNER :] = dwc[:, : EXTENT - 2 * INNER]
+        summed = pars[0]
+        for m in range(1, nm):
+            summed = summed + pars[m]
+        narrow[...] = summed[0:base_row, :]
+        row = narrow[pl.ds(lax.div(owner, 2), 1), :]
+        norm_out[...] = jnp.where(lax.rem(owner, 2) == 0, row[:, :rows], row[:, rows:])
+        for i in range(nd):
+            for m in range(nm):
+                every[:, tile_of(i * nm + m)] = pars[m, base_row + 8 * i : base_row + 8 * i + 8, :]
+        for i in range(2):
+            at = base_row + 8 * (nd + i)
+            every[:, tile_of(nd * nm + i)] = summed[at : at + 8, :]
+        start = owner * own_conv
+        window = every[:, pl.ds(pl.multiple_of(lax.div(start, TILE) * TILE, TILE), 2 * TILE)]
+        window = pltpu.roll(window, lax.rem(2 * TILE - lax.rem(start, TILE), 2 * TILE), 1)
+        tap_out[...] = window[4 : 4 + KW, :own_conv]
+        bias_out[...] = window[2:3, :own_conv]
+        at = base_row + 8 * (nd + 2)
+        step_out[...] = summed[at : at + 1, :HEADS]
+        rate_out[...] = summed[at + 1 : at + 2, :HEADS]
+        skip_out[...] = summed[at + 2 : at + 3, :HEADS]
+        mine = pars[lax.rem(owner, nm), pl.ds(pl.multiple_of(base_row + 8 * dp, 8), 8), :]
+        gain_out[...] = mine[0:1, :]
+
+    def finish(self, *args):
+        nd, nm, rows = self.nd, self.nm, self.rows_in
+        own_conv = CONV // (nd * nm)
+        like = jax.ShapeDtypeStruct
+        return pl.pallas_call(
+            self.finish_kernel,
+            out_shape=[
+                like((SPAN, MODEL), BF16),
+                like((SPAN, MODEL), BF16),
+                like((1, rows), F32),
+                like((rows, EXTENT), F32),
+                like((KW, own_conv), F32),
+                like((1, own_conv), F32),
+                like((1, HEADS), F32),
+                like((1, HEADS), F32),
+                like((1, HEADS), F32),
+                like((1, TILE), F32),
+                like((TILE, MODEL), F32),
+            ],
+            in_specs=[VM] * 6,
+            out_specs=[VM] * 11,
+            scratch_shapes=[pltpu.VMEM((8, CONV), F32), pltpu.VMEM((MODEL // TILE, TILE), F32)],
+            compiler_params=pltpu.CompilerParams(vmem_limit_bytes=63 * 2**20),
+            name="finish",
+        )(*args)
+
     def local(
         self, layer_input, out_grad, norm_gain, in_weight, conv_weight, conv_bias, step_bias, log_rate,
         skip_gain, gate_gain, out_weight, nest_level, doc_lengths,
     ):
-        nd, nz, nm, rows, wide = self.nd, self.nz, self.nm, self.rows_in, self.wide
-        dp, c, z = self.place()
-        me = c * nz + z
         docs = doc_lengths.shape[1]
         x = layer_input.reshape(SPAN, MODEL)
         g = out_grad.reshape(SPAN, MODEL)
-        own_conv = conv_bias.shape[0]
-        y_out, dx_out, dw, dwc, dwo, pars = self.run(
+        parts = self.run(
             docs, doc_lengths, nest_level, x, conv_weight.T, conv_bias[None], norm_gain[None], gate_gain[None],
             step_bias[None], log_rate[None], skip_gain[None], in_weight, g, out_weight,
         )
-        dw = jnp.transpose(dw.reshape(nm, rows, 2 * nd, TILE), (1, 2, 0, 3)).reshape(rows, 2 * INNER)
-        in_weight_grad = jnp.concatenate([dw.astype(F32), dwc[:, : EXTENT - 2 * INNER]], axis=1)
-        owner = dp * nm + me
-        gains = jnp.sum(pars[:, : MODEL // TILE], axis=0).reshape(MODEL)
-        norm_gain_grad = lax.dynamic_slice_in_dim(gains, owner * rows, rows)
-        base = MODEL // TILE
-        per_row = pars[:, base : base + 8 * (nd + 2)].reshape(nm, 8, nd + 2, TILE)
-        mains = per_row[:, :, :nd]
-        shared = jnp.sum(per_row[:, :, nd:], axis=0).reshape(8, 2 * TILE)
-        head_sums = pars[:, base + 8 * (nd + 2) :]
-        gate_gain_grad = lax.dynamic_index_in_dim(mains[me, 0], dp, 0, keepdims=False)
-        everything = jnp.transpose(mains[:, 1:], (1, 2, 0, 3)).reshape(7, INNER)
-        skip_gain_grad = jnp.sum(everything[0].reshape(HEADS, HEAD_DIM), axis=1)
-        bias_sum = jnp.concatenate([everything[1], shared[2]])
-        taps_sum = jnp.concatenate([everything[3:], shared[4:]], axis=1).T
-        conv_bias_grad = lax.dynamic_slice_in_dim(bias_sum, owner * own_conv, own_conv)
-        conv_weight_grad = lax.dynamic_slice_in_dim(taps_sum, owner * own_conv, own_conv)
-        mine = nd * self.per
-        by_head = lambda v: jnp.swapaxes(v[:, :mine].reshape(nm, nd, self.per), 0, 1).reshape(HEADS)
-        step_bias_grad, log_rate_grad = by_head(head_sums[:, 0]), by_head(head_sums[:, 1])
+        y_out, dx_out, norm, in_weight_grad, taps, bias, step, rate, skip, gain, dwo = self.finish(*parts)
         return (
             y_out.reshape(1, SPAN, MODEL),
             dx_out.reshape(1, SPAN, MODEL),
-            norm_gain_grad,
+            norm[0],
             in_weight_grad,
-            conv_weight_grad,
-            conv_bias_grad,
-            step_bias_grad,
-            log_rate_grad,
-            skip_gain_grad,
-            gate_gain_grad,
-            dwo.astype(F32),
+            taps.T,
+            bias[0],
+            step[0],
+            rate[0],
+            skip[0],
+            gain[0],
+            dwo,
         )
 
 

time: 264 us -> 253 us (0.958)
  local copies, waits for them, and re-layouts: 8.57 us -> 0 us
  other arithmetic: 5.41 us -> 0 us
  Pallas kernels: 248 us -> 252 us
    unnamed x18 -> x0, local copies, waits for them, and re-layouts: 4.35 us -> none
    pallas_call x0 -> x1, Pallas kernels: none -> 3.91 us  [finish(): pl.pallas_call(self.finish_kernel, out_shape=[like((SPAN, MODEL), BF16),...]
where the time goes in v5:
time: 253 us
  Pallas kernels  252 us (100%)
    pallas_call x1, Pallas kernels, run(): pl.pallas_call(functools.partial(self.kernel, docs), out_shape=[like(bloc...  248 us

profile of v5, /device:TPU:0, one launch (start us, length us, event | category | flops | bytes accessed | tf_op | source)
XLA Modules:
  0.0 253.1 jit_solution(8949374709768654648)
XLA Ops:
  1.3 247.9 %first.1 = (bf16[128,2048]{1,0:T(8,128)(2,1)}, bf16[128,2048]{1,0:T(8,128)(2,1)}, bf16[8,64,1024]{2,1,0:T(8,128)(2,1)}, f32[64,384]{1,0:T(8,128)}, bf16[128,2048]{1,0:T(8,128)(2,1)}, /*index=5*/f32[8,72,128]{2,1,0:T(8,128)}) custom-call(s32[1,4]{1,0:T(1,128)} %lengths.1, s32[1]{0:T(128)S(6)} %copy.24.level, bf16[128,2048]{1,0:T(8,128)(2,1)} %bitcast.18, ...), custom_call_target="tpu_custom_call" | custom-call | tf_op jit(solution)/shard_map/first/pallas_call | solution.py:1426
  249.2 3.9 %finish.1 = (bf16[128,2048]{1,0:T(8,128)(2,1)}, bf16[128,2048]{1,0:T(8,128)(2,1)}, f32[1,64]{1,0:T(1,128)}, f32[64,8512]{1,0:T(8,128)}, f32[4,136]{1,0:T(4,128)}...) custom-call(bf16[128,2048]{1,0:T(8,128)(2,1)} %get-tuple-element.28., ...), custom_call_target="tpu_custom_call" | custom-call | tf_op jit(solution)/shard_map/finish/pallas_call | solution.py:1510

commit v6 on v5

--- a/solution.py
+++ b/solution.py
@@ -908,6 +908,8 @@
             chp[0:2, tile_of(i)] = spread[2:4, :]
             chp[2:3, tile_of(i)] = parbuf_[i][6:7, :TILE]
         x_line.step(1)
+        own[3].wait()
+        g_line.begin()
         for j in range(1, 4):
             w_square.step(j)
         for j in range(1, nz):
@@ -916,8 +918,6 @@
         for j in range(4, nm):
             w_square.step(j)
         x_line.step(3)
-        own[3].wait()
-        g_line.begin()
         for j in range(nz):
             c_square.arrive(j)
         for i in range(nd):
@@ -978,18 +978,18 @@
         lanes_at = iota((SPAN, TILE), 1)
 
         def gate_grad(n, _):
-            at = rows_of(n, 256)
+            at = rows_of(n, 512)
             grad = dot(gall[at, :], woall[...].reshape(wide, MODEL), ((1,), (1,)))
             dg[at, :] = grad
-            for half in range(2):
+            for half in range(4):
                 product = jnp.zeros((SPAN, TILE), F32)
                 for i in range(nd):
-                    mine = scaled[pl.ds(pl.multiple_of(n * 256 + half * SPAN, SPAN), SPAN), tile_of(i)]
+                    mine = scaled[pl.ds(pl.multiple_of(n * 512 + half * SPAN, SPAN), SPAN), tile_of(i)]
                     product = product + mine.astype(F32) * grad[half * SPAN : (half + 1) * SPAN, tile_of(i)]
-                st[1, pl.ds(2 * n + half, 1), :] = lane_sum(product).T[0:1, :]
+                st[1, pl.ds(4 * n + half, 1), :] = lane_sum(product).T[0:1, :]
             return 0
 
-        lax.fori_loop(0, nm // 2, gate_grad, 0)
+        lax.fori_loop(0, nm // 4, gate_grad, 0)
         sent = []
         for j, step in enumerate(steps):
             device, _ = self.target(step)
@@ -1066,11 +1066,11 @@
 
         def weight_grad(owner):
             def piece(n, _):
-                at = pl.ds(pl.multiple_of(owner * (nm * rows) + n * 256, 256), 256)
-                wall[owner, rows_of(n, 256), :] = dot(xall[:, at], projm[PAD:, :], ((0,), (0,))).astype(BF16)
+                at = pl.ds(pl.multiple_of(owner * (nm * rows) + n * 512, 512), 512)
+                wall[owner, rows_of(n, 512), :] = dot(xall[:, at], projm[PAD:, :], ((0,), (0,))).astype(BF16)
                 return 0
 
-            lax.fori_loop(0, nm * rows // 256, piece, 0)
+            lax.fori_loop(0, nm * rows // 512, piece, 0)
 
         weight_grad(w_sum.diag)
         weight_grad(w_sum.dx)

time: 253 us -> 251 us (level)
  no operation moved by 1% of the time
where the time goes in v6:
time: 251 us
  Pallas kernels  250 us (100%)
    pallas_call x1, Pallas kernels, run(): pl.pallas_call(functools.partial(self.kernel, docs), out_shape=[like(bloc...  246 us

profile of v6, /device:TPU:0, one launch (start us, length us, event | category | flops | bytes accessed | tf_op | source)
XLA Modules:
  0.0 251.2 jit_solution(12719374548094028128)
XLA Ops:
  1.3 246.0 %first.1 = (bf16[128,2048]{1,0:T(8,128)(2,1)}, bf16[128,2048]{1,0:T(8,128)(2,1)}, bf16[8,64,1024]{2,1,0:T(8,128)(2,1)}, f32[64,384]{1,0:T(8,128)}, bf16[128,2048]{1,0:T(8,128)(2,1)}, /*index=5*/f32[8,72,128]{2,1,0:T(8,128)}) custom-call(s32[1,4]{1,0:T(1,128)} %lengths.1, s32[1]{0:T(128)S(6)} %copy.24.level, bf16[128,2048]{1,0:T(8,128)(2,1)} %bitcast.18, ...), custom_call_target="tpu_custom_call" | custom-call | tf_op jit(solution)/shard_map/first/pallas_call | solution.py:1426
  247.3 3.9 %finish.1 = (bf16[128,2048]{1,0:T(8,128)(2,1)}, bf16[128,2048]{1,0:T(8,128)(2,1)}, f32[1,64]{1,0:T(1,128)}, f32[64,8512]{1,0:T(8,128)}, f32[4,136]{1,0:T(4,128)}...) custom-call(bf16[128,2048]{1,0:T(8,128)(2,1)} %get-tuple-element.28., ...), custom_call_target="tpu_custom_call" | custom-call | tf_op jit(solution)/shard_map/finish/pallas_call | solution.py:1510

commit v7 on v6

--- a/solution.py
+++ b/solution.py
@@ -350,7 +350,7 @@
 COMMON = 384
 PAD = 16
 NEG = -1e30
-SLOTS = (1, 4)
+SLOTS = (0, 3)
 VM = pl.BlockSpec(memory_space=pltpu.VMEM)
 SM = pl.BlockSpec(memory_space=pltpu.SMEM)
 ANY = pl.BlockSpec(memory_space=pl.ANY)

time: 251 us -> 251 us (level)
  no operation moved by 1% of the time
where the time goes in v7:
time: 251 us
  Pallas kernels  250 us (100%)
    pallas_call x1, Pallas kernels, run(): pl.pallas_call(functools.partial(self.kernel, docs), out_shape=[like(bloc...  246 us

profile of v7, /device:TPU:0, one launch (start us, length us, event | category | flops | bytes accessed | tf_op | source)
XLA Modules:
  0.0 251.2 jit_solution(16404835693705818655)
XLA Ops:
  1.3 246.0 %first.1 = (bf16[128,2048]{1,0:T(8,128)(2,1)}, bf16[128,2048]{1,0:T(8,128)(2,1)}, bf16[8,64,1024]{2,1,0:T(8,128)(2,1)}, f32[64,384]{1,0:T(8,128)}, bf16[128,2048]{1,0:T(8,128)(2,1)}, /*index=5*/f32[8,72,128]{2,1,0:T(8,128)}) custom-call(s32[1,4]{1,0:T(1,128)} %lengths.1, s32[1]{0:T(128)S(6)} %copy.24.level, bf16[128,2048]{1,0:T(8,128)(2,1)} %bitcast.18, ...), custom_call_target="tpu_custom_call" | custom-call | tf_op jit(solution)/shard_map/first/pallas_call | solution.py:1426
  247.3 3.9 %finish.1 = (bf16[128,2048]{1,0:T(8,128)(2,1)}, bf16[128,2048]{1,0:T(8,128)(2,1)}, f32[1,64]{1,0:T(1,128)}, f32[64,8512]{1,0:T(8,128)}, f32[4,136]{1,0:T(4,128)}...) custom-call(bf16[128,2048]{1,0:T(8,128)(2,1)} %get-tuple-element.28., ...), custom_call_target="tpu_custom_call" | custom-call | tf_op jit(solution)/shard_map/finish/pallas_call | solution.py:1510
